TPU v7x, 256 devices: a whole 4x4x8 slice. The times are simulated.
256 devices in a mesh: samp: 8 (over z_hi, core), seq: 32 (over x, y, z_lo).
Axes of the slice: x: 4, y: 4, z: 8 (z_hi: 4, z_lo: 2; z = z_hi * 2 + z_lo), core: 2. Of those that a mesh axis runs over, the one named last changes fastest.
Arguments:
- atom_act: bfloat16 [16, 12288, 128], P('samp', 'seq'), may hold values from -6 to 6
- atom_gain: float32 [128], replicated, may hold values from 0.25 to 1.75
- atom_query: bfloat16 [128, 128], replicated, may hold values from -0.5 to 0.5
- atom_keyval: bfloat16 [128, 256], replicated, may hold values from -0.5 to 0.5
- atom_output: bfloat16 [128, 128], replicated, may hold values from -0.5 to 0.5
- atom_bias: bfloat16 [4, 384, 32, 128], P(None, 'seq'), may hold values from -4 to 298
- key_range: int32 [384, 2], P('seq'), may hold values from 0 to 12288, as said below
- atom_token: int32 [12288], P('seq'), may hold values from 0 to 1535, as said below
- token_counts: int32 [1536], P('seq'), may hold values from 1 to 15, as said below
- gather_weight: bfloat16 [128, 768], replicated, may hold values from -0.5 to 0.5
- token_gain: float32 [768], replicated, may hold values from 0.25 to 1.75
- token_query: bfloat16 [768, 768], replicated, may hold values from -0.21875 to 0.21875
- token_keyval: bfloat16 [768, 1536], replicated, may hold values from -0.21875 to 0.21875
- token_output: bfloat16 [768, 768], replicated, may hold values from -0.21875 to 0.21875
- pair_bias: bfloat16 [16, 1536, 1536], P('samp', 'seq'), may hold values from -4 to 298
- trans_gain: float32 [768], replicated, may hold values from 0.25 to 1.75
- trans_gate_up: bfloat16 [768, 3072], replicated, may hold values from -0.21875 to 0.21875
- trans_down: bfloat16 [1536, 768], replicated, may hold values from -0.15625 to 0.15625
- back_weight: bfloat16 [768, 128], replicated, may hold values from -0.21875 to 0.21875
Outputs:
- atom_out: bfloat16 [16, 12288, 128], P('samp', 'seq')
- token_out: bfloat16 [16, 1536, 768], P('samp', 'seq')
Inputs may be any that keep to these rules, and one draw needn't show every extreme that they name: max(0, 32 * b - 48) <= key_range[b, 0] <= 32 * b and 32 * b + 32 <= key_range[b, 1] <= min(12288, 32 * b + 80). atom_token never falls along the atoms; atom a belongs to token a // 8 or a // 8 - 1. token_counts[t] is the number of atoms a with atom_token[a] = t.
All inputs are finite; a program needn't handle non-finite values.
Results may differ from a plain program's by a relative error of at most 0.025.
Values may be sent and summed in bfloat16 or wider, within the bound.
No kernel may reach another device: no remote copies, remote signals or barrier semaphores. Data moves between devices by JAX's collectives and lax.ppermute only.
A program may use at most 128 MiB of HBM per device.

v0:
```python
import math

import jax
import jax.numpy as jnp
from jax import lax
from jax.sharding import PartitionSpec as P

AH = 4
HEADS = 16
WQ = 32
WK = 128
EDGE = 48


EPSILON = 1e-05
NEGATIVE = -1e30


def extended(cells, sides, width):
    for axis, dim in sides:
        count = lax.axis_size(axis)
        ends = count - 1
        head = lax.slice_in_dim(cells, 0, width, axis=dim)
        tail = lax.slice_in_dim(cells, cells.shape[dim] - width, cells.shape[dim], axis=dim)
        cells = jnp.concatenate(
            [
                lax.ppermute(tail, axis, [(i, (i + 1) % count) for i in range(ends)]),
                cells,
                lax.ppermute(head, axis, [((i + 1) % count, i) for i in range(ends)]),
            ],
            axis=dim,
        )
    return cells


def passed_along(value, axis, by):
    devices = lax.axis_size(axis)
    pairs = [(i, i + by) for i in range(devices) if 0 <= i + by < devices]
    return lax.ppermute(value, axis, pairs)


def layer_norm(values, gain_vector):
    widened = values.astype(jnp.float32)
    centred = widened - jnp.mean(widened, axis=-1, keepdims=True)
    variance = jnp.mean(centred * centred, axis=-1, keepdims=True)
    return (centred * lax.rsqrt(variance + EPSILON) * gain_vector).astype(jnp.bfloat16)


def softmax_rows(scores):
    maxima = jnp.max(scores, axis=-1, keepdims=True)
    exponent = jnp.exp(scores - maxima)
    return exponent / jnp.sum(exponent, axis=-1, keepdims=True)


def project(values, weight):
    return jnp.einsum("sac,cd->sad", values, weight, preferred_element_type=jnp.float32)


def make_attend(query_heads, bias_rows, head_count, head_size, score_scale):

    def attend(running, keyval_piece, first_key):
        best_score, row_total, value_sum = running
        sample_count = keyval_piece.shape[0]
        piece_rows = keyval_piece.shape[1]
        key_heads = keyval_piece[:, :, 0].reshape(sample_count, piece_rows, head_count, head_size)
        value_heads = keyval_piece[:, :, 1].reshape(sample_count, piece_rows, head_count, head_size)
        piece_scores = jnp.einsum(
            "sqhd,skhd->shqk", query_heads, key_heads, preferred_element_type=jnp.float32
        )
        piece_scores = piece_scores * score_scale + bias_rows.astype(jnp.float32)[None]
        new_best = jnp.maximum(best_score, jnp.max(piece_scores, axis=-1))
        exponent = jnp.exp(piece_scores - new_best[..., None])
        row_total = jnp.sum(exponent, axis=-1)
        value_sum = jnp.einsum(
            "shqk,skhd->shqd",
            exponent.astype(jnp.bfloat16),
            value_heads,
            preferred_element_type=jnp.float32,
        )
        return (new_best, row_total, value_sum)

    return attend


def initial_state(sample_count, head_count, token_rows, head_size):
    return (
        jnp.full((sample_count, head_count, token_rows), NEGATIVE, jnp.float32),
        jnp.zeros((sample_count, head_count, token_rows), jnp.float32),
        jnp.zeros((sample_count, head_count, token_rows, head_size), jnp.float32),
    )


def per_device(
    atom_act,
    atom_gain,
    atom_query,
    atom_keyval,
    atom_output,
    atom_bias,
    key_range,
    atom_token,
    token_counts,
    gather_weight,
    token_gain,
    token_query,
    token_keyval,
    token_output,
    pair_bias,
    trans_gain,
    trans_gate_up,
    trans_down,
    back_weight,
):
    samples, atom_rows, channels = atom_act.shape
    windows = atom_rows // WQ
    head_width = channels // AH
    atom_scale = 1.0 / math.sqrt(head_width)
    normed = layer_norm(atom_act, atom_gain)
    queries = project(normed, atom_query).astype(jnp.bfloat16)
    keyvals = project(normed, atom_keyval).astype(jnp.bfloat16)
    padded = extended(keyvals, (("seq", 1),), EDGE)
    blocks = padded.reshape(samples, windows + 2 * EDGE // WQ, WQ, 2 * channels)
    window_keys = jnp.concatenate(
        [blocks[:, shift_at : shift_at + windows] for shift_at in range(WK // WQ)], axis=2
    )
    key_part = window_keys[..., :channels].reshape(samples, windows, WK, AH, head_width)
    value_part = window_keys[..., channels:].reshape(samples, windows, WK, AH, head_width)
    query_part = queries.reshape(samples, windows, WQ, AH, head_width)
    scores = jnp.einsum(
        "swqhd,swkhd->shwqk", query_part, key_part, preferred_element_type=jnp.float32
    )
    scores = scores * atom_scale + atom_bias.astype(jnp.float32)[None]
    window_base = lax.axis_index("seq") * windows + jnp.arange(windows, dtype=jnp.int32)
    position = WQ * window_base[:, None] - EDGE + jnp.arange(WK, dtype=jnp.int32)[None, :]
    key_valid = (position >= key_range[:, 0:1]) & (position < key_range[:, 1:2])
    scores = jnp.where(key_valid[None, None, :, None, :], scores, NEGATIVE)
    weights = softmax_rows(scores).astype(jnp.bfloat16)
    attended = jnp.einsum(
        "shwqk,swkhd->swqhd", weights, value_part, preferred_element_type=jnp.float32
    )
    attended = attended.astype(jnp.bfloat16).reshape(samples, atom_rows, channels)
    atom_mid = (atom_act.astype(jnp.float32) + project(attended, atom_output)).astype(jnp.bfloat16)
    token_rows = token_counts.shape[0]
    first_token = lax.axis_index("seq") * token_rows
    token_slot = atom_token - first_token
    hidden_atoms = jax.nn.relu(project(atom_mid, gather_weight)).astype(jnp.bfloat16)
    own_table = (token_slot[:, None] == jnp.arange(token_rows, dtype=jnp.int32)[None, :]).astype(
        jnp.bfloat16
    )
    own_sums = jnp.einsum(
        "at,sad->std", own_table, hidden_atoms, preferred_element_type=jnp.float32
    )
    before_table = (token_slot == -1).astype(jnp.bfloat16)
    before_sum = jnp.einsum(
        "a,sad->sd", before_table, hidden_atoms, preferred_element_type=jnp.float32
    )
    arrived = passed_along(before_sum, "seq", -1)
    own_sums = own_sums.at[:, token_rows - 1].add(arrived)
    token_act = (own_sums / token_counts.astype(jnp.float32)[None, :, None]).astype(jnp.bfloat16)
    token_norm = layer_norm(token_act, token_gain)
    token_queries = project(token_norm, token_query).astype(jnp.bfloat16)
    model_width = token_norm.shape[-1]
    head_size = model_width // HEADS
    score_scale = 1.0 / math.sqrt(head_size)
    all_bias = lax.all_gather(pair_bias, "samp", axis=0, tiled=True)
    query_heads = token_queries.reshape(samples, token_rows, HEADS, head_size)
    attend = make_attend(query_heads, all_bias, HEADS, head_size, score_scale)
    initial = initial_state(samples, HEADS, token_rows, head_size)
    token_keyvals = (
        project(token_norm, token_keyval)
        .astype(jnp.bfloat16)
        .reshape(samples, token_rows, 2, model_width)
    )
    best_score, row_total, value_sum = attend(
        initial, lax.all_gather(token_keyvals, "seq", axis=1, tiled=True), jnp.int32(0)
    )
    attended_tokens = (value_sum / row_total[..., None]).astype(jnp.bfloat16)
    merged = jnp.einsum(
        "shqd,hde->sqe",
        attended_tokens,
        token_output.reshape(HEADS, head_size, model_width),
        preferred_element_type=jnp.float32,
    )
    token_mid = (token_act.astype(jnp.float32) + merged).astype(jnp.bfloat16)
    trans_norm = layer_norm(token_mid, trans_gain)
    gate_up = project(trans_norm, trans_gate_up)
    hidden_width = trans_down.shape[0]
    hidden = (jax.nn.silu(gate_up[..., :hidden_width]) * gate_up[..., hidden_width:]).astype(
        jnp.bfloat16
    )
    token_out = (token_mid.astype(jnp.float32) + project(hidden, trans_down)).astype(jnp.bfloat16)
    back_rows = project(token_out, back_weight).astype(jnp.bfloat16)
    previous = passed_along(back_rows[:, token_rows - 1], "seq", 1)
    back_table = jnp.concatenate([previous[:, None], back_rows], axis=1)
    lookup = (
        (token_slot + 1)[:, None] == jnp.arange(token_rows + 1, dtype=jnp.int32)[None, :]
    ).astype(jnp.bfloat16)
    gathered_back = jnp.einsum(
        "at,stc->sac", lookup, back_table, preferred_element_type=jnp.float32
    )
    atom_out = (atom_mid.astype(jnp.float32) + gathered_back).astype(jnp.bfloat16)
    return (atom_out, token_out)


def solution(mesh):
    placed = (
        P("samp", "seq", None),
        P(),
        P(),
        P(),
        P(),
        P(None, "seq", None, None),
        P("seq", None),
        P("seq"),
        P("seq"),
        P(),
        P(),
        P(),
        P(),
        P(),
        P("samp", "seq", None),
        P(),
        P(),
        P(),
        P(),
    )
    return jax.shard_map(
        per_device,
        mesh=mesh,
        in_specs=placed,
        out_specs=(P("samp", "seq", None), P("samp", "seq", None)),
        check_vma=False,
    )
```

profile of v0, /device:TPU:6, one launch (start us, length us, event | category | flops | bytes accessed | tf_op | source)
XLA Modules:
  0.0 380.0 jit_solution(8645867233082741902)
XLA Ops:
  7.2 1.3 convert_reduce_fusion
  8.5 1.2 fusion.52
  9.7 1.3 convolution_convert_fusion.1
  11.1 6.5 %collective-permute-start.1 = (bf16[2,48,256]{2,1,0:T(8,128)(2,1)S(1)}, bf16[2,48,256]{2,1,0:T(8,128)(2,1)S(1)}, u32[]{:S(2)}, u32[]{:S(2)}) collective-permute-start(bf16[2,48,256]{2,1,0:T(8,128)(2,1)S(1)} %get-tuple-element.27), channel_id=1, source_target_pairs={{1,0},{2,1},{3,2},{4,3},{5,4},{6,5},{7,6},{8,7},{9,8},{10,9},{11,1... | collective-permute-start | bytes 147464 | tf_op jit(solution)/shard_map/ppermute | solution.py:29
  17.7 1.9 collective-permute-start
  19.7 1.3 convolution_convert_fusion.2
  21.0 0.8 slice_bitcast_fusion.1
  21.8 1.2 broadcast_compare_fusion
  23.0 1.2 reshape.168
  24.3 1.0 convert_element_type.91
  25.2 0.7 reshape.180
  25.9 0.7 convert_element_type.98
  26.7 1.0 fusion.97
  27.7 2.4 copy.78
  30.1 1.5 copy.77
  31.6 1.6 copy.76
  33.1 1.5 copy.75
  34.7 5.0 %pad_maximum_fusion = bf16[2,12,128,256]{2,3,1,0:T(8,128)(2,1)S(1)} fusion(bf16[2,12,32,256]{2,3,1,0:T(8,128)(2,1)} %copy.78, bf16[2,12,32,256]{2,3,1,0:T(8,128)(2,1)} %copy.77, bf16[2,12,32,256]{2,3,1,0:T(8,128)(2,1)} %copy.76, bf16[2,12,32,256]{2,3,1,0:T(8,128)(2,1)} %copy.75), kind=kLoop, calls=%fused_computation.19 | loop fusion | flops 6291456 | bytes 3145728 | tf_op jit(solution)/shard_map/concatenate | solution.py:123
  39.7 1.3 fusion.96
  41.0 3.2 fusion.99
  44.2 3.2 fusion.20
  47.4 1.5 copy.62
  49.0 0.4 reshape.170
  49.4 1.0 fusion.25
  50.4 1.4 maximum_convert_fusion
  52.1 6.6 %collective-permute-start.2 = (f32[2,768]{1,0:T(2,128)S(1)}, f32[2,768]{1,0:T(2,128)S(1)}, u32[]{:S(2)}, u32[]{:S(2)}) collective-permute-start(f32[2,768]{1,0:T(2,128)S(1)} %bitcast.103), channel_id=1, source_target_pairs={{1,0},{2,1},{3,2},{4,3},{5,4},{6,5},{7,6},{8,7},{9,8},{10,9},{11,1... | collective-permute-start | bytes 18440 | tf_op jit(solution)/shard_map/ppermute | solution.py:39
  58.7 0.3 fusion.77
  59.0 1.0 collective-permute-done.2
  60.0 0.3 scatter-add.4
  60.7 0.6 fusion.15
  61.4 0.9 copy.64
  62.4 1.6 fusion.33
  64.0 0.5 reshape.172
  64.5 4.5 %convert_element_type.104 = f32[16,48,1536]{2,1,0:T(8,128)} convert(bf16[16,48,1536]{2,1,0:T(8,128)(2,1)} %all-gather.5.cloned.1.call-done) | non-fusion elementwise | flops 1179648 | bytes 7077888 | tf_op jit(solution)/shard_map/convert_element_type | solution.py:70
  69.0 208.9 %all-gather.3.cloned.1.call-done = bf16[2,1536,2,768]{3,2,0,1:T(2,128)(2,1)} async-done(((bf16[2,48,2,768]{3,2,0,1:T(2,128)(2,1)}), bf16[2,1536,2,768]{3,2,0,1:T(2,128)(2,1)}) %all-gather.3.cloned.1.call-update) | async-done | bytes 9437200 | tf_op jit(solution)/shard_map/all_gather | solution.py:175
  277.9 19.5 %fusion.95 = (bf16[2,1536,1,768]{3,2,0,1:T(2,128)(2,1)}, bf16[2,1536,1,768]{3,2,0,1:T(2,128)(2,1)}) fusion(bf16[2,1536,2,768]{3,2,0,1:T(2,128)(2,1)} %all-gather.3.cloned.1.call-done), kind=kLoop, calls=%fused_computation.113 | loop fusion | bytes 18874368 | tf_op jit(solution)/shard_map/slice | solution.py:65
  297.5 22.4 %copy.79 = bf16[2,1536,1,768]{1,3,0,2:T(8,128)(2,1)} copy(bf16[2,1536,1,768]{3,2,0,1:T(2,128)(2,1)} %get-tuple-element.19) | data formatting | bytes 9437184
  319.9 22.4 %copy.65 = bf16[2,1536,1,768]{1,3,0,2:T(8,128)(2,1)} copy(bf16[2,1536,1,768]{3,2,0,1:T(2,128)(2,1)} %get-tuple-element.18) | data formatting | bytes 9437184 | tf_op jit(solution)/shard_map/slice | solution.py:65
  342.3 5.1 %fusion.1 = (f32[2,16,48]{2,1,0:T(8,128)S(1)}, f32[2,16,48,1536]{3,2,1,0:T(8,128)S(1)}) fusion(f32[16,48,1536]{2,1,0:T(8,128)} %convert_element_type.104, bf16[2,1536,16,48]{1,3,2,0:T(8,128)(2,1)} %bitcast.96, bf16[2,48,16,48]{3,2,1,0:T(8,128)(2,1)S(1)} %reshape.172), kind=kOutput, calls=%fused_computation.3 | convolution fusion | flops 233568768 | bytes 19027968 | tf_op jit(solution)/shard_map/sqhd,skhd->shqk/dot_general | solution.py:67
  347.5 2.1 fusion.2
  349.6 1.4 copy-done.2
  351.0 8.0 %fusion.100 = (f32[2,48]{1,0:T(2,128)S(1)}, f32[2,48,768]{2,1,0:T(8,128)S(1)}) fusion(bf16[16,48,768,1]{2,1,0,3:T(8,128)(2,1)S(1)} %bitcast.100, bf16[2,1536,16,48]{1,3,2,0:T(8,128)(2,1)} %bitcast.97, f32[2,16,48,1536]{3,2,1,0:T(8,128)} %copy-done.2, f32[2,16,48]{2,1,0:T(8,128)S(1)} %broadcast_maximum_fusion, f32[16,48,1536]{2,1,0:T(8,128)} %convert_element_type.104, ...), kind=kOutput, calls=%fused_computation.118 | convolution fusion | flops 349691808 | bytes 20509056 | tf_op jit(solution)/shard_map/shqd,hde->sqe/dot_general | solution.py:178
  359.2 3.4 fusion.6
  362.6 0.6 fusion.30
  363.2 0.4 copy-done.7
  363.8 1.9 collective-permute-start.3
  365.7 6.5 %collective-permute-done.3 = bf16[2,128]{1,0:T(2,128)(2,1)S(1)} collective-permute-done((bf16[2,128]{1,0:T(2,128)(2,1)S(1)}, bf16[2,128]{1,0:T(2,128)(2,1)S(1)}, u32[]{:S(2)}, u32[]{:S(2)}) %collective-permute-start.3) | collective-permute-done | bytes 544 | tf_op jit(solution)/shard_map/ppermute | solution.py:39
  372.2 0.9 fusion.24
  (59 shorter events, 1.6 us)
Async XLA Ops:
  7.2 53.6 %copy-start = (bf16[768,1536]{1,0:T(8,128)(2,1)S(1)}, bf16[768,1536]{1,0:T(8,128)(2,1)}, u32[]{:S(2)}) copy-start(bf16[768,1536]{1,0:T(8,128)(2,1)} %param.33) | copy-start | bytes 7077892
  7.2 17.1 %copy-start.6 = (bf16[4,12,32,128]{3,2,1,0:T(8,128)(2,1)S(1)}, bf16[4,12,32,128]{3,2,1,0:T(8,128)(2,1)}, u32[]{:S(2)}) copy-start(bf16[4,12,32,128]{3,2,1,0:T(8,128)(2,1)} %param.26) | copy-start | bytes 1179652
  7.2 57.3 %all-gather.5.cloned.1.call-start = ((), (), s32[]{:S(2)}) async-start(), calls=%async_computation.1 | async-start | bytes 2654208 | tf_op jit(solution)/shard_map/all_gather | solution.py:165
  11.1 15.5 %collective-permute-start.1 = (bf16[2,48,256]{2,1,0:T(8,128)(2,1)S(1)}, bf16[2,48,256]{2,1,0:T(8,128)(2,1)S(1)}, u32[]{:S(2)}, u32[]{:S(2)}) collective-permute-start(bf16[2,48,256]{2,1,0:T(8,128)(2,1)S(1)} %get-tuple-element.27), channel_id=1, source_target_pairs={{1,0},{2,1},{3,2},{4,3},{5,4},{6,5},{7,6},{8,7},{9,8},{10,9},{11,1... | collective-permute-start | bytes 147464 | tf_op jit(solution)/shard_map/ppermute | solution.py:29
  17.7 9.0 %collective-permute-start = (bf16[2,48,256]{2,1,0:T(8,128)(2,1)S(1)}, bf16[2,48,256]{2,1,0:T(8,128)(2,1)S(1)}, u32[]{:S(2)}, u32[]{:S(2)}) collective-permute-start(bf16[2,48,256]{2,1,0:T(8,128)(2,1)S(1)} %get-tuple-element.26), channel_id=1, source_target_pairs={{0,1},{1,2},{2,3},{3,4},{4,5},{5,6},{6,7},{7,8},{8,9},{9,10},{10,1... | collective-permute-start | bytes 147464 | tf_op jit(solution)/shard_map/ppermute | solution.py:27
  19.6 258.3 %all-gather.3.cloned.1.call-start = ((), (), s32[]{:S(2)}) async-start(), calls=%async_computation | async-start | bytes 9732096 | tf_op jit(solution)/shard_map/all_gather | solution.py:175
  39.7 1.3 copy-start.5
  47.4 2.0 copy-start.3
  50.4 10.4 %copy-start.10 = (f32[768]{0:T(1024)S(1)}, f32[768]{0:T(1024)}, u32[]{:S(2)}) copy-start(f32[768]{0:T(1024)} %param.31) | copy-start | bytes 9220
  52.1 8.0 %collective-permute-start.2 = (f32[2,768]{1,0:T(2,128)S(1)}, f32[2,768]{1,0:T(2,128)S(1)}, u32[]{:S(2)}, u32[]{:S(2)}) collective-permute-start(f32[2,768]{1,0:T(2,128)S(1)} %bitcast.103), channel_id=1, source_target_pairs={{1,0},{2,1},{3,2},{4,3},{5,4},{6,5},{7,6},{8,7},{9,8},{10,9},{11,1... | collective-permute-start | bytes 18440 | tf_op jit(solution)/shard_map/ppermute | solution.py:39
  342.3 5.2 %slice-start = ((s8[4718592]{0:T(1024)(128)(4,1)}), s8[4194304]{0:T(1024)(128)(4,1)S(1)}, s32[]{:S(2)}) async-start(s8[4718592]{0:T(1024)(128)(4,1)} %bitcast.94), calls=%async_computation.2 | async-start | bytes 8388608
  342.3 5.2 %slice-start.1 = ((s8[4718592]{0:T(1024)(128)(4,1)}), s8[524288]{0:T(1024)(128)(4,1)S(1)}, s32[]{:S(2)}) async-start(s8[4718592]{0:T(1024)(128)(4,1)} %bitcast.94), calls=%async_computation.3 | async-start | bytes 1048576
  347.4 3.6 copy-start.2
  347.5 3.5 copy-start.4
  351.0 8.2 %copy-start.9 = (f32[768]{0:T(1024)S(1)}, f32[768]{0:T(1024)}, u32[]{:S(2)}) copy-start(f32[768]{0:T(1024)} %param.36) | copy-start | bytes 9220
  359.2 3.5 copy-start.11
  359.2 14.0 %copy-start.1 = (bf16[768,1536]{1,0:T(8,128)(2,1)S(1)}, bf16[768,1536]{1,0:T(8,128)(2,1)}, u32[]{:S(2)}) copy-start(bf16[768,1536]{1,0:T(8,128)(2,1)} %param.33) | copy-start | bytes 7077892
  362.6 0.9 copy-start.7
  363.6 9.6 %copy-start.8 = (bf16[2,48,768]{2,1,0:T(8,128)(2,1)}, bf16[2,48,768]{2,1,0:T(8,128)(2,1)S(1)}, u32[]{:S(2)}) copy-start(bf16[2,48,768]{2,1,0:T(8,128)(2,1)S(1)} %fusion.30) | copy-start | bytes 442372
  363.8 8.4 %collective-permute-start.3 = (bf16[2,128]{1,0:T(2,128)(2,1)S(1)}, bf16[2,128]{1,0:T(2,128)(2,1)S(1)}, u32[]{:S(2)}, u32[]{:S(2)}) collective-permute-start(bf16[2,128]{1,0:T(2,128)(2,1)S(1)} %bitcast.104), channel_id=1, source_target_pairs={{0,1},{1,2},{2,3},{3,4},{4,5},{5,6},{6,7},{7,8},{8,9},{9,10},{10,1... | collective-permute-start | bytes 1544 | tf_op jit(solution)/shard_map/ppermute | solution.py:39
Sparse Core Ops, SparseCore 0:
  19.7 41.0 all-gather.4
  62.6 215.2 all-gather.2
where the time goes:
time: 382 us; the launch traced here: 380 us
  waiting for transfers between devices  217 us (57%)
  local copies, waits for them, and re-layouts  81.8 us (21%)
  matrix products  32.4 us (8%)
  other arithmetic  17.7 us (5%)
  starting transfers between devices  17.1 us (4%)
  between operations  14.4 us (4%)
    all_gather x1, waiting for transfers between devices, per_device(): lax.all_gather(token_keyvals, 'seq', axis=1, tiled=True)  209 us
    slice x2, local copies, waits for them, and re-layouts, attend(): keyval_piece[:, :, 0]  41.9 us
    unnamed x34, local copies, waits for them, and re-layouts  31.2 us
    dot_general x9, matrix products, project(): jnp.einsum('sac,cd->sad', values, weight, preferred_element_type=jnp.floa...  11.4 us
    ppermute x2, starting transfers between devices, passed_along(): return lax.ppermute(value, axis, pairs)  8.56 us
    dot_general x1, matrix products, per_device(): jnp.einsum('shqd,hde->sqe', attended_tokens, token_output.reshape(HEADS,...  7.96 us
  transfers between devices with their start and end apart: 6, of which 4 were waited for; matrix products, arithmetic and copies ran while one was open for 11% of the time, Pallas kernels for 0%

commit v1 on v0

v1 whole, which is shorter than its diff:
```python
import functools
import math

import jax
import jax.numpy as jnp
from jax import lax
from jax.experimental import pallas as pl
from jax.experimental.pallas import tpu as pltpu
from jax.sharding import PartitionSpec as P

AH = 4
HEADS = 16
WQ = 32
WK = 128
EDGE = 48
APT = 8
BEFORE = EDGE
AFTER = WQ + EDGE
META = 16
GROUP = 8

EPSILON = 1e-05
NEGATIVE = -1e30
F32 = jnp.float32
BF16 = jnp.bfloat16

NT = (((1,), (1,)), ((), ()))
TN = (((0,), (0,)), ((), ()))


def dot(a, b):
    return jnp.dot(a, b, preferred_element_type=F32)


def dot_nt(a, b):
    return lax.dot_general(a, b, NT, preferred_element_type=F32)


def dot_tn(a, b):
    return lax.dot_general(a, b, TN, preferred_element_type=F32)


def layer_norm(widened, gain):
    centred = widened - jnp.mean(widened, axis=-1, keepdims=True)
    variance = jnp.mean(centred * centred, axis=-1, keepdims=True)
    return (centred * lax.rsqrt(variance + EPSILON) * gain).astype(BF16)


def lane_group(rows, lanes, width):
    return lax.broadcasted_iota(jnp.int32, (rows, lanes), 1) // width


def atom_kernel(
    range_ref,
    act_ref,
    before_ref,
    after_ref,
    gain_ref,
    query_ref,
    keyval_ref,
    output_ref,
    bias_ref,
    token_ref,
    gather_ref,
    token_gain_ref,
    mid_ref,
    tokact_ref,
    norm_ref,
    att_ref,
):
    samples, atoms, channels = act_ref.shape
    windows = atoms // WQ
    tokens = norm_ref.shape[1]
    head_width = channels // AH
    scale = 1.0 / math.sqrt(head_width)
    device = lax.axis_index("seq")
    gain = gain_ref[...]
    bias_at = samples * AFTER
    meta_at = bias_at + AH * WQ

    head_of = lane_group(WQ, channels, head_width)
    masks = [(head_of == h).astype(BF16) for h in range(AH)]
    masks32 = [(head_of == h).astype(F32) for h in range(AH)]
    index = lax.broadcasted_iota(jnp.int32, (1, WK), 1)

    meta = after_ref[meta_at : meta_at + META, :].astype(F32)
    indexf = index.astype(F32)
    valid_after = (indexf >= meta[0:1, :]) & (indexf < meta[1:2, :])

    slot = token_ref[...] - device * tokens
    rows = lax.broadcasted_iota(jnp.int32, (tokens, atoms), 0)
    own_table = (rows == slot).astype(BF16)
    lane = lax.broadcasted_iota(jnp.int32, (tokens, WQ), 1)
    back_step = meta[2:3, :WQ] > 0.5
    after_table = (
        (lax.broadcasted_iota(jnp.int32, (tokens, WQ), 0) == tokens - 1) & (lane < APT) & back_step
    ).astype(BF16)
    counts = jnp.sum(own_table.astype(F32), axis=1, keepdims=True) + jnp.sum(
        after_table.astype(F32), axis=1, keepdims=True
    )
    counts = jnp.maximum(counts, 1.0)

    for s in range(samples):
        own = act_ref[s]
        extended = jnp.concatenate(
            [
                before_ref[s * BEFORE : (s + 1) * BEFORE, :],
                own,
                after_ref[s * AFTER : (s + 1) * AFTER, :],
            ],
            axis=0,
        ).astype(F32)
        normed = layer_norm(extended, gain)
        queries = dot(normed, query_ref[...]).astype(BF16)
        keyvals = dot(normed, keyval_ref[...]).astype(BF16)
        for w in range(windows + 1):
            q = queries[BEFORE + WQ * w : BEFORE + WQ * (w + 1), :]
            keys = keyvals[WQ * w : WQ * w + WK, :channels]
            values = keyvals[WQ * w : WQ * w + WK, channels:]
            stacked = jnp.concatenate([q * m for m in masks], axis=0)
            scores = dot_nt(stacked, keys) * scale
            if w < windows:
                bias = bias_ref[:, w].reshape(AH * WQ, WK)
                start = (device * windows + w) * WQ - EDGE
                valid = (index >= range_ref[w, 0] - start) & (index < range_ref[w, 1] - start)
            else:
                bias = after_ref[bias_at : bias_at + AH * WQ, :]
                valid = valid_after
            scores = jnp.where(valid, scores + bias.astype(F32), NEGATIVE)
            exponent = jnp.exp(scores - jnp.max(scores, axis=-1, keepdims=True))
            weights = exponent / jnp.sum(exponent, axis=-1, keepdims=True)
            mixed = dot(weights.astype(BF16), values)
            attended = mixed[:WQ] * masks32[0]
            for h in range(1, AH):
                attended = attended + mixed[WQ * h : WQ * (h + 1)] * masks32[h]
            att_ref[WQ * w : WQ * (w + 1), :] = attended.astype(BF16)
        merged = dot(att_ref[...], output_ref[...])
        mid = (extended[BEFORE : BEFORE + atoms + WQ, :] + merged).astype(BF16)
        mid_ref[s] = mid[:atoms]
        hidden = jnp.maximum(dot(mid, gather_ref[...]), 0.0).astype(BF16)
        sums = dot(own_table, hidden[:atoms]) + dot(after_table, hidden[atoms:])
        token_act = (sums / counts).astype(BF16)
        tokact_ref[s] = token_act
        norm_ref[s] = layer_norm(token_act.astype(F32), token_gain_ref[...])


def vmem():
    return pl.BlockSpec(memory_space=pltpu.VMEM)


def smem():
    return pl.BlockSpec(memory_space=pltpu.SMEM)


def anywhere():
    return pl.BlockSpec(memory_space=pl.ANY)


def run_atoms(key_range, act, before, after, *rest):
    samples, atoms, channels = act.shape
    width = rest[-2].shape[1]
    tokens = atoms // APT
    return pl.pallas_call(
        atom_kernel,
        out_shape=(
            jax.ShapeDtypeStruct((samples, atoms, channels), BF16),
            jax.ShapeDtypeStruct((samples, tokens, width), BF16),
            jax.ShapeDtypeStruct((samples, tokens, width), BF16),
        ),
        in_specs=[smem()] + [vmem()] * (3 + len(rest)),
        out_specs=(vmem(),) * 3,
        scratch_shapes=[pltpu.VMEM((atoms + WQ, channels), BF16)],
        compiler_params=pltpu.CompilerParams(vmem_limit_bytes=24 * 2**20),
        cost_estimate=pl.CostEstimate(
            flops=800_000_000, bytes_accessed=4_000_000, transcendentals=500_000
        ),
        name="atoms",
    )(key_range, act, before, after, *rest)


def block_rows(dx, dy, dz, rows):
    device = lax.axis_index("seq")
    x, y, z = device // 8, (device // 2) % 4, device % 2
    source = ((x + dx) % 4) * 8 + ((y + dy) % 4) * 2 + (z + dz) % 2
    return source * rows


def token_kernel(plan, pieces, *refs):
    parts = refs[:pieces]
    (
        bias_ref,
        norm_ref,
        tokact_ref,
        mid_ref,
        token_ref,
        gain_ref,
        query_hbm,
        keyval_hbm,
        output_hbm,
        gate_hbm,
        down_hbm,
        back_hbm,
        atom_out_ref,
        token_out_ref,
        back_rows_ref,
        all_ref,
        query_ref,
        keyval_ref,
        output_ref,
        gate_ref,
        down_ref,
        back_ref,
        att_ref,
        weight_sems,
        part_sems,
    ) = refs[pieces:]
    samples, tokens, width = norm_ref.shape
    head_size = width // HEADS
    scale = 1.0 / math.sqrt(head_size)
    device = lax.axis_index("seq")

    weight_copies = []
    for i, (source, target) in enumerate(
        (
            (query_hbm, query_ref),
            (keyval_hbm, keyval_ref),
            (output_hbm, output_ref),
            (gate_hbm, gate_ref),
            (down_hbm, down_ref),
            (back_hbm, back_ref),
        )
    ):
        copy = pltpu.make_async_copy(source, target, weight_sems.at[i])
        copy.start()
        weight_copies.append(copy)
    part_copies = []
    for i, (part, at, sample, offset) in enumerate(plan):
        target = pl.multiple_of(block_rows(*offset, tokens), 16)
        copy = pltpu.make_async_copy(
            parts[part].at[at : at + tokens],
            all_ref.at[sample, pl.ds(target, tokens)],
            part_sems.at[i],
        )
        copy.start()
        part_copies.append(copy)

    weight_copies[0].wait()
    norm = norm_ref[...].reshape(samples * tokens, width)
    queries = dot(norm, query_ref[...]).astype(BF16)
    weight_copies[1].wait()
    lanes = GROUP * head_size
    head_of = lane_group(tokens, lanes, head_size)
    masks = [(head_of == h).astype(BF16) for h in range(GROUP)]
    masks32 = [(head_of == h).astype(F32) for h in range(GROUP)]
    for copy in part_copies:
        copy.wait()
    for s in range(samples):
        for g in range(HEADS // GROUP):
            columns = slice(lanes * g, lanes * (g + 1))
            q = queries[tokens * s : tokens * (s + 1), columns]
            stacked = jnp.concatenate([q * m for m in masks], axis=0)
            absorbed = (dot_nt(stacked, keyval_ref[:, columns]) * scale).astype(BF16)
            scores = dot_nt(absorbed, all_ref[s])
            bias = bias_ref[GROUP * g : GROUP * (g + 1)].reshape(GROUP * tokens, -1)
            scores = scores + bias.astype(F32)
            exponent = jnp.exp(scores - jnp.max(scores, axis=-1, keepdims=True))
            total = jnp.sum(exponent, axis=-1, keepdims=True)
            mixed = dot(exponent.astype(BF16), all_ref[s]) / total
            value_at = slice(width + lanes * g, width + lanes * (g + 1))
            valued = dot(mixed.astype(BF16), keyval_ref[:, value_at])
            attended = valued[:tokens] * masks32[0]
            for h in range(1, GROUP):
                attended = attended + valued[tokens * h : tokens * (h + 1)] * masks32[h]
            att_ref[tokens * s : tokens * (s + 1), columns] = attended.astype(BF16)

    weight_copies[2].wait()
    merged = dot(att_ref[...], output_ref[...])
    token_act = tokact_ref[...].reshape(samples * tokens, width).astype(F32)
    token_mid = (token_act + merged).astype(BF16).astype(F32)
    trans = layer_norm(token_mid, gain_ref[...])
    weight_copies[3].wait()
    hidden_width = down_ref.shape[0]
    gate = dot(trans, gate_ref[:, :hidden_width])
    up = dot(trans, gate_ref[:, hidden_width:])
    hidden = (gate / (1.0 + jnp.exp(-gate)) * up).astype(BF16)
    weight_copies[4].wait()
    token_out = (token_mid + dot(hidden, down_ref[...])).astype(BF16)
    token_out_ref[...] = token_out.reshape(samples, tokens, width)
    weight_copies[5].wait()
    back_rows = dot(token_out, back_ref[...]).astype(BF16)
    back_rows_ref[...] = back_rows.reshape(samples, tokens, -1)
    atoms = mid_ref.shape[1]
    slot = token_ref[...] - device * tokens
    table = (lax.broadcasted_iota(jnp.int32, (tokens, atoms), 0) == slot).astype(BF16)
    for s in range(samples):
        gathered = dot_tn(table, back_rows[tokens * s : tokens * (s + 1)])
        atom_out_ref[s] = (mid_ref[s].astype(F32) + gathered).astype(BF16)


def run_tokens(plan, parts, bias, norm, tokact, mid, token, gain, weights):
    samples, tokens, width = norm.shape
    return pl.pallas_call(
        functools.partial(token_kernel, plan, len(parts)),
        out_shape=(
            jax.ShapeDtypeStruct(mid.shape, BF16),
            jax.ShapeDtypeStruct(norm.shape, BF16),
            jax.ShapeDtypeStruct((samples, tokens, mid.shape[2]), BF16),
        ),
        in_specs=[anywhere()] * len(parts) + [vmem()] * 6 + [anywhere()] * 6,
        out_specs=(vmem(),) * 3,
        scratch_shapes=[pltpu.VMEM((samples, bias.shape[2], width), BF16)]
        + [pltpu.VMEM(w.shape, w.dtype) for w in weights]
        + [
            pltpu.VMEM((samples * tokens, width), BF16),
            pltpu.SemaphoreType.DMA((len(weights),)),
            pltpu.SemaphoreType.DMA((len(plan),)),
        ],
        compiler_params=pltpu.CompilerParams(vmem_limit_bytes=52 * 2**20),
        cost_estimate=pl.CostEstimate(
            flops=10_000_000_000, bytes_accessed=20_000_000, transcendentals=3_000_000
        ),
        name="tokens",
    )(*parts, bias, norm, tokact, mid, token, gain, *weights)


def shifted(value, dx, dy, dz=0):
    pairs = []
    for t in range(32):
        x, y, z = t // 8, (t // 2) % 4, t % 2
        pairs.append((t, ((x + dx) % 4) * 8 + ((y + dy) % 4) * 2 + (z + dz) % 2))
    return lax.ppermute(value, "seq", pairs)


def ring(value, dx, dy):
    half = value.shape[0] // 2
    low = shifted(value, dx, dy)
    high = shifted(value, -dx, -dy)
    far_low = shifted(low[:half], dx, dy)
    far_high = shifted(high[half:], -dx, -dy)
    return [value, low, high, far_low, far_high]


def spread(norm):
    samples, tokens, _ = norm.shape
    other = shifted(norm, 0, 0, 1)
    parts, plan = [], []
    for s in range(samples):
        dx, dy = (1, 0) if s % 2 == 0 else (0, 1)
        first = jnp.concatenate([norm[s], other[s]], axis=0)
        line = ring(first, dx, dy)
        steps = (0, 0, -1, -1, 1, 1, 2, 2)
        plane = ring(jnp.concatenate(line, axis=0), dy, dx)
        base = len(parts)
        parts += plane
        for piece, (value, far) in enumerate(zip(plane, (0, -1, 1, 2, 2))):
            skip = 4 if piece == 4 else 0
            for k in range(value.shape[0] // tokens):
                near = steps[k + skip]
                offset = (near * dx + far * dy, near * dy + far * dx, (k + skip) % 2)
                plan.append((base + piece, k * tokens, s, offset))
    return parts, plan


def per_device(
    atom_act,
    atom_gain,
    atom_query,
    atom_keyval,
    atom_output,
    atom_bias,
    key_range,
    atom_token,
    token_counts,
    gather_weight,
    token_gain,
    token_query,
    token_keyval,
    token_output,
    pair_bias,
    trans_gain,
    trans_gate_up,
    trans_down,
    back_weight,
):
    samples, atoms, channels = atom_act.shape
    tokens = token_counts.shape[0]
    device = lax.axis_index("seq")
    count = lax.axis_size("seq")
    to_next = [(i, i + 1) for i in range(count - 1)]
    to_previous = [(i + 1, i) for i in range(count - 1)]

    first_start = device * atoms - EDGE
    meta = jnp.zeros((META, channels), F32)
    meta = meta.at[0].set((key_range[0, 0] - first_start).astype(F32))
    meta = meta.at[1].set((key_range[0, 1] - first_start).astype(F32))
    step = (device * atoms + jnp.arange(WQ, dtype=jnp.int32)) // APT - atom_token[:WQ]
    meta = meta.at[2, :WQ].set(step.astype(F32))
    packed = jnp.concatenate(
        [
            atom_act[:, :AFTER].reshape(samples * AFTER, channels),
            atom_bias[:, 0].reshape(AH * WQ, WK),
            meta.astype(BF16),
        ],
        axis=0,
    )
    after = lax.ppermute(packed, "seq", to_previous)
    before = lax.ppermute(
        atom_act[:, atoms - BEFORE :].reshape(samples * BEFORE, channels), "seq", to_next
    )
    all_bias = lax.all_gather(pair_bias, "samp", axis=0, tiled=True)
    token_row = atom_token.reshape(1, atoms)
    atom_mid, token_act, token_norm = run_atoms(
        key_range,
        atom_act,
        before,
        after,
        atom_gain.reshape(1, -1),
        atom_query,
        atom_keyval,
        atom_output,
        atom_bias,
        token_row,
        gather_weight,
        token_gain.reshape(1, -1),
    )
    parts, plan = spread(token_norm)
    atom_out, token_out, back_rows = run_tokens(
        plan,
        parts,
        all_bias,
        token_norm,
        token_act,
        atom_mid,
        token_row,
        trans_gain.reshape(1, -1),
        [token_query, token_keyval, token_output, trans_gate_up, trans_down, back_weight],
    )
    previous = lax.ppermute(back_rows[:, tokens - 1], "seq", to_next)
    earlier = (atom_token[:APT] < device * tokens)[None, :, None]
    extra = jnp.where(earlier, previous[:, None, :].astype(F32), 0.0)
    head = (atom_out[:, :APT].astype(F32) + extra).astype(BF16)
    atom_out = lax.dynamic_update_slice(atom_out, head, (0, 0, 0))
    return (atom_out, token_out)


def solution(mesh):
    placed = (
        P("samp", "seq", None),
        P(),
        P(),
        P(),
        P(),
        P(None, "seq", None, None),
        P("seq", None),
        P("seq"),
        P("seq"),
        P(),
        P(),
        P(),
        P(),
        P(),
        P("samp", "seq", None),
        P(),
        P(),
        P(),
        P(),
    )
    return jax.shard_map(
        per_device,
        mesh=mesh,
        in_specs=placed,
        out_specs=(P("samp", "seq", None), P("samp", "seq", None)),
        check_vma=False,
    )
```

time: 382 us -> 136 us (0.36)
  waiting for transfers between devices: 217 us -> 28.7 us
  local copies, waits for them, and re-layouts: 81.8 us -> 15.1 us
  Pallas kernels: 0 us -> 34.3 us
  matrix products: 32.4 us -> 0 us
  starting transfers between devices: 17.1 us -> 36.6 us
  other arithmetic: 17.7 us -> 2.77 us
    all_gather x1 -> x0, waiting for transfers between devices: 209 us -> none  [per_device(): lax.all_gather(token_keyvals, 'seq', axis=1, tiled=True)]
    slice x6 -> x13, local copies, waits for them, and re-layouts: 44.2 us -> 3.68 us  [the longest x1 1.27 us: per_device(): meta = meta.at[1].set((key_range[0, 1] - first_start).astype(F32))]
    pallas_call x0 -> x2, Pallas kernels: none -> 34.3 us  [the longest x1 24.1 us: run_tokens(): pl.pallas_call(functools.partial(token_kernel, plan, len(parts)), out_sha...]
    dot_general x15 -> x0, matrix products: 29.2 us -> none  [the longest x9 11.4 us: project(): jnp.einsum('sac,cd->sad', values, weight, preferred_element_type=jnp.floa...]
    unnamed x34 -> x40, local copies, waits for them, and re-layouts: 31.2 us -> 9.75 us
    ppermute x4 -> x20, waiting for transfers between devices: 7.6 us -> 28 us  [the longest x17 19.1 us: shifted(): return lax.ppermute(value, 'seq', pairs)]
    ppermute x4 -> x20, starting transfers between devices: 17 us -> 36.5 us  [the longest x17 24.5 us: shifted(): return lax.ppermute(value, 'seq', pairs)]
    convert_element_type x3 -> x1, other arithmetic: 6.16 us -> 0.01 us  [per_device(): extra = jnp.where(earlier, previous[:, None, :].astype(F32), 0.0)]
  transfers between devices with their start and end apart: 6 -> 21, of which waited for: 4 -> 9; matrix products, arithmetic and copies ran while one was open for 11% -> 6% of each run, Pallas kernels for 0% -> 8%
where the time goes in v1:
time: 136 us; the launch traced here: 133 us
  starting transfers between devices  36.6 us (27%)
  Pallas kernels  34.3 us (25%)
  waiting for transfers between devices  28.7 us (21%)
  between operations  15.7 us (12%)
  local copies, waits for them, and re-layouts  15.1 us (11%)
  other arithmetic  2.77 us (2%)
    ppermute x17, starting transfers between devices, shifted(): return lax.ppermute(value, 'seq', pairs)  24.5 us
    pallas_call x1, Pallas kernels, run_tokens(): pl.pallas_call(functools.partial(token_kernel, plan, len(parts)), out_sha...  24.1 us
    ppermute x17, waiting for transfers between devices, shifted(): return lax.ppermute(value, 'seq', pairs)  19.1 us
    pallas_call x1, Pallas kernels, run_atoms(): pl.pallas_call(atom_kernel, out_shape=(jax.ShapeDtypeStruct((samples, ato...  10.2 us
    unnamed x40, local copies, waits for them, and re-layouts  9.75 us
    ppermute x1, starting transfers between devices, per_device(): after = lax.ppermute(packed, 'seq', to_previous)  6.54 us
    ppermute x1, waiting for transfers between devices, per_device(): lax.ppermute(atom_act[:, atoms - BEFORE:].reshape(samples * BEFORE, chann...  4.66 us
    ppermute x1, waiting for transfers between devices, per_device(): previous = lax.ppermute(back_rows[:, tokens - 1], 'seq', to_next)  4.2 us
  transfers between devices with their start and end apart: 21, of which 9 were waited for; matrix products, arithmetic and copies ran while one was open for 6% of the time, Pallas kernels for 8%

profile of v1, /device:TPU:6, one launch (start us, length us, event | category | flops | bytes accessed | tf_op | source)
XLA Modules:
  0.0 133.1 jit_solution(17892566514850291386)
XLA Ops:
  7.2 0.7 all-gather.2.cloned.1.call-update
  7.9 1.3 fusion.1
  10.5 0.8 slice.112
  11.3 0.8 slice.111
  12.1 0.7 convert_bitcast_fusion
  12.8 0.2 scatter.20
  13.0 6.5 %collective-permute-start.1 = (bf16[304,128]{1,0:T(8,128)(2,1)S(1)}, bf16[304,128]{1,0:T(8,128)(2,1)S(1)}, u32[]{:S(2)}, u32[]{:S(2)}) collective-permute-start(bf16[304,128]{1,0:T(8,128)(2,1)S(1)} %pad_maximum_fusion.2), channel_id=1, source_target_pairs={{1,0},{2,1},{3,2},{4,3},{5,4},{6,5},{7,6},{8,7},{9,8},{10,9},{11,1... | collective-permute-start | bytes 233480 | tf_op jit(solution)/shard_map/ppermute | solution.py:406
  19.6 0.7 slice.110
  20.3 1.9 %collective-permute-start = (bf16[96,128]{1,0:T(8,128)(2,1)S(1)}, bf16[96,128]{1,0:T(8,128)(2,1)S(1)}, u32[]{:S(2)}, u32[]{:S(2)}) collective-permute-start(bf16[96,128]{1,0:T(8,128)(2,1)S(1)} %bitcast.31), channel_id=1, source_target_pairs={{0,1},{1,2},{2,3},{3,4},{4,5},{5,6},{6,7},{7,8},{8,9},{9,10},{10,1... | collective-permute-start | bytes 73736 | tf_op jit(solution)/shard_map/ppermute | solution.py:407
  22.2 0.7 reshape.103.token_ref.refs_14_
  22.9 0.8 copy.22.range_ref
  23.7 0.7 reshape.104.token_gain_ref
  24.4 4.7 %collective-permute-done.before_ref = bf16[96,128]{1,0:T(8,128)(2,1)S(1)} collective-permute-done((bf16[96,128]{1,0:T(8,128)(2,1)S(1)}, bf16[96,128]{1,0:T(8,128)(2,1)S(1)}, u32[]{:S(2)}, u32[]{:S(2)}) %collective-permute-start) | collective-permute-done | bytes 24608 | tf_op jit(solution)/shard_map/ppermute | solution.py:407
  29.0 0.9 copy-done
  30.0 1.0 copy-done.1
  31.0 0.9 copy-done.2
  31.9 0.8 copy-done.4
  32.7 0.8 copy-done.5
  33.5 0.8 copy-done.6
  34.3 0.7 copy-done.7
  34.9 10.2 %atoms.1 = (bf16[2,384,128]{2,1,0:T(8,128)(2,1)S(1)}, bf16[2,48,768]{2,1,0:T(8,128)(2,1)S(1)}, bf16[2,48,768]{2,1,0:T(8,128)(2,1)S(1)}) custom-call(s32[12,2]{1,0:T(8,128)S(1)} %copy.22.range_ref, bf16[2,384,128]{2,1,0:T(8,128)(2,1)S(1)} %copy-done, bf16[96,128]{1,0:T(8,128)(2,1)S(1)} %collective-permute-done.before_ref, ...), custom_call_target="tpu_custom_call" | custom-call | flops 800000000 | bytes 4000000 | tf_op jit(solution)/shard_map/atoms/pallas_call | solution.py:163
  45.1 0.1 collective-permute-start.2
  45.3 6.5 %collective-permute-done.2 = bf16[2,48,768]{2,1,0:T(8,128)(2,1)S(1)} collective-permute-done((bf16[2,48,768]{2,1,0:T(8,128)(2,1)S(1)}, bf16[2,48,768]{2,1,0:T(8,128)(2,1)S(1)}, u32[]{:S(2)}, u32[]{:S(2)}) %collective-permute-start.2) | collective-permute-done | bytes 147488 | tf_op jit(solution)/shard_map/ppermute | solution.py:331
  51.8 1.1 collective-permute-start.4
  52.9 2.2 %collective-permute-start.3 = (bf16[96,768]{1,0:T(8,128)(2,1)S(1)}, bf16[96,768]{1,0:T(8,128)(2,1)S(1)}, u32[]{:S(2)}, u32[]{:S(2)}) collective-permute-start(bf16[96,768]{1,0:T(8,128)(2,1)S(1)} %pad_maximum_fusion), channel_id=1, source_target_pairs={{0,8},{1,9},{2,10},{3,11},{4,12},{5,13},{6,14},{7,15},{8,16},{9,17... | collective-permute-start | bytes 442376 | tf_op jit(solution)/shard_map/ppermute | solution.py:331
  55.2 2.1 %collective-permute-start.12 = (bf16[96,768]{1,0:T(8,128)(2,1)S(1)}, bf16[96,768]{1,0:T(8,128)(2,1)S(1)}, u32[]{:S(2)}, u32[]{:S(2)}) collective-permute-start(bf16[96,768]{1,0:T(8,128)(2,1)S(1)} %pad_maximum_fusion.1), channel_id=1, source_target_pairs={{0,6},{1,7},{2,0},{3,1},{4,2},{5,3},{6,4},{7,5},{8,14},{9,15},{10,... | collective-permute-start | bytes 442376 | tf_op jit(solution)/shard_map/ppermute | solution.py:331
  57.3 1.0 collective-permute-done.4
  58.3 3.3 %collective-permute-start.5 = (bf16[48,768]{1,0:T(8,128)(2,1)S(1)}, bf16[48,768]{1,0:T(8,128)(2,1)S(1)}, u32[]{:S(2)}, u32[]{:S(2)}) collective-permute-start(bf16[48,768]{1,0:T(8,128)(2,1)S(1)} %slice.132), channel_id=1, source_target_pairs={{0,8},{1,9},{2,10},{3,11},{4,12},{5,13},{6,14},{7,15},{8,16},{9,17... | collective-permute-start | bytes 221192 | tf_op jit(solution)/shard_map/ppermute | solution.py:331
  61.6 2.4 %collective-permute-start.14 = (bf16[48,768]{1,0:T(8,128)(2,1)S(1)}, bf16[48,768]{1,0:T(8,128)(2,1)S(1)}, u32[]{:S(2)}, u32[]{:S(2)}) collective-permute-start(bf16[48,768]{1,0:T(8,128)(2,1)S(1)} %slice.138), channel_id=1, source_target_pairs={{0,6},{1,7},{2,0},{3,1},{4,2},{5,3},{6,4},{7,5},{8,14},{9,15},{10,... | collective-permute-start | bytes 221192 | tf_op jit(solution)/shard_map/ppermute | solution.py:331
  64.0 0.1 collective-permute-start.13
  64.2 3.5 %collective-permute-start.8 = (bf16[384,768]{1,0:T(8,128)(2,1)S(1)}, bf16[384,768]{1,0:T(8,128)(2,1)S(1)}, u32[]{:S(2)}, u32[]{:S(2)}) collective-permute-start(bf16[384,768]{1,0:T(8,128)(2,1)S(1)} %constant_dynamic-update-slice_fusion.refs_0_), channel_id=1, source_target_pairs={{0,6},{1,7},{2,0},{3,1},{4,2},{5,3},{6,4},{7,5},{8,14},{9,15},{10,... | collective-permute-start | bytes 1769480 | tf_op jit(solution)/shard_map/ppermute | solution.py:331
  67.7 2.6 %collective-permute-done.13 = bf16[48,768]{1,0:T(8,128)(2,1)S(1)} collective-permute-done((bf16[48,768]{1,0:T(8,128)(2,1)S(1)}, bf16[48,768]{1,0:T(8,128)(2,1)S(1)}, u32[]{:S(2)}, u32[]{:S(2)}) %collective-permute-start.13) | collective-permute-done | bytes 73760 | tf_op jit(solution)/shard_map/ppermute | solution.py:331
  70.5 3.2 %collective-permute-start.15 = (bf16[384,768]{1,0:T(8,128)(2,1)S(1)}, bf16[384,768]{1,0:T(8,128)(2,1)S(1)}, u32[]{:S(2)}, u32[]{:S(2)}) collective-permute-start(bf16[384,768]{1,0:T(8,128)(2,1)S(1)} %constant_dynamic-update-slice_fusion.6.refs_5_), channel_id=1, source_target_pairs={{0,8},{1,9},{2,10},{3,11},{4,12},{5,13},{6,14},{7,15},{8,16},{9,17... | collective-permute-start | bytes 1769480 | tf_op jit(solution)/shard_map/ppermute | solution.py:331
  73.7 4.8 %collective-permute-done.8.refs_2_ = bf16[384,768]{1,0:T(8,128)(2,1)S(1)} collective-permute-done((bf16[384,768]{1,0:T(8,128)(2,1)S(1)}, bf16[384,768]{1,0:T(8,128)(2,1)S(1)}, u32[]{:S(2)}, u32[]{:S(2)}) %collective-permute-start.8) | collective-permute-done | bytes 589856 | tf_op jit(solution)/shard_map/ppermute | solution.py:331
  78.5 0.8 copy-done.8
  79.3 3.8 %collective-permute-start.10 = (bf16[192,768]{1,0:T(8,128)(2,1)S(1)}, bf16[192,768]{1,0:T(8,128)(2,1)S(1)}, u32[]{:S(2)}, u32[]{:S(2)}) collective-permute-start(bf16[192,768]{1,0:T(8,128)(2,1)S(1)} %slice.135), channel_id=1, source_target_pairs={{0,6},{1,7},{2,0},{3,1},{4,2},{5,3},{6,4},{7,5},{8,14},{9,15},{10,... | collective-permute-start | bytes 884744 | tf_op jit(solution)/shard_map/ppermute | solution.py:331
  83.2 0.7 copy-done.9
  84.1 0.7 copy-done.10
  84.8 0.8 copy-done.11
  85.6 2.5 %collective-permute-start.17 = (bf16[192,768]{1,0:T(8,128)(2,1)S(1)}, bf16[192,768]{1,0:T(8,128)(2,1)S(1)}, u32[]{:S(2)}, u32[]{:S(2)}) collective-permute-start(bf16[192,768]{1,0:T(8,128)(2,1)S(1)} %slice.139), channel_id=1, source_target_pairs={{0,8},{1,9},{2,10},{3,11},{4,12},{5,13},{6,14},{7,15},{8,16},{9,17... | collective-permute-start | bytes 884744 | tf_op jit(solution)/shard_map/ppermute | solution.py:331
  88.1 3.0 %collective-permute-done.9.refs_3_ = bf16[192,768]{1,0:T(8,128)(2,1)S(1)} collective-permute-done((bf16[192,768]{1,0:T(8,128)(2,1)S(1)}, bf16[192,768]{1,0:T(8,128)(2,1)S(1)}, u32[]{:S(2)}, u32[]{:S(2)}) %collective-permute-start.9) | collective-permute-done | bytes 294944 | tf_op jit(solution)/shard_map/ppermute | solution.py:331
  91.2 0.8 collective-permute-done.18.refs_9_
  92.0 0.4 collective-permute-done.17.refs_8_
  92.4 24.1 %tokens.1 = (bf16[2,384,128]{2,1,0:T(8,128)(2,1)}, bf16[2,48,768]{2,1,0:T(8,128)(2,1)}, bf16[2,48,128]{2,1,0:T(8,128)(2,1)S(1)}) custom-call(bf16[384,768]{1,0:T(8,128)(2,1)} %copy-done.13, bf16[384,768]{1,0:T(8,128)(2,1)} %copy-done.9, bf16[384,768]{1,0:T(8,128)(2,1)} %copy-done.8, bf16[192,768]{1,0:T(8,128)(2,1)S(1)} %collective-permute-done.9.refs_3_, ...), custom_call_target="tpu_custom_call" | custom-call | flops 10000000000 | bytes 20000000 | tf_op jit(solution)/shard_map/tokens/pallas_call | solution.py:302
  116.5 3.5 %collective-permute-start.19 = (bf16[2,128]{1,0:T(2,128)(2,1)S(1)}, bf16[2,128]{1,0:T(2,128)(2,1)S(1)}, u32[]{:S(2)}, u32[]{:S(2)}) collective-permute-start(bf16[2,128]{1,0:T(2,128)(2,1)S(1)} %bitcast.32), channel_id=1, source_target_pairs={{0,1},{1,2},{2,3},{3,4},{4,5},{5,6},{6,7},{7,8},{8,9},{9,10},{10,1... | collective-permute-start | bytes 1544 | tf_op jit(solution)/shard_map/ppermute | solution.py:438
  120.0 0.7 slice_compare_fusion
  120.7 4.2 %collective-permute-done.19 = bf16[2,128]{1,0:T(2,128)(2,1)S(1)} collective-permute-done((bf16[2,128]{1,0:T(2,128)(2,1)S(1)}, bf16[2,128]{1,0:T(2,128)(2,1)S(1)}, u32[]{:S(2)}, u32[]{:S(2)}) %collective-permute-start.19) | collective-permute-done | bytes 544 | tf_op jit(solution)/shard_map/ppermute | solution.py:438
  124.9 1.4 %fusion = bf16[2,384,128]{2,1,0:T(8,128)(2,1)} fusion(bf16[2,384,128]{2,1,0:T(8,128)(2,1)} %get-tuple-element.47, f32[2,128]{1,0:T(2,128)S(1)} %convert_element_type.27, pred[8]{0:T(512)(128)(4,1)S(1)} %slice_compare_fusion), kind=kLoop, calls=%fused_computation.20 | loop fusion | flops 8192 | bytes 9224 | tf_op jit(solution)/shard_map/dynamic_update_slice | solution.py:442
  (69 shorter events, 0.8 us)
Async XLA Ops:
  7.2 85.2 %all-gather.2.cloned.1.call-start = ((), (), s32[]{:S(2)}) async-start(), calls=%async_computation | async-start | bytes 2654208 | tf_op jit(solution)/shard_map/all_gather | solution.py:410
  13.0 16.0 %collective-permute-start.1 = (bf16[304,128]{1,0:T(8,128)(2,1)S(1)}, bf16[304,128]{1,0:T(8,128)(2,1)S(1)}, u32[]{:S(2)}, u32[]{:S(2)}) collective-permute-start(bf16[304,128]{1,0:T(8,128)(2,1)S(1)} %pad_maximum_fusion.2), channel_id=1, source_target_pairs={{1,0},{2,1},{3,2},{4,3},{5,4},{6,5},{7,6},{8,7},{9,8},{10,9},{11,1... | collective-permute-start | bytes 233480 | tf_op jit(solution)/shard_map/ppermute | solution.py:406
  20.3 8.7 %collective-permute-start = (bf16[96,128]{1,0:T(8,128)(2,1)S(1)}, bf16[96,128]{1,0:T(8,128)(2,1)S(1)}, u32[]{:S(2)}, u32[]{:S(2)}) collective-permute-start(bf16[96,128]{1,0:T(8,128)(2,1)S(1)} %bitcast.31), channel_id=1, source_target_pairs={{0,1},{1,2},{2,3},{3,4},{4,5},{5,6},{6,7},{7,8},{8,9},{9,10},{10,1... | collective-permute-start | bytes 73736 | tf_op jit(solution)/shard_map/ppermute | solution.py:407
  29.0 0.9 copy-start
  30.0 1.0 copy-start.1
  31.0 0.9 copy-start.2
  31.9 0.8 copy-start.4
  32.7 0.8 copy-start.5
  33.5 0.8 copy-start.6
  34.3 0.7 copy-start.7
  45.1 6.7 %collective-permute-start.2 = (bf16[2,48,768]{2,1,0:T(8,128)(2,1)S(1)}, bf16[2,48,768]{2,1,0:T(8,128)(2,1)S(1)}, u32[]{:S(2)}, u32[]{:S(2)}) collective-permute-start(bf16[2,48,768]{2,1,0:T(8,128)(2,1)S(1)} %get-tuple-element.44.refs_11_), channel_id=1, source_target_pairs={{0,1},{1,0},{2,3},{3,2},{4,5},{5,4},{6,7},{7,6},{8,9},{9,8},{10,11... | collective-permute-start | bytes 442376 | tf_op jit(solution)/shard_map/ppermute | solution.py:331
  51.8 6.4 %collective-permute-start.4 = (bf16[96,768]{1,0:T(8,128)(2,1)S(1)}, bf16[96,768]{1,0:T(8,128)(2,1)S(1)}, u32[]{:S(2)}, u32[]{:S(2)}) collective-permute-start(bf16[96,768]{1,0:T(8,128)(2,1)S(1)} %pad_maximum_fusion), channel_id=1, source_target_pairs={{0,24},{1,25},{2,26},{3,27},{4,28},{5,29},{6,30},{7,31},{8,0},{9,1... | collective-permute-start | bytes 442376 | tf_op jit(solution)/shard_map/ppermute | solution.py:331
  52.9 5.4 %collective-permute-start.3 = (bf16[96,768]{1,0:T(8,128)(2,1)S(1)}, bf16[96,768]{1,0:T(8,128)(2,1)S(1)}, u32[]{:S(2)}, u32[]{:S(2)}) collective-permute-start(bf16[96,768]{1,0:T(8,128)(2,1)S(1)} %pad_maximum_fusion), channel_id=1, source_target_pairs={{0,8},{1,9},{2,10},{3,11},{4,12},{5,13},{6,14},{7,15},{8,16},{9,17... | collective-permute-start | bytes 442376 | tf_op jit(solution)/shard_map/ppermute | solution.py:331
  55.2 6.4 %collective-permute-start.12 = (bf16[96,768]{1,0:T(8,128)(2,1)S(1)}, bf16[96,768]{1,0:T(8,128)(2,1)S(1)}, u32[]{:S(2)}, u32[]{:S(2)}) collective-permute-start(bf16[96,768]{1,0:T(8,128)(2,1)S(1)} %pad_maximum_fusion.1), channel_id=1, source_target_pairs={{0,6},{1,7},{2,0},{3,1},{4,2},{5,3},{6,4},{7,5},{8,14},{9,15},{10,... | collective-permute-start | bytes 442376 | tf_op jit(solution)/shard_map/ppermute | solution.py:331
  57.2 6.8 %collective-permute-start.11 = (bf16[96,768]{1,0:T(8,128)(2,1)S(1)}, bf16[96,768]{1,0:T(8,128)(2,1)S(1)}, u32[]{:S(2)}, u32[]{:S(2)}) collective-permute-start(bf16[96,768]{1,0:T(8,128)(2,1)S(1)} %pad_maximum_fusion.1), channel_id=1, source_target_pairs={{0,2},{1,3},{2,4},{3,5},{4,6},{5,7},{6,0},{7,1},{8,10},{9,11},{10,... | collective-permute-start | bytes 442376 | tf_op jit(solution)/shard_map/ppermute | solution.py:331
  57.3 30.9 %copy-start.14 = (f32[768]{0:T(1024)S(1)}, f32[768]{0:T(1024)}, u32[]{:S(2)}) copy-start(f32[768]{0:T(1024)} %param.39) | copy-start | bytes 9220
  57.3 35.1 %copy-start.3 = (bf16[768,128]{1,0:T(8,128)(2,1)S(1)}, bf16[768,128]{1,0:T(8,128)(2,1)}, u32[]{:S(2)}) copy-start(bf16[768,128]{1,0:T(8,128)(2,1)} %refs_21_.1) | copy-start | bytes 589828
  58.3 5.9 %collective-permute-start.6 = (bf16[48,768]{1,0:T(8,128)(2,1)S(1)}, bf16[48,768]{1,0:T(8,128)(2,1)S(1)}, u32[]{:S(2)}, u32[]{:S(2)}) collective-permute-start(bf16[48,768]{1,0:T(8,128)(2,1)S(1)} %slice.133), channel_id=1, source_target_pairs={{0,24},{1,25},{2,26},{3,27},{4,28},{5,29},{6,30},{7,31},{8,0},{9,1... | collective-permute-start | bytes 221192 | tf_op jit(solution)/shard_map/ppermute | solution.py:331
  58.3 5.9 %collective-permute-start.5 = (bf16[48,768]{1,0:T(8,128)(2,1)S(1)}, bf16[48,768]{1,0:T(8,128)(2,1)S(1)}, u32[]{:S(2)}, u32[]{:S(2)}) collective-permute-start(bf16[48,768]{1,0:T(8,128)(2,1)S(1)} %slice.132), channel_id=1, source_target_pairs={{0,8},{1,9},{2,10},{3,11},{4,12},{5,13},{6,14},{7,15},{8,16},{9,17... | collective-permute-start | bytes 221192 | tf_op jit(solution)/shard_map/ppermute | solution.py:331
  61.6 8.8 %collective-permute-start.14 = (bf16[48,768]{1,0:T(8,128)(2,1)S(1)}, bf16[48,768]{1,0:T(8,128)(2,1)S(1)}, u32[]{:S(2)}, u32[]{:S(2)}) collective-permute-start(bf16[48,768]{1,0:T(8,128)(2,1)S(1)} %slice.138), channel_id=1, source_target_pairs={{0,6},{1,7},{2,0},{3,1},{4,2},{5,3},{6,4},{7,5},{8,14},{9,15},{10,... | collective-permute-start | bytes 221192 | tf_op jit(solution)/shard_map/ppermute | solution.py:331
  64.0 6.3 %collective-permute-start.13 = (bf16[48,768]{1,0:T(8,128)(2,1)S(1)}, bf16[48,768]{1,0:T(8,128)(2,1)S(1)}, u32[]{:S(2)}, u32[]{:S(2)}) collective-permute-start(bf16[48,768]{1,0:T(8,128)(2,1)S(1)} %slice.137), channel_id=1, source_target_pairs={{0,2},{1,3},{2,4},{3,5},{4,6},{5,7},{6,0},{7,1},{8,10},{9,11},{10,... | collective-permute-start | bytes 221192 | tf_op jit(solution)/shard_map/ppermute | solution.py:331
  64.2 20.5 %copy-start.13 = (bf16[384,768]{1,0:T(8,128)(2,1)}, bf16[384,768]{1,0:T(8,128)(2,1)S(1)}, u32[]{:S(2)}) copy-start(bf16[384,768]{1,0:T(8,128)(2,1)S(1)} %constant_dynamic-update-slice_fusion.refs_0_) | copy-start | bytes 1769476
  64.2 14.2 %collective-permute-start.8 = (bf16[384,768]{1,0:T(8,128)(2,1)S(1)}, bf16[384,768]{1,0:T(8,128)(2,1)S(1)}, u32[]{:S(2)}, u32[]{:S(2)}) collective-permute-start(bf16[384,768]{1,0:T(8,128)(2,1)S(1)} %constant_dynamic-update-slice_fusion.refs_0_), channel_id=1, source_target_pairs={{0,6},{1,7},{2,0},{3,1},{4,2},{5,3},{6,4},{7,5},{8,14},{9,15},{10,... | collective-permute-start | bytes 1769480 | tf_op jit(solution)/shard_map/ppermute | solution.py:331
  67.7 15.4 %collective-permute-start.7 = (bf16[384,768]{1,0:T(8,128)(2,1)S(1)}, bf16[384,768]{1,0:T(8,128)(2,1)S(1)}, u32[]{:S(2)}, u32[]{:S(2)}) collective-permute-start(bf16[384,768]{1,0:T(8,128)(2,1)S(1)} %constant_dynamic-update-slice_fusion.refs_0_), channel_id=1, source_target_pairs={{0,2},{1,3},{2,4},{3,5},{4,6},{5,7},{6,0},{7,1},{8,10},{9,11},{10,... | collective-permute-start | bytes 1769480 | tf_op jit(solution)/shard_map/ppermute | solution.py:331
  70.4 14.4 %copy-start.12 = (bf16[384,768]{1,0:T(8,128)(2,1)}, bf16[384,768]{1,0:T(8,128)(2,1)S(1)}, u32[]{:S(2)}) copy-start(bf16[384,768]{1,0:T(8,128)(2,1)S(1)} %constant_dynamic-update-slice_fusion.6.refs_5_) | copy-start | bytes 1769476
  70.4 12.8 %collective-permute-start.16 = (bf16[384,768]{1,0:T(8,128)(2,1)S(1)}, bf16[384,768]{1,0:T(8,128)(2,1)S(1)}, u32[]{:S(2)}, u32[]{:S(2)}) collective-permute-start(bf16[384,768]{1,0:T(8,128)(2,1)S(1)} %constant_dynamic-update-slice_fusion.6.refs_5_), channel_id=1, source_target_pairs={{0,24},{1,25},{2,26},{3,27},{4,28},{5,29},{6,30},{7,31},{8,0},{9,1... | collective-permute-start | bytes 1769480 | tf_op jit(solution)/shard_map/ppermute | solution.py:331
  70.5 13.6 %collective-permute-start.15 = (bf16[384,768]{1,0:T(8,128)(2,1)S(1)}, bf16[384,768]{1,0:T(8,128)(2,1)S(1)}, u32[]{:S(2)}, u32[]{:S(2)}) collective-permute-start(bf16[384,768]{1,0:T(8,128)(2,1)S(1)} %constant_dynamic-update-slice_fusion.6.refs_5_), channel_id=1, source_target_pairs={{0,8},{1,9},{2,10},{3,11},{4,12},{5,13},{6,14},{7,15},{8,16},{9,17... | collective-permute-start | bytes 1769480 | tf_op jit(solution)/shard_map/ppermute | solution.py:331
  78.5 0.8 copy-start.8
  79.3 8.8 %collective-permute-start.10 = (bf16[192,768]{1,0:T(8,128)(2,1)S(1)}, bf16[192,768]{1,0:T(8,128)(2,1)S(1)}, u32[]{:S(2)}, u32[]{:S(2)}) collective-permute-start(bf16[192,768]{1,0:T(8,128)(2,1)S(1)} %slice.135), channel_id=1, source_target_pairs={{0,6},{1,7},{2,0},{3,1},{4,2},{5,3},{6,4},{7,5},{8,14},{9,15},{10,... | collective-permute-start | bytes 884744 | tf_op jit(solution)/shard_map/ppermute | solution.py:331
  83.1 0.8 copy-start.9
  83.1 8.0 %collective-permute-start.9 = (bf16[192,768]{1,0:T(8,128)(2,1)S(1)}, bf16[192,768]{1,0:T(8,128)(2,1)S(1)}, u32[]{:S(2)}, u32[]{:S(2)}) collective-permute-start(bf16[192,768]{1,0:T(8,128)(2,1)S(1)} %slice.134), channel_id=1, source_target_pairs={{0,2},{1,3},{2,4},{3,5},{4,6},{5,7},{6,0},{7,1},{8,10},{9,11},{10,... | collective-permute-start | bytes 884744 | tf_op jit(solution)/shard_map/ppermute | solution.py:331
  83.9 0.8 copy-start.10
  84.0 8.0 %collective-permute-start.18 = (bf16[192,768]{1,0:T(8,128)(2,1)S(1)}, bf16[192,768]{1,0:T(8,128)(2,1)S(1)}, u32[]{:S(2)}, u32[]{:S(2)}) collective-permute-start(bf16[192,768]{1,0:T(8,128)(2,1)S(1)} %slice.140), channel_id=1, source_target_pairs={{0,24},{1,25},{2,26},{3,27},{4,28},{5,29},{6,30},{7,31},{8,0},{9,1... | collective-permute-start | bytes 884744 | tf_op jit(solution)/shard_map/ppermute | solution.py:331
  84.8 0.8 copy-start.11
  85.6 6.8 %collective-permute-start.17 = (bf16[192,768]{1,0:T(8,128)(2,1)S(1)}, bf16[192,768]{1,0:T(8,128)(2,1)S(1)}, u32[]{:S(2)}, u32[]{:S(2)}) collective-permute-start(bf16[192,768]{1,0:T(8,128)(2,1)S(1)} %slice.139), channel_id=1, source_target_pairs={{0,8},{1,9},{2,10},{3,11},{4,12},{5,13},{6,14},{7,15},{8,16},{9,17... | collective-permute-start | bytes 884744 | tf_op jit(solution)/shard_map/ppermute | solution.py:331
  116.5 8.4 %collective-permute-start.19 = (bf16[2,128]{1,0:T(2,128)(2,1)S(1)}, bf16[2,128]{1,0:T(2,128)(2,1)S(1)}, u32[]{:S(2)}, u32[]{:S(2)}) collective-permute-start(bf16[2,128]{1,0:T(2,128)(2,1)S(1)} %bitcast.32), channel_id=1, source_target_pairs={{0,1},{1,2},{2,3},{3,4},{4,5},{5,6},{6,7},{7,8},{8,9},{9,10},{10,1... | collective-permute-start | bytes 1544 | tf_op jit(solution)/shard_map/ppermute | solution.py:438
Sparse Core Ops, SparseCore 0:
  9.8 41.2 all-gather.1

commit v2 on v1

v2 whole, which is shorter than its diff:
```python
import functools
import math

import jax
import jax.numpy as jnp
from jax import lax
from jax.experimental import pallas as pl
from jax.experimental.pallas import tpu as pltpu
from jax.sharding import PartitionSpec as P

AH = 4
HEADS = 16
WQ = 32
WK = 128
EDGE = 48
APT = 8
BEFORE = EDGE
AFTER = WQ + EDGE
META = 16
GROUP = 8

EPSILON = 1e-05
NEGATIVE = -1e30
F32 = jnp.float32
BF16 = jnp.bfloat16

NT = (((1,), (1,)), ((), ()))
TN = (((0,), (0,)), ((), ()))


def dot(a, b):
    return jnp.dot(a, b, preferred_element_type=F32)


def dot_nt(a, b):
    return lax.dot_general(a, b, NT, preferred_element_type=F32)


def dot_tn(a, b):
    return lax.dot_general(a, b, TN, preferred_element_type=F32)


def layer_norm(widened, gain):
    centred = widened - jnp.mean(widened, axis=-1, keepdims=True)
    variance = jnp.mean(centred * centred, axis=-1, keepdims=True)
    return (centred * lax.rsqrt(variance + EPSILON) * gain).astype(BF16)


def lane_group(rows, lanes, width):
    return lax.broadcasted_iota(jnp.int32, (rows, lanes), 1) // width


def pack_kernel(range_ref, act_hbm, bias_hbm, first_ref, last_ref, sems):
    samples, atoms, _ = act_hbm.shape
    bias_at = samples * AFTER
    meta_at = bias_at + AH * WQ
    copies = []
    for s in range(samples):
        copies.append((act_hbm.at[s, :AFTER], first_ref.at[AFTER * s : AFTER * (s + 1)]))
        copies.append((act_hbm.at[s, atoms - BEFORE :], last_ref.at[BEFORE * s : BEFORE * (s + 1)]))
    for h in range(AH):
        copies.append((bias_hbm.at[h, 0], first_ref.at[bias_at + WQ * h : bias_at + WQ * (h + 1)]))
    started = []
    for i, (source, target) in enumerate(copies):
        copy = pltpu.make_async_copy(source, target, sems.at[i])
        copy.start()
        started.append(copy)
    start = lax.axis_index("seq") * atoms - EDGE
    row = lax.broadcasted_iota(jnp.int32, (META, WK), 0)
    meta = jnp.where(row == 0, range_ref[0, 0] - start, range_ref[0, 1] - start)
    first_ref[meta_at : meta_at + META, :] = meta.astype(F32).astype(BF16)
    for copy in started:
        copy.wait()


def run_pack(key_range, act, bias):
    samples, _, channels = act.shape
    return pl.pallas_call(
        pack_kernel,
        out_shape=(
            jax.ShapeDtypeStruct((samples * AFTER + AH * WQ + META, channels), BF16),
            jax.ShapeDtypeStruct((samples * BEFORE, channels), BF16),
        ),
        in_specs=[smem(), anywhere(), anywhere()],
        out_specs=(vmem(), vmem()),
        scratch_shapes=[pltpu.SemaphoreType.DMA((2 * samples + AH,))],
        compiler_params=pltpu.CompilerParams(vmem_limit_bytes=60 * 2**20),
        name="pack",
    )(key_range, act, bias)


def atom_kernel(
    range_ref,
    count_ref,
    before_ref,
    after_ref,
    gain_ref,
    token_ref,
    token_gain_ref,
    act_hbm,
    query_hbm,
    keyval_hbm,
    bias_hbm,
    output_hbm,
    gather_hbm,
    mid_ref,
    tokact_ref,
    norm_ref,
    act_ref,
    query_ref,
    keyval_ref,
    bias_ref,
    output_ref,
    gather_ref,
    att_ref,
    sems,
):
    copies = []
    for i, (source, target) in enumerate(
        (
            (act_hbm, act_ref),
            (query_hbm, query_ref),
            (keyval_hbm, keyval_ref),
            (bias_hbm, bias_ref),
            (output_hbm, output_ref),
            (gather_hbm, gather_ref),
        )
    ):
        copy = pltpu.make_async_copy(source, target, sems.at[i])
        copy.start()
        copies.append(copy)
    samples, atoms, channels = act_ref.shape
    windows = atoms // WQ
    tokens = norm_ref.shape[1]
    head_width = channels // AH
    scale = 1.0 / math.sqrt(head_width)
    device = lax.axis_index("seq")
    gain = gain_ref[...]
    bias_at = samples * AFTER
    meta_at = bias_at + AH * WQ

    head_of = lane_group(WQ, channels, head_width)
    masks = [(head_of == h).astype(BF16) for h in range(AH)]
    masks32 = [(head_of == h).astype(F32) for h in range(AH)]
    index = lax.broadcasted_iota(jnp.int32, (1, WK), 1)

    meta = after_ref[meta_at : meta_at + META, :].astype(F32)
    indexf = index.astype(F32)
    valid_after = (indexf >= meta[0:1, :]) & (indexf < meta[1:2, :])

    slot = token_ref[...] - device * tokens
    own_table = (lax.broadcasted_iota(jnp.int32, (tokens, atoms), 0) == slot).astype(F32)
    own_counts = jnp.sum(own_table, axis=1, keepdims=True)
    own_table = own_table.astype(BF16)
    row = lax.broadcasted_iota(jnp.int32, (tokens, 1), 0)
    remaining = jnp.where(
        row == tokens - 1, count_ref[tokens - 1].astype(F32) - own_counts, jnp.zeros_like(own_counts)
    )
    lane = lax.broadcasted_iota(jnp.int32, (tokens, WQ), 1).astype(F32)
    after_table = (lane < remaining).astype(BF16)
    counts = jnp.maximum(own_counts + remaining, 1.0)

    for copy in copies[:4]:
        copy.wait()
    for s in range(samples):
        extended = jnp.concatenate(
            [
                before_ref[s * BEFORE : (s + 1) * BEFORE, :],
                act_ref[s],
                after_ref[s * AFTER : (s + 1) * AFTER, :],
            ],
            axis=0,
        ).astype(F32)
        normed = layer_norm(extended, gain)
        queries = dot(normed, query_ref[...]).astype(BF16)
        keyvals = dot(normed, keyval_ref[...]).astype(BF16)
        for w in range(windows + 1):
            q = queries[BEFORE + WQ * w : BEFORE + WQ * (w + 1), :]
            keys = keyvals[WQ * w : WQ * w + WK, :channels]
            values = keyvals[WQ * w : WQ * w + WK, channels:]
            stacked = jnp.concatenate([q * m for m in masks], axis=0)
            scores = dot_nt(stacked, keys) * scale
            if w < windows:
                bias = bias_ref[:, w].reshape(AH * WQ, WK)
                start = (device * windows + w) * WQ - EDGE
                valid = (index >= range_ref[w, 0] - start) & (index < range_ref[w, 1] - start)
            else:
                bias = after_ref[bias_at : bias_at + AH * WQ, :]
                valid = valid_after
            scores = jnp.where(valid, scores + bias.astype(F32), NEGATIVE)
            exponent = jnp.exp(scores - jnp.max(scores, axis=-1, keepdims=True))
            total = jnp.sum(exponent, axis=-1, keepdims=True)
            mixed = dot(exponent.astype(BF16), values) / total
            attended = mixed[:WQ] * masks32[0]
            for h in range(1, AH):
                attended = attended + mixed[WQ * h : WQ * (h + 1)] * masks32[h]
            att_ref[s, WQ * w : WQ * (w + 1), :] = attended.astype(BF16)
        if s == 0:
            copies[4].wait()
            copies[5].wait()
        merged = dot(att_ref[s], output_ref[...])
        mid = (extended[BEFORE : BEFORE + atoms + WQ, :] + merged).astype(BF16)
        mid_ref[s] = mid[:atoms]
        hidden = jnp.maximum(dot(mid, gather_ref[...]), 0.0).astype(BF16)
        sums = dot(own_table, hidden[:atoms]) + dot(after_table, hidden[atoms:])
        token_act = (sums / counts).astype(BF16)
        tokact_ref[s] = token_act
        norm_ref[s] = layer_norm(token_act.astype(F32), token_gain_ref[...])


def vmem():
    return pl.BlockSpec(memory_space=pltpu.VMEM)


def smem():
    return pl.BlockSpec(memory_space=pltpu.SMEM)


def anywhere():
    return pl.BlockSpec(memory_space=pl.ANY)


def run_atoms(key_range, counts, before, after, gain, token, token_gain, *arrays):
    samples, atoms, channels = arrays[0].shape
    width = arrays[-1].shape[1]
    tokens = atoms // APT
    return pl.pallas_call(
        atom_kernel,
        out_shape=(
            jax.ShapeDtypeStruct((samples, atoms, channels), BF16),
            jax.ShapeDtypeStruct((samples, tokens, width), BF16),
            jax.ShapeDtypeStruct((samples, tokens, width), BF16),
        ),
        in_specs=[smem()] * 2 + [vmem()] * 5 + [anywhere()] * len(arrays),
        out_specs=(vmem(),) * 3,
        scratch_shapes=[pltpu.VMEM(a.shape, a.dtype) for a in arrays]
        + [
            pltpu.VMEM((samples, atoms + WQ, channels), BF16),
            pltpu.SemaphoreType.DMA((len(arrays),)),
        ],
        compiler_params=pltpu.CompilerParams(vmem_limit_bytes=60 * 2**20),
        cost_estimate=pl.CostEstimate(
            flops=800_000_000, bytes_accessed=4_000_000, transcendentals=500_000
        ),
        name="atoms",
    )(key_range, counts, before, after, gain, token, token_gain, *arrays)


def block_rows(dx, dy, dz, rows):
    device = lax.axis_index("seq")
    x, y, z = device // 8, (device // 2) % 4, device % 2
    source = ((x + dx) % 4) * 8 + ((y + dy) % 4) * 2 + (z + dz) % 2
    return source * rows


def query_kernel(norm_ref, query_hbm, keyval_hbm, absorbed_ref, query_ref, key_ref, sems):
    samples, tokens, width = norm_ref.shape
    first = pltpu.make_async_copy(query_hbm, query_ref, sems.at[0])
    second = pltpu.make_async_copy(keyval_hbm.at[:, :width], key_ref, sems.at[1])
    first.start()
    second.start()
    head_size = width // HEADS
    scale = 1.0 / math.sqrt(head_size)
    lanes = GROUP * head_size
    head_of = lane_group(tokens, lanes, head_size)
    masks = [(head_of == h).astype(BF16) for h in range(GROUP)]
    first.wait()
    queries = dot(norm_ref[...].reshape(samples * tokens, width), query_ref[...]).astype(BF16)
    second.wait()
    for s in range(samples):
        for g in range(HEADS // GROUP):
            columns = slice(lanes * g, lanes * (g + 1))
            q = queries[tokens * s : tokens * (s + 1), columns]
            stacked = jnp.concatenate([q * m for m in masks], axis=0)
            absorbed = dot_nt(stacked, key_ref[:, columns]) * scale
            absorbed_ref[s, lanes * g : lanes * (g + 1)] = absorbed.astype(BF16)


def run_queries(norm, token_query, token_keyval):
    samples, tokens, width = norm.shape
    return pl.pallas_call(
        query_kernel,
        out_shape=jax.ShapeDtypeStruct((samples, HEADS * tokens, width), BF16),
        in_specs=[vmem(), anywhere(), anywhere()],
        out_specs=vmem(),
        scratch_shapes=[
            pltpu.VMEM((width, width), BF16),
            pltpu.VMEM((width, width), BF16),
            pltpu.SemaphoreType.DMA((2,)),
        ],
        compiler_params=pltpu.CompilerParams(vmem_limit_bytes=30 * 2**20),
        cost_estimate=pl.CostEstimate(
            flops=2_000_000_000, bytes_accessed=5_000_000, transcendentals=0
        ),
        name="queries",
    )(norm, token_query, token_keyval)


def token_kernel(plan, bias_plan, pieces, *refs):
    parts = refs[:pieces]
    (
        bias_near_hbm,
        bias_far_hbm,
        absorbed_ref,
        tokact_ref,
        mid_ref,
        token_ref,
        gain_ref,
        keyval_hbm,
        output_hbm,
        gate_hbm,
        down_hbm,
        back_hbm,
        atom_out_ref,
        token_out_ref,
        back_rows_ref,
        all_ref,
        bias_ref,
        value_ref,
        output_ref,
        gate_ref,
        down_ref,
        back_ref,
        att_ref,
        weight_sems,
        part_sems,
        bias_sems,
    ) = refs[pieces:]
    samples, tokens, width = tokact_ref.shape
    head_size = width // HEADS
    device = lax.axis_index("seq")
    mine = lax.axis_index("samp")

    part_copies = []
    for i, (part, at, sample, offset) in enumerate(plan):
        target = pl.multiple_of(block_rows(*offset, tokens), 16)
        copy = pltpu.make_async_copy(
            parts[part].at[at : at + tokens],
            all_ref.at[sample, pl.ds(target, tokens)],
            part_sems.at[i],
        )
        copy.start()
        part_copies.append(copy)
    bias_copies = []
    for i, (near, at, hop) in enumerate(bias_plan):
        source = (mine // 2 + hop) % 4 * 2 + (mine % 2 if near else 1 - mine % 2)
        heads = bias_ref.shape[0] // len(bias_plan)
        copy = pltpu.make_async_copy(
            (bias_near_hbm if near else bias_far_hbm).at[at],
            bias_ref.at[pl.ds(source * heads, heads)],
            bias_sems.at[i],
        )
        copy.start()
        bias_copies.append(copy)
    weight_copies = []
    for i, (source, target) in enumerate(
        (
            (keyval_hbm.at[:, width:], value_ref),
            (output_hbm, output_ref),
            (gate_hbm, gate_ref),
            (down_hbm, down_ref),
            (back_hbm, back_ref),
        )
    ):
        copy = pltpu.make_async_copy(source, target, weight_sems.at[i])
        copy.start()
        weight_copies.append(copy)

    lanes = GROUP * head_size
    head_of = lane_group(tokens, lanes, head_size)
    masks32 = [(head_of == h).astype(F32) for h in range(GROUP)]
    for copy in part_copies:
        copy.wait()
    for copy in bias_copies:
        copy.wait()
    for s in range(samples):
        for g in range(HEADS // GROUP):
            columns = slice(lanes * g, lanes * (g + 1))
            scores = dot_nt(absorbed_ref[s, columns], all_ref[s])
            bias = bias_ref[GROUP * g : GROUP * (g + 1)].reshape(GROUP * tokens, -1)
            scores = scores + bias.astype(F32)
            exponent = jnp.exp(scores - jnp.max(scores, axis=-1, keepdims=True))
            total = jnp.sum(exponent, axis=-1, keepdims=True)
            mixed = dot(exponent.astype(BF16), all_ref[s]) / total
            if s == 0 and g == 0:
                weight_copies[0].wait()
            valued = dot(mixed.astype(BF16), value_ref[:, columns])
            attended = valued[:tokens] * masks32[0]
            for h in range(1, GROUP):
                attended = attended + valued[tokens * h : tokens * (h + 1)] * masks32[h]
            att_ref[tokens * s : tokens * (s + 1), columns] = attended.astype(BF16)

    weight_copies[1].wait()
    merged = dot(att_ref[...], output_ref[...])
    token_act = tokact_ref[...].reshape(samples * tokens, width).astype(F32)
    token_mid = (token_act + merged).astype(BF16).astype(F32)
    trans = layer_norm(token_mid, gain_ref[...])
    weight_copies[2].wait()
    hidden_width = down_ref.shape[0]
    gate = dot(trans, gate_ref[:, :hidden_width])
    up = dot(trans, gate_ref[:, hidden_width:])
    hidden = (gate / (1.0 + jnp.exp(-gate)) * up).astype(BF16)
    weight_copies[3].wait()
    token_out = (token_mid + dot(hidden, down_ref[...])).astype(BF16)
    token_out_ref[...] = token_out.reshape(samples, tokens, width)
    weight_copies[4].wait()
    back_rows = dot(token_out, back_ref[...]).astype(BF16)
    back_rows_ref[...] = back_rows.reshape(samples, tokens, -1)
    atoms = mid_ref.shape[1]
    slot = token_ref[...] - device * tokens
    table = (lax.broadcasted_iota(jnp.int32, (tokens, atoms), 0) == slot).astype(BF16)
    for s in range(samples):
        gathered = dot_tn(table, back_rows[tokens * s : tokens * (s + 1)])
        atom_out_ref[s] = (mid_ref[s].astype(F32) + gathered).astype(BF16)


def run_tokens(plan, parts, bias_plan, bias_near, bias_far, absorbed, tokact, mid, token, gain, weights):
    samples, tokens, width = tokact.shape
    keys = bias_near.shape[-1]
    return pl.pallas_call(
        functools.partial(token_kernel, plan, bias_plan, len(parts)),
        out_shape=(
            jax.ShapeDtypeStruct(mid.shape, BF16),
            jax.ShapeDtypeStruct(tokact.shape, BF16),
            jax.ShapeDtypeStruct((samples, tokens, mid.shape[2]), BF16),
        ),
        in_specs=[anywhere()] * (len(parts) + 2) + [vmem()] * 5 + [anywhere()] * 5,
        out_specs=(vmem(),) * 3,
        scratch_shapes=[
            pltpu.VMEM((samples, keys, width), BF16),
            pltpu.VMEM((HEADS, tokens, keys), BF16),
            pltpu.VMEM((width, width), BF16),
        ]
        + [pltpu.VMEM(w.shape, w.dtype) for w in weights[1:]]
        + [
            pltpu.VMEM((samples * tokens, width), BF16),
            pltpu.SemaphoreType.DMA((len(weights),)),
            pltpu.SemaphoreType.DMA((len(plan),)),
            pltpu.SemaphoreType.DMA((len(bias_plan),)),
        ],
        compiler_params=pltpu.CompilerParams(vmem_limit_bytes=44 * 2**20),
        cost_estimate=pl.CostEstimate(
            flops=10_000_000_000, bytes_accessed=20_000_000, transcendentals=3_000_000
        ),
        name="tokens",
    )(*parts, bias_near, bias_far, absorbed, tokact, mid, token, gain, *weights)


def shifted(value, dx, dy, dz=0):
    pairs = []
    for t in range(32):
        x, y, z = t // 8, (t // 2) % 4, t % 2
        pairs.append((t, ((x + dx) % 4) * 8 + ((y + dy) % 4) * 2 + (z + dz) % 2))
    return lax.ppermute(value, "seq", pairs)


def line_of(value, dx, dy):
    return [
        value,
        shifted(value, dx, dy),
        shifted(value, -dx, -dy),
        shifted(value, 2 * dx, 2 * dy),
    ]


def spread(norm):
    samples, tokens, _ = norm.shape
    other = shifted(norm, 0, 0, 1)
    parts, plan = [], []
    for s in range(samples):
        dx, dy = (0, 1) if s % 2 == 0 else (1, 0)
        first = jnp.concatenate([norm[s], other[s]], axis=0)
        line = line_of(first, dx, dy)
        plane = line_of(jnp.concatenate(line, axis=0), dy, dx)
        steps = (0, -1, 1, 2)
        base = len(parts)
        parts += plane
        for piece, far in enumerate(steps):
            for k in range(2 * len(steps)):
                near = steps[k // 2]
                offset = (near * dx + far * dy, near * dy + far * dx, k % 2)
                plan.append((base + piece, k * tokens, s, offset))
    return parts, plan, parts[1]


def stack_kernel(count, *refs):
    pieces, stacked, sems = refs[:count], refs[-2], refs[-1]
    copies = []
    for i, piece in enumerate(pieces):
        copy = pltpu.make_async_copy(piece, stacked.at[i], sems.at[i])
        copy.start()
        copies.append(copy)
    for copy in copies:
        copy.wait()


def run_stack(pieces, after):
    count = len(pieces)
    return pl.pallas_call(
        functools.partial(stack_kernel, count),
        out_shape=jax.ShapeDtypeStruct((count,) + pieces[0].shape, pieces[0].dtype),
        in_specs=[anywhere()] * (count + 1),
        out_specs=anywhere(),
        scratch_shapes=[pltpu.SemaphoreType.DMA((count,))],
        compiler_params=pltpu.CompilerParams(vmem_limit_bytes=60 * 2**20),
        name="stack",
    )(*pieces, after)


BIAS_STEPS = (0, -1, 1, 2)


def column_of(bias):
    count = lax.axis_size("samp")

    def hop(by):
        return lax.ppermute(bias, "samp", [(i, (i + 2 * by) % count) for i in range(count)])

    return [bias, hop(1), hop(-1), hop(2)]


def other_core(value):
    return lax.ppermute(value, "samp", [(i, i ^ 1) for i in range(lax.axis_size("samp"))])


def per_device(
    atom_act,
    atom_gain,
    atom_query,
    atom_keyval,
    atom_output,
    atom_bias,
    key_range,
    atom_token,
    token_counts,
    gather_weight,
    token_gain,
    token_query,
    token_keyval,
    token_output,
    pair_bias,
    trans_gain,
    trans_gate_up,
    trans_down,
    back_weight,
):
    samples, atoms, channels = atom_act.shape
    tokens = token_counts.shape[0]
    device = lax.axis_index("seq")
    count = lax.axis_size("seq")
    to_next = [(i, i + 1) for i in range(count - 1)]
    to_previous = [(i + 1, i) for i in range(count - 1)]

    first, last = run_pack(key_range, atom_act, atom_bias)
    after = lax.ppermute(first, "seq", to_previous)
    before = lax.ppermute(last, "seq", to_next)
    column = column_of(pair_bias)
    token_row = atom_token.reshape(1, atoms)
    atom_mid, token_act, token_norm = run_atoms(
        key_range,
        token_counts,
        before,
        after,
        atom_gain.reshape(1, -1),
        token_row,
        token_gain.reshape(1, -1),
        atom_act,
        atom_query,
        atom_keyval,
        atom_bias,
        atom_output,
        gather_weight,
    )
    absorbed = run_queries(token_norm, token_query, token_keyval)
    parts, plan, ready = spread(token_norm)
    bias_near = run_stack(column, ready)
    bias_far = other_core(bias_near)
    bias_plan = [(side == 0, at, step) for side in range(2) for at, step in enumerate(BIAS_STEPS)]
    atom_out, token_out, back_rows = run_tokens(
        plan,
        parts,
        bias_plan,
        bias_near,
        bias_far,
        absorbed,
        token_act,
        atom_mid,
        token_row,
        trans_gain.reshape(1, -1),
        [token_keyval, token_output, trans_gate_up, trans_down, back_weight],
    )
    previous = lax.ppermute(back_rows[:, tokens - 1], "seq", to_next)
    earlier = (atom_token[:APT] < device * tokens)[None, :, None]
    extra = jnp.where(earlier, previous[:, None, :].astype(F32), 0.0)
    head = (atom_out[:, :APT].astype(F32) + extra).astype(BF16)
    atom_out = lax.dynamic_update_slice(atom_out, head, (0, 0, 0))
    return (atom_out, token_out)


def solution(mesh):
    placed = (
        P("samp", "seq", None),
        P(),
        P(),
        P(),
        P(),
        P(None, "seq", None, None),
        P("seq", None),
        P("seq"),
        P("seq"),
        P(),
        P(),
        P(),
        P(),
        P(),
        P("samp", "seq", None),
        P(),
        P(),
        P(),
        P(),
    )
    return jax.shard_map(
        per_device,
        mesh=mesh,
        in_specs=placed,
        out_specs=(P("samp", "seq", None), P("samp", "seq", None)),
        check_vma=False,
    )
```

time: 136 us -> 182 us (1.34)
  Pallas kernels: 34.3 us -> 74.5 us
  waiting for transfers between devices: 28.7 us -> 54.8 us
  between operations: 15.7 us -> 0.98 us
  local copies, waits for them, and re-layouts: 15.1 us -> 11.2 us
    pallas_call x1 -> x4, Pallas kernels: 24.1 us -> 64 us  [the longest x1 36.9 us: run_stack(): pl.pallas_call(functools.partial(stack_kernel, count), out_shape=jax.Shap...]
    ppermute x17 -> x13, waiting for transfers between devices: 19.1 us -> 43.8 us  [shifted(): return lax.ppermute(value, 'seq', pairs)]
    ppermute x2 -> x6, starting transfers between devices: 8.45 us -> 21.8 us  [the longest x3 13.3 us: hop(): lax.ppermute(bias, 'samp', [(i, (i + 2 * by) % count) for i in range(coun...]
    ppermute x17 -> x13, starting transfers between devices: 24.5 us -> 11.4 us  [shifted(): return lax.ppermute(value, 'seq', pairs)]
    slice x12 -> x0, local copies, waits for them, and re-layouts: 3.67 us -> none  [the longest x1 1.27 us: per_device(): meta = meta.at[1].set((key_range[0, 1] - first_start).astype(F32))]
    ppermute x2 -> x6, waiting for transfers between devices: 4.66 us -> 7.39 us  [the longest x1 4.5 us: per_device(): before = lax.ppermute(last, 'seq', to_next)]
    unnamed x40 -> x46, local copies, waits for them, and re-layouts: 9.75 us -> 7.7 us
  transfers between devices with their start and end apart: 21 -> 20, of which waited for: 9 -> 13; matrix products, arithmetic and copies ran while one was open for 6% -> 2% of each run, Pallas kernels for 8% -> 22%
where the time goes in v2:
time: 182 us; the launch traced here: 181 us
  Pallas kernels  74.5 us (41%)
  waiting for transfers between devices  54.8 us (30%)
  starting transfers between devices  37.3 us (20%)
  local copies, waits for them, and re-layouts  11.2 us (6%)
  other arithmetic  2.07 us (1%)
    ppermute x13, waiting for transfers between devices, shifted(): return lax.ppermute(value, 'seq', pairs)  43.8 us
    pallas_call x1, Pallas kernels, run_stack(): pl.pallas_call(functools.partial(stack_kernel, count), out_shape=jax.Shap...  36.9 us
    pallas_call x1, Pallas kernels, run_tokens(): pl.pallas_call(functools.partial(token_kernel, plan, bias_plan, len(parts...  22.6 us
    ppermute x3, starting transfers between devices, hop(): lax.ppermute(bias, 'samp', [(i, (i + 2 * by) % count) for i in range(coun...  13.3 us
    ppermute x13, starting transfers between devices, shifted(): return lax.ppermute(value, 'seq', pairs)  11.4 us
    pallas_call x1, Pallas kernels, run_atoms(): pl.pallas_call(atom_kernel, out_shape=(jax.ShapeDtypeStruct((samples, ato...  10.6 us
    unnamed x46, local copies, waits for them, and re-layouts  7.7 us
    ppermute x1, starting transfers between devices, per_device(): after = lax.ppermute(first, 'seq', to_previous)  6.54 us
  transfers between devices with their start and end apart: 20, of which 13 were waited for; matrix products, arithmetic and copies ran while one was open for 2% of the time, Pallas kernels for 22%

profile of v2, /device:TPU:6, one launch (start us, length us, event | category | flops | bytes accessed | tf_op | source)
XLA Modules:
  0.0 180.9 jit_solution(15727771563096375507)
XLA Ops:
  0.6 1.4 copy.24.range_ref
  2.0 2.3 %pack.1 = (bf16[304,128]{1,0:T(8,128)(2,1)}, bf16[96,128]{1,0:T(8,128)(2,1)}) custom-call(s32[12,2]{1,0:T(8,128)} %copy.24.range_ref, bf16[2,384,128]{2,1,0:T(8,128)(2,1)} %act_hbm.3, bf16[4,12,32,128]{3,2,1,0:T(8,128)(2,1)} %bias_hbm.3), custom_call_target="tpu_custom_call" | custom-call | tf_op jit(solution)/shard_map/pack/pallas_call | solution.py:78
  4.3 6.5 %collective-permute-start.1 = (bf16[304,128]{1,0:T(8,128)(2,1)}, bf16[304,128]{1,0:T(8,128)(2,1)S(1)}, u32[]{:S(2)}, u32[]{:S(2)}) collective-permute-start(bf16[304,128]{1,0:T(8,128)(2,1)} %get-tuple-element.11), channel_id=1, source_target_pairs={{1,0},{2,1},{3,2},{4,3},{5,4},{6,5},{7,6},{8,7},{9,8},{10,9},{11,1... | collective-permute-start | bytes 233480 | tf_op jit(solution)/shard_map/ppermute | solution.py:555
  10.9 1.9 %collective-permute-start = (bf16[96,128]{1,0:T(8,128)(2,1)}, bf16[96,128]{1,0:T(8,128)(2,1)S(1)}, u32[]{:S(2)}, u32[]{:S(2)}) collective-permute-start(bf16[96,128]{1,0:T(8,128)(2,1)} %get-tuple-element.10), channel_id=1, source_target_pairs={{0,1},{1,2},{2,3},{3,4},{4,5},{5,6},{6,7},{7,8},{8,9},{9,10},{10,1... | collective-permute-start | bytes 73736 | tf_op jit(solution)/shard_map/ppermute | solution.py:556
  12.8 1.2 reshape.20.token_ref.refs_13_
  14.0 1.3 reshape.21.token_gain_ref
  15.3 4.5 %collective-permute-done.before_ref = bf16[96,128]{1,0:T(8,128)(2,1)S(1)} collective-permute-done((bf16[96,128]{1,0:T(8,128)(2,1)}, bf16[96,128]{1,0:T(8,128)(2,1)S(1)}, u32[]{:S(2)}, u32[]{:S(2)}) %collective-permute-start) | collective-permute-done | bytes 24608 | tf_op jit(solution)/shard_map/ppermute | solution.py:556
  19.8 0.6 copy-done.18
  20.4 10.6 %atoms.1 = (bf16[2,384,128]{2,1,0:T(8,128)(2,1)}, bf16[2,48,768]{2,1,0:T(8,128)(2,1)}, bf16[2,48,768]{2,1,0:T(8,128)(2,1)}) custom-call(s32[12,2]{1,0:T(8,128)} %copy.24.range_ref, s32[48]{0:T(128)} %count_ref.1, bf16[96,128]{1,0:T(8,128)(2,1)} %copy-done.18, bf16[304,128]{1,0:T(8,128)(2,1)} %copy-done.17, f32[1,128]{1,0:T(1,128)} %bitcast.20, ...), custom_call_target="tpu_custom_call" | custom-call | flops 800000000 | bytes 4000000 | tf_op jit(solution)/shard_map/atoms/pallas_call | solution.py:227
  31.0 0.9 constant_dynamic-update-slice_fusion.9
  31.9 0.1 collective-permute-start.2
  32.0 1.0 slice_bitcast_fusion.2
  33.0 4.4 %collective-permute-done.2 = bf16[2,48,768]{2,1,0:T(8,128)(2,1)S(1)} collective-permute-done((bf16[2,48,768]{2,1,0:T(8,128)(2,1)}, bf16[2,48,768]{2,1,0:T(8,128)(2,1)S(1)}, u32[]{:S(2)}, u32[]{:S(2)}) %collective-permute-start.2) | collective-permute-done | bytes 147488 | tf_op jit(solution)/shard_map/ppermute | solution.py:454
  37.4 0.1 collective-permute-start.3
  37.5 3.2 %collective-permute-start.4 = (bf16[96,768]{1,0:T(8,128)(2,1)S(1)}, bf16[96,768]{1,0:T(8,128)(2,1)S(1)}, u32[]{:S(2)}, u32[]{:S(2)}) collective-permute-start(bf16[96,768]{1,0:T(8,128)(2,1)S(1)} %pad_maximum_fusion), channel_id=1, source_target_pairs={{0,6},{1,7},{2,0},{3,1},{4,2},{5,3},{6,4},{7,5},{8,14},{9,15},{10,... | collective-permute-start | bytes 442376 | tf_op jit(solution)/shard_map/ppermute | solution.py:454
  40.7 3.9 %collective-permute-done.3 = bf16[96,768]{1,0:T(8,128)(2,1)S(1)} collective-permute-done((bf16[96,768]{1,0:T(8,128)(2,1)S(1)}, bf16[96,768]{1,0:T(8,128)(2,1)S(1)}, u32[]{:S(2)}, u32[]{:S(2)}) %collective-permute-start.3) | collective-permute-done | bytes 147488 | tf_op jit(solution)/shard_map/ppermute | solution.py:454
  44.7 0.3 collective-permute-done.4
  45.0 2.4 %collective-permute-done.5 = bf16[96,768]{1,0:T(8,128)(2,1)S(1)} collective-permute-done((bf16[96,768]{1,0:T(8,128)(2,1)S(1)}, bf16[96,768]{1,0:T(8,128)(2,1)S(1)}, u32[]{:S(2)}, u32[]{:S(2)}) %collective-permute-start.5) | collective-permute-done | bytes 147488 | tf_op jit(solution)/shard_map/ppermute | solution.py:454
  47.4 0.1 collective-permute-start.6
  47.5 1.7 collective-permute-start.9
  49.2 0.4 collective-permute-start.10
  49.7 3.3 %collective-permute-start.15 = (bf16[2,48,1536]{2,1,0:T(8,128)(2,1)S(1)}, bf16[2,48,1536]{2,1,0:T(8,128)(2,1)S(1)}, u32[]{:S(2)}, u32[]{:S(2)}) collective-permute-start(bf16[2,48,1536]{2,1,0:T(8,128)(2,1)S(1)} %copy-done.12), channel_id=1, source_target_pairs={{0,64},{32,96},{64,128},{96,160},{128,192},{160,224},{192,0},{224,... | collective-permute-start | bytes 884744 | tf_op jit(solution)/shard_map/ppermute | solution.py:517
  53.0 2.1 %collective-permute-start.16 = (bf16[2,48,1536]{2,1,0:T(8,128)(2,1)S(1)}, bf16[2,48,1536]{2,1,0:T(8,128)(2,1)S(1)}, u32[]{:S(2)}, u32[]{:S(2)}) collective-permute-start(bf16[2,48,1536]{2,1,0:T(8,128)(2,1)S(1)} %copy-done.12), channel_id=1, source_target_pairs={{0,192},{32,224},{64,0},{96,32},{128,64},{160,96},{192,128},{224,1... | collective-permute-start | bytes 884744 | tf_op jit(solution)/shard_map/ppermute | solution.py:517
  55.1 6.4 %collective-permute-done.9 = bf16[96,768]{1,0:T(8,128)(2,1)S(1)} collective-permute-done((bf16[96,768]{1,0:T(8,128)(2,1)S(1)}, bf16[96,768]{1,0:T(8,128)(2,1)S(1)}, u32[]{:S(2)}, u32[]{:S(2)}) %collective-permute-start.9) | collective-permute-done | bytes 147488 | tf_op jit(solution)/shard_map/ppermute | solution.py:454
  61.5 7.9 %collective-permute-start.17 = (bf16[2,48,1536]{2,1,0:T(8,128)(2,1)S(1)}, bf16[2,48,1536]{2,1,0:T(8,128)(2,1)S(1)}, u32[]{:S(2)}, u32[]{:S(2)}) collective-permute-start(bf16[2,48,1536]{2,1,0:T(8,128)(2,1)S(1)} %copy-done.12), channel_id=1, source_target_pairs={{0,128},{32,160},{64,192},{96,224},{128,0},{160,32},{192,64},{224,... | collective-permute-start | bytes 884744 | tf_op jit(solution)/shard_map/ppermute | solution.py:517
  69.4 0.6 collective-permute-start.11
  70.0 6.0 %collective-permute-done.11 = bf16[96,768]{1,0:T(8,128)(2,1)S(1)} collective-permute-done((bf16[96,768]{1,0:T(8,128)(2,1)S(1)}, bf16[96,768]{1,0:T(8,128)(2,1)S(1)}, u32[]{:S(2)}, u32[]{:S(2)}) %collective-permute-start.11) | collective-permute-done | bytes 147488 | tf_op jit(solution)/shard_map/ppermute | solution.py:454
  76.0 0.3 collective-permute-start.12
  76.4 2.9 %collective-permute-done.17.refs_3_ = bf16[2,48,1536]{2,1,0:T(8,128)(2,1)S(1)} collective-permute-done((bf16[2,48,1536]{2,1,0:T(8,128)(2,1)S(1)}, bf16[2,48,1536]{2,1,0:T(8,128)(2,1)S(1)}, u32[]{:S(2)}, u32[]{:S(2)}) %collective-permute-start.17) | collective-permute-done | bytes 294944 | tf_op jit(solution)/shard_map/ppermute | solution.py:517
  79.2 0.7 copy-done.15
  80.0 0.8 copy-done.2
  80.8 36.9 %stack.1.refs_8_ = bf16[4,2,48,1536]{3,2,1,0:T(8,128)(2,1)} custom-call(bf16[2,48,1536]{2,1,0:T(8,128)(2,1)} %refs_0_.1, bf16[2,48,1536]{2,1,0:T(8,128)(2,1)} %copy-done.13, bf16[2,48,1536]{2,1,0:T(8,128)(2,1)} %copy-done.14, bf16[2,48,1536]{2,1,0:T(8,128)(2,1)} %copy-done.15, bf16[384,768]{1,0:T(8,128)(2,1)} %copy-done.2), custom_call_target="tpu_custom_call" | custom-call | tf_op jit(solution)/shard_map/stack/pallas_call | solution.py:499
  117.7 0.1 collective-permute-start.18
  117.8 1.1 collective-permute-start.13
  118.9 1.1 collective-permute-start.7
  120.0 2.6 %collective-permute-start.8 = (bf16[384,768]{1,0:T(8,128)(2,1)S(1)}, bf16[384,768]{1,0:T(8,128)(2,1)}, u32[]{:S(2)}, u32[]{:S(2)}) collective-permute-start(bf16[384,768]{1,0:T(8,128)(2,1)S(1)} %constant_dynamic-update-slice_fusion.refs_0_), channel_id=1, source_target_pairs={{0,16},{1,17},{2,18},{3,19},{4,20},{5,21},{6,22},{7,23},{8,24},{9,... | collective-permute-start | bytes 1769480 | tf_op jit(solution)/shard_map/ppermute | solution.py:454
  122.7 1.7 copy-done.5
  124.4 2.2 %queries.1.refs_10_ = bf16[2,768,768]{2,1,0:T(8,128)(2,1)S(1)} custom-call(bf16[2,48,768]{2,1,0:T(8,128)(2,1)S(1)} %copy-done.1, bf16[768,768]{1,0:T(8,128)(2,1)S(1)} %copy-done.6, bf16[768,1536]{1,0:T(8,128)(2,1)S(1)} %copy-done.5), custom_call_target="tpu_custom_call" | custom-call | flops 2000000000 | bytes 5000000 | tf_op jit(solution)/shard_map/queries/pallas_call | solution.py:281
  126.6 1.4 copy-done.9
  128.0 6.1 %collective-permute-done.13.refs_6_ = bf16[384,768]{1,0:T(8,128)(2,1)} collective-permute-done((bf16[384,768]{1,0:T(8,128)(2,1)S(1)}, bf16[384,768]{1,0:T(8,128)(2,1)}, u32[]{:S(2)}, u32[]{:S(2)}) %collective-permute-start.13) | collective-permute-done | bytes 589856 | tf_op jit(solution)/shard_map/ppermute | solution.py:454
  134.1 1.8 %collective-permute-done.14.refs_7_ = bf16[384,768]{1,0:T(8,128)(2,1)} collective-permute-done((bf16[384,768]{1,0:T(8,128)(2,1)S(1)}, bf16[384,768]{1,0:T(8,128)(2,1)}, u32[]{:S(2)}, u32[]{:S(2)}) %collective-permute-start.14) | collective-permute-done | bytes 589856 | tf_op jit(solution)/shard_map/ppermute | solution.py:454
  135.9 0.6 collective-permute-done.7.refs_2_
  136.5 11.9 %collective-permute-done.8.refs_3_ = bf16[384,768]{1,0:T(8,128)(2,1)} collective-permute-done((bf16[384,768]{1,0:T(8,128)(2,1)S(1)}, bf16[384,768]{1,0:T(8,128)(2,1)}, u32[]{:S(2)}, u32[]{:S(2)}) %collective-permute-start.8) | collective-permute-done | bytes 589856 | tf_op jit(solution)/shard_map/ppermute | solution.py:454
  148.5 22.6 %tokens.1 = (bf16[2,384,128]{2,1,0:T(8,128)(2,1)}, bf16[2,48,768]{2,1,0:T(8,128)(2,1)}, bf16[2,48,128]{2,1,0:T(8,128)(2,1)S(1)}) custom-call(bf16[384,768]{1,0:T(8,128)(2,1)S(1)} %constant_dynamic-update-slice_fusion.refs_0_, bf16[384,768]{1,0:T(8,128)(2,1)S(1)} %copy-done.3, bf16[384,768]{1,0:T(8,128)(2,1)} %collective-permute-done.7.refs_2_, ...), custom_call_target="tpu_custom_call" | custom-call | flops 10000000000 | bytes 20000000 | tf_op jit(solution)/shard_map/tokens/pallas_call | solution.py:420
  171.1 4.1 %collective-permute-start.19 = (bf16[2,128]{1,0:T(2,128)(2,1)S(1)}, bf16[2,128]{1,0:T(2,128)(2,1)S(1)}, u32[]{:S(2)}, u32[]{:S(2)}) collective-permute-start(bf16[2,128]{1,0:T(2,128)(2,1)S(1)} %bitcast.21), channel_id=1, source_target_pairs={{0,1},{1,2},{2,3},{3,4},{4,5},{5,6},{6,7},{7,8},{8,9},{9,10},{10,1... | collective-permute-start | bytes 1544 | tf_op jit(solution)/shard_map/ppermute | solution.py:592
  175.2 0.7 slice_compare_fusion
  175.9 3.7 %collective-permute-done.19 = bf16[2,128]{1,0:T(2,128)(2,1)S(1)} collective-permute-done((bf16[2,128]{1,0:T(2,128)(2,1)S(1)}, bf16[2,128]{1,0:T(2,128)(2,1)S(1)}, u32[]{:S(2)}, u32[]{:S(2)}) %collective-permute-start.19) | collective-permute-done | bytes 544 | tf_op jit(solution)/shard_map/ppermute | solution.py:592
  179.6 1.4 fusion
  (56 shorter events, 0.3 us)
Async XLA Ops:
  4.3 15.5 %collective-permute-start.1 = (bf16[304,128]{1,0:T(8,128)(2,1)}, bf16[304,128]{1,0:T(8,128)(2,1)S(1)}, u32[]{:S(2)}, u32[]{:S(2)}) collective-permute-start(bf16[304,128]{1,0:T(8,128)(2,1)} %get-tuple-element.11), channel_id=1, source_target_pairs={{1,0},{2,1},{3,2},{4,3},{5,4},{6,5},{7,6},{8,7},{9,8},{10,9},{11,1... | collective-permute-start | bytes 233480 | tf_op jit(solution)/shard_map/ppermute | solution.py:555
  10.9 8.9 %collective-permute-start = (bf16[96,128]{1,0:T(8,128)(2,1)}, bf16[96,128]{1,0:T(8,128)(2,1)S(1)}, u32[]{:S(2)}, u32[]{:S(2)}) collective-permute-start(bf16[96,128]{1,0:T(8,128)(2,1)} %get-tuple-element.10), channel_id=1, source_target_pairs={{0,1},{1,2},{2,3},{3,4},{4,5},{5,6},{6,7},{7,8},{8,9},{9,10},{10,1... | collective-permute-start | bytes 73736 | tf_op jit(solution)/shard_map/ppermute | solution.py:556
  19.8 0.6 copy-start.18
  19.8 0.6 copy-start.17
  20.4 29.2 %copy-start.12 = (bf16[2,48,1536]{2,1,0:T(8,128)(2,1)S(1)}, bf16[2,48,1536]{2,1,0:T(8,128)(2,1)}, u32[]{:S(2)}) copy-start(bf16[2,48,1536]{2,1,0:T(8,128)(2,1)} %refs_0_.1) | copy-start | bytes 884740
  31.9 5.4 %collective-permute-start.2 = (bf16[2,48,768]{2,1,0:T(8,128)(2,1)}, bf16[2,48,768]{2,1,0:T(8,128)(2,1)S(1)}, u32[]{:S(2)}, u32[]{:S(2)}) collective-permute-start(bf16[2,48,768]{2,1,0:T(8,128)(2,1)} %get-tuple-element.12.norm_ref), channel_id=1, source_target_pairs={{0,1},{1,0},{2,3},{3,2},{4,5},{5,4},{6,7},{7,6},{8,9},{9,8},{10,11... | collective-permute-start | bytes 442376 | tf_op jit(solution)/shard_map/ppermute | solution.py:454
  37.4 7.3 %collective-permute-start.3 = (bf16[96,768]{1,0:T(8,128)(2,1)S(1)}, bf16[96,768]{1,0:T(8,128)(2,1)S(1)}, u32[]{:S(2)}, u32[]{:S(2)}) collective-permute-start(bf16[96,768]{1,0:T(8,128)(2,1)S(1)} %pad_maximum_fusion), channel_id=1, source_target_pairs={{0,2},{1,3},{2,4},{3,5},{4,6},{5,7},{6,0},{7,1},{8,10},{9,11},{10,... | collective-permute-start | bytes 442376 | tf_op jit(solution)/shard_map/ppermute | solution.py:454
  37.5 7.5 %collective-permute-start.4 = (bf16[96,768]{1,0:T(8,128)(2,1)S(1)}, bf16[96,768]{1,0:T(8,128)(2,1)S(1)}, u32[]{:S(2)}, u32[]{:S(2)}) collective-permute-start(bf16[96,768]{1,0:T(8,128)(2,1)S(1)} %pad_maximum_fusion), channel_id=1, source_target_pairs={{0,6},{1,7},{2,0},{3,1},{4,2},{5,3},{6,4},{7,5},{8,14},{9,15},{10,... | collective-permute-start | bytes 442376 | tf_op jit(solution)/shard_map/ppermute | solution.py:454
  40.7 6.6 %collective-permute-start.5 = (bf16[96,768]{1,0:T(8,128)(2,1)S(1)}, bf16[96,768]{1,0:T(8,128)(2,1)S(1)}, u32[]{:S(2)}, u32[]{:S(2)}) collective-permute-start(bf16[96,768]{1,0:T(8,128)(2,1)S(1)} %pad_maximum_fusion), channel_id=1, source_target_pairs={{0,4},{1,5},{2,6},{3,7},{4,0},{5,1},{6,2},{7,3},{8,12},{9,13},{10,... | collective-permute-start | bytes 442376 | tf_op jit(solution)/shard_map/ppermute | solution.py:454
  44.7 77.9 %copy-start.16 = (f32[768]{0:T(1024)S(1)}, f32[768]{0:T(1024)}, u32[]{:S(2)}) copy-start(f32[768]{0:T(1024)} %param.34) | copy-start | bytes 9220
  44.7 77.9 %copy-start.1 = (bf16[2,48,768]{2,1,0:T(8,128)(2,1)S(1)}, bf16[2,48,768]{2,1,0:T(8,128)(2,1)}, u32[]{:S(2)}) copy-start(bf16[2,48,768]{2,1,0:T(8,128)(2,1)} %get-tuple-element.12.norm_ref) | copy-start | bytes 442372
  44.7 77.9 %copy-start.6 = (bf16[768,768]{1,0:T(8,128)(2,1)S(1)}, bf16[768,768]{1,0:T(8,128)(2,1)}, u32[]{:S(2)}) copy-start(bf16[768,768]{1,0:T(8,128)(2,1)} %query_hbm.3) | copy-start | bytes 3538948
  47.4 32.6 %collective-permute-start.6 = (bf16[384,768]{1,0:T(8,128)(2,1)S(1)}, bf16[384,768]{1,0:T(8,128)(2,1)S(1)}, u32[]{:S(2)}, u32[]{:S(2)}) collective-permute-start(bf16[384,768]{1,0:T(8,128)(2,1)S(1)} %constant_dynamic-update-slice_fusion.refs_0_), channel_id=1, source_target_pairs={{0,8},{1,9},{2,10},{3,11},{4,12},{5,13},{6,14},{7,15},{8,16},{9,17... | collective-permute-start | bytes 1769480 | tf_op jit(solution)/shard_map/ppermute | solution.py:454
  47.5 14.0 %collective-permute-start.9 = (bf16[96,768]{1,0:T(8,128)(2,1)S(1)}, bf16[96,768]{1,0:T(8,128)(2,1)S(1)}, u32[]{:S(2)}, u32[]{:S(2)}) collective-permute-start(bf16[96,768]{1,0:T(8,128)(2,1)S(1)} %pad_maximum_fusion.1), channel_id=1, source_target_pairs={{0,8},{1,9},{2,10},{3,11},{4,12},{5,13},{6,14},{7,15},{8,16},{9,17... | collective-permute-start | bytes 442376 | tf_op jit(solution)/shard_map/ppermute | solution.py:454
  49.2 20.1 %collective-permute-start.10 = (bf16[96,768]{1,0:T(8,128)(2,1)S(1)}, bf16[96,768]{1,0:T(8,128)(2,1)S(1)}, u32[]{:S(2)}, u32[]{:S(2)}) collective-permute-start(bf16[96,768]{1,0:T(8,128)(2,1)S(1)} %pad_maximum_fusion.1), channel_id=1, source_target_pairs={{0,24},{1,25},{2,26},{3,27},{4,28},{5,29},{6,30},{7,31},{8,0},{9,1... | collective-permute-start | bytes 442376 | tf_op jit(solution)/shard_map/ppermute | solution.py:454
  49.7 26.6 %collective-permute-start.15 = (bf16[2,48,1536]{2,1,0:T(8,128)(2,1)S(1)}, bf16[2,48,1536]{2,1,0:T(8,128)(2,1)S(1)}, u32[]{:S(2)}, u32[]{:S(2)}) collective-permute-start(bf16[2,48,1536]{2,1,0:T(8,128)(2,1)S(1)} %copy-done.12), channel_id=1, source_target_pairs={{0,64},{32,96},{64,128},{96,160},{128,192},{160,224},{192,0},{224,... | collective-permute-start | bytes 884744 | tf_op jit(solution)/shard_map/ppermute | solution.py:517
  53.0 23.4 %collective-permute-start.16 = (bf16[2,48,1536]{2,1,0:T(8,128)(2,1)S(1)}, bf16[2,48,1536]{2,1,0:T(8,128)(2,1)S(1)}, u32[]{:S(2)}, u32[]{:S(2)}) collective-permute-start(bf16[2,48,1536]{2,1,0:T(8,128)(2,1)S(1)} %copy-done.12), channel_id=1, source_target_pairs={{0,192},{32,224},{64,0},{96,32},{128,64},{160,96},{192,128},{224,1... | collective-permute-start | bytes 884744 | tf_op jit(solution)/shard_map/ppermute | solution.py:517
  61.5 17.7 %collective-permute-start.17 = (bf16[2,48,1536]{2,1,0:T(8,128)(2,1)S(1)}, bf16[2,48,1536]{2,1,0:T(8,128)(2,1)S(1)}, u32[]{:S(2)}, u32[]{:S(2)}) collective-permute-start(bf16[2,48,1536]{2,1,0:T(8,128)(2,1)S(1)} %copy-done.12), channel_id=1, source_target_pairs={{0,128},{32,160},{64,192},{96,224},{128,0},{160,32},{192,64},{224,... | collective-permute-start | bytes 884744 | tf_op jit(solution)/shard_map/ppermute | solution.py:517
  69.4 6.6 %collective-permute-start.11 = (bf16[96,768]{1,0:T(8,128)(2,1)S(1)}, bf16[96,768]{1,0:T(8,128)(2,1)S(1)}, u32[]{:S(2)}, u32[]{:S(2)}) collective-permute-start(bf16[96,768]{1,0:T(8,128)(2,1)S(1)} %pad_maximum_fusion.1), channel_id=1, source_target_pairs={{0,16},{1,17},{2,18},{3,19},{4,20},{5,21},{6,22},{7,23},{8,24},{9,... | collective-permute-start | bytes 442376 | tf_op jit(solution)/shard_map/ppermute | solution.py:454
  76.0 44.0 %collective-permute-start.12 = (bf16[384,768]{1,0:T(8,128)(2,1)S(1)}, bf16[384,768]{1,0:T(8,128)(2,1)}, u32[]{:S(2)}, u32[]{:S(2)}) collective-permute-start(bf16[384,768]{1,0:T(8,128)(2,1)S(1)} %constant_dynamic-update-slice_fusion.5.refs_4_), channel_id=1, source_target_pairs={{0,2},{1,3},{2,4},{3,5},{4,6},{5,7},{6,0},{7,1},{8,10},{9,11},{10,... | collective-permute-start | bytes 1769480 | tf_op jit(solution)/shard_map/ppermute | solution.py:454
  76.3 3.6 %copy-start.13 = (bf16[2,48,1536]{2,1,0:T(8,128)(2,1)}, bf16[2,48,1536]{2,1,0:T(8,128)(2,1)S(1)}, u32[]{:S(2)}) copy-start(bf16[2,48,1536]{2,1,0:T(8,128)(2,1)S(1)} %collective-permute-done.15.refs_1_) | copy-start | bytes 884740
  76.3 2.9 %copy-start.14 = (bf16[2,48,1536]{2,1,0:T(8,128)(2,1)}, bf16[2,48,1536]{2,1,0:T(8,128)(2,1)S(1)}, u32[]{:S(2)}) copy-start(bf16[2,48,1536]{2,1,0:T(8,128)(2,1)S(1)} %collective-permute-done.16.refs_2_) | copy-start | bytes 884740
  79.2 0.7 copy-start.15
  80.0 0.8 copy-start.2
  117.7 30.8 %collective-permute-start.18 = (bf16[4,2,48,1536]{3,2,1,0:T(8,128)(2,1)}, bf16[4,2,48,1536]{3,2,1,0:T(8,128)(2,1)}, u32[]{:S(2)}, u32[]{:S(2)}) collective-permute-start(bf16[4,2,48,1536]{3,2,1,0:T(8,128)(2,1)} %stack.1.refs_8_), channel_id=1, source_target_pairs={{0,32},{32,0},{64,96},{96,64},{128,160},{160,128},{192,224},{224,1... | collective-permute-start | bytes 3538952 | tf_op jit(solution)/shard_map/ppermute | solution.py:523
  117.8 16.3 %collective-permute-start.13 = (bf16[384,768]{1,0:T(8,128)(2,1)S(1)}, bf16[384,768]{1,0:T(8,128)(2,1)}, u32[]{:S(2)}, u32[]{:S(2)}) collective-permute-start(bf16[384,768]{1,0:T(8,128)(2,1)S(1)} %constant_dynamic-update-slice_fusion.5.refs_4_), channel_id=1, source_target_pairs={{0,6},{1,7},{2,0},{3,1},{4,2},{5,3},{6,4},{7,5},{8,14},{9,15},{10,... | collective-permute-start | bytes 1769480 | tf_op jit(solution)/shard_map/ppermute | solution.py:454
  118.9 17.0 %collective-permute-start.14 = (bf16[384,768]{1,0:T(8,128)(2,1)S(1)}, bf16[384,768]{1,0:T(8,128)(2,1)}, u32[]{:S(2)}, u32[]{:S(2)}) collective-permute-start(bf16[384,768]{1,0:T(8,128)(2,1)S(1)} %constant_dynamic-update-slice_fusion.5.refs_4_), channel_id=1, source_target_pairs={{0,4},{1,5},{2,6},{3,7},{4,0},{5,1},{6,2},{7,3},{8,12},{9,13},{10,... | collective-permute-start | bytes 1769480 | tf_op jit(solution)/shard_map/ppermute | solution.py:454
  118.9 17.6 %collective-permute-start.7 = (bf16[384,768]{1,0:T(8,128)(2,1)S(1)}, bf16[384,768]{1,0:T(8,128)(2,1)}, u32[]{:S(2)}, u32[]{:S(2)}) collective-permute-start(bf16[384,768]{1,0:T(8,128)(2,1)S(1)} %constant_dynamic-update-slice_fusion.refs_0_), channel_id=1, source_target_pairs={{0,24},{1,25},{2,26},{3,27},{4,28},{5,29},{6,30},{7,31},{8,0},{9,1... | collective-permute-start | bytes 1769480 | tf_op jit(solution)/shard_map/ppermute | solution.py:454
  120.0 28.4 %collective-permute-start.8 = (bf16[384,768]{1,0:T(8,128)(2,1)S(1)}, bf16[384,768]{1,0:T(8,128)(2,1)}, u32[]{:S(2)}, u32[]{:S(2)}) collective-permute-start(bf16[384,768]{1,0:T(8,128)(2,1)S(1)} %constant_dynamic-update-slice_fusion.refs_0_), channel_id=1, source_target_pairs={{0,16},{1,17},{2,18},{3,19},{4,20},{5,21},{6,22},{7,23},{8,24},{9,... | collective-permute-start | bytes 1769480 | tf_op jit(solution)/shard_map/ppermute | solution.py:454
  122.6 1.7 copy-start.5
  124.3 24.1 %copy-start = (bf16[4,2,48,1536]{3,2,1,0:T(8,128)(2,1)S(1)}, bf16[4,2,48,1536]{3,2,1,0:T(8,128)(2,1)}, u32[]{:S(2)}) copy-start(bf16[4,2,48,1536]{3,2,1,0:T(8,128)(2,1)} %stack.1.refs_8_) | copy-start | bytes 3538948
  124.3 24.1 %copy-start.3 = (bf16[384,768]{1,0:T(8,128)(2,1)S(1)}, bf16[384,768]{1,0:T(8,128)(2,1)}, u32[]{:S(2)}) copy-start(bf16[384,768]{1,0:T(8,128)(2,1)} %copy-done.2) | copy-start | bytes 1769476
  124.3 24.1 %copy-start.4 = (s32[1,384]{1,0:T(1,128)S(1)}, s32[1,384]{1,0:T(1,128)}, u32[]{:S(2)}) copy-start(s32[1,384]{1,0:T(1,128)} %reshape.20.token_ref.refs_13_) | copy-start | bytes 4612
  124.3 24.1 %copy-start.7 = (bf16[768,768]{1,0:T(8,128)(2,1)S(1)}, bf16[768,768]{1,0:T(8,128)(2,1)}, u32[]{:S(2)}) copy-start(bf16[768,768]{1,0:T(8,128)(2,1)} %refs_16_.1) | copy-start | bytes 3538948
  124.3 24.2 %copy-start.8 = (bf16[768,128]{1,0:T(8,128)(2,1)S(1)}, bf16[768,128]{1,0:T(8,128)(2,1)}, u32[]{:S(2)}) copy-start(bf16[768,128]{1,0:T(8,128)(2,1)} %refs_19_.1) | copy-start | bytes 589828
  124.3 24.2 %copy-start.10 = (bf16[2,384,128]{2,1,0:T(8,128)(2,1)S(1)}, bf16[2,384,128]{2,1,0:T(8,128)(2,1)}, u32[]{:S(2)}) copy-start(bf16[2,384,128]{2,1,0:T(8,128)(2,1)} %get-tuple-element.14.refs_12_) | copy-start | bytes 589828
  124.4 24.1 %copy-start.11 = (bf16[2,48,768]{2,1,0:T(8,128)(2,1)S(1)}, bf16[2,48,768]{2,1,0:T(8,128)(2,1)}, u32[]{:S(2)}) copy-start(bf16[2,48,768]{2,1,0:T(8,128)(2,1)} %get-tuple-element.13.refs_11_) | copy-start | bytes 442372
  126.6 1.4 copy-start.9
  171.1 8.4 %collective-permute-start.19 = (bf16[2,128]{1,0:T(2,128)(2,1)S(1)}, bf16[2,128]{1,0:T(2,128)(2,1)S(1)}, u32[]{:S(2)}, u32[]{:S(2)}) collective-permute-start(bf16[2,128]{1,0:T(2,128)(2,1)S(1)} %bitcast.21), channel_id=1, source_target_pairs={{0,1},{1,2},{2,3},{3,4},{4,5},{5,6},{6,7},{7,8},{8,9},{9,10},{10,1... | collective-permute-start | bytes 1544 | tf_op jit(solution)/shard_map/ppermute | solution.py:592

commit v3 on v2

--- a/solution.py
+++ b/solution.py
@@ -23,6 +23,11 @@
 NEGATIVE = -1e30
 F32 = jnp.float32
 BF16 = jnp.bfloat16
+
+
+def cost(flops):
+    return pl.CostEstimate(flops=flops, bytes_accessed=1000, transcendentals=0)
+
 
 NT = (((1,), (1,)), ((), ()))
 TN = (((0,), (0,)), ((), ()))
@@ -67,7 +72,7 @@
         started.append(copy)
     start = lax.axis_index("seq") * atoms - EDGE
     row = lax.broadcasted_iota(jnp.int32, (META, WK), 0)
-    meta = jnp.where(row == 0, range_ref[0, 0] - start, range_ref[0, 1] - start)
+    meta = jnp.where(row == 0, range_ref[0, 0] - start, range_ref[1, 0] - start)
     first_ref[meta_at : meta_at + META, :] = meta.astype(F32).astype(BF16)
     for copy in started:
         copy.wait()
@@ -183,7 +188,7 @@
             if w < windows:
                 bias = bias_ref[:, w].reshape(AH * WQ, WK)
                 start = (device * windows + w) * WQ - EDGE
-                valid = (index >= range_ref[w, 0] - start) & (index < range_ref[w, 1] - start)
+                valid = (index >= range_ref[0, w] - start) & (index < range_ref[1, w] - start)
             else:
                 bias = after_ref[bias_at : bias_at + AH * WQ, :]
                 valid = valid_after
@@ -239,18 +244,9 @@
             pltpu.SemaphoreType.DMA((len(arrays),)),
         ],
         compiler_params=pltpu.CompilerParams(vmem_limit_bytes=60 * 2**20),
-        cost_estimate=pl.CostEstimate(
-            flops=800_000_000, bytes_accessed=4_000_000, transcendentals=500_000
-        ),
+        cost_estimate=cost(5_000_000_000),
         name="atoms",
     )(key_range, counts, before, after, gain, token, token_gain, *arrays)
-
-
-def block_rows(dx, dy, dz, rows):
-    device = lax.axis_index("seq")
-    x, y, z = device // 8, (device // 2) % 4, device % 2
-    source = ((x + dx) % 4) * 8 + ((y + dy) % 4) * 2 + (z + dz) % 2
-    return source * rows
 
 
 def query_kernel(norm_ref, query_hbm, keyval_hbm, absorbed_ref, query_ref, key_ref, sems):
@@ -289,69 +285,138 @@
             pltpu.SemaphoreType.DMA((2,)),
         ],
         compiler_params=pltpu.CompilerParams(vmem_limit_bytes=30 * 2**20),
-        cost_estimate=pl.CostEstimate(
-            flops=2_000_000_000, bytes_accessed=5_000_000, transcendentals=0
-        ),
+        cost_estimate=cost(2_000_000_000),
         name="queries",
     )(norm, token_query, token_keyval)
 
 
-def token_kernel(plan, bias_plan, pieces, *refs):
-    parts = refs[:pieces]
-    (
-        bias_near_hbm,
-        bias_far_hbm,
-        absorbed_ref,
-        tokact_ref,
-        mid_ref,
-        token_ref,
-        gain_ref,
-        keyval_hbm,
-        output_hbm,
-        gate_hbm,
-        down_hbm,
-        back_hbm,
-        atom_out_ref,
-        token_out_ref,
-        back_rows_ref,
-        all_ref,
-        bias_ref,
-        value_ref,
-        output_ref,
-        gate_ref,
-        down_ref,
-        back_ref,
-        att_ref,
-        weight_sems,
-        part_sems,
-        bias_sems,
-    ) = refs[pieces:]
+def reorder_kernel(bias_ref, after_hbm, out_ref):
+    heads, tokens, keys = bias_ref.shape
+    line = keys // 4
+    part = line // 4
+    for h in range(heads):
+        rows = bias_ref[h]
+        blocks = [
+            rows[:, line * x + part * y : line * x + part * (y + 1)] for y in range(4) for x in range(4)
+        ]
+        out_ref[h] = jnp.concatenate(blocks, axis=1)
+
+
+def run_reorder(bias, after):
+    return pl.pallas_call(
+        reorder_kernel,
+        out_shape=jax.ShapeDtypeStruct(bias.shape, BF16),
+        in_specs=[vmem(), anywhere()],
+        out_specs=vmem(),
+        compiler_params=pltpu.CompilerParams(vmem_limit_bytes=24 * 2**20),
+        cost_estimate=cost(2_000_000_000),
+        name="reorder",
+    )(bias, after)
+
+
+def place(device, sample):
+    x, y = device // 8, (device // 2) % 4
+    return x if sample % 2 == 0 else y
+
+
+def piece_scores(q, piece, bias_ref, group, chunk):
+    size = piece.shape[0]
+    start = pl.multiple_of(chunk * size, 128)
+    bias = bias_ref[GROUP * group : GROUP * (group + 1), :, pl.ds(start, size)]
+    return dot_nt(q, piece) + bias.reshape(q.shape[0], size).astype(F32)
+
+
+def early_kernel(
+    absorbed_ref,
+    bias0_ref,
+    bias1_ref,
+    own0_ref,
+    low0_ref,
+    high0_ref,
+    own1_ref,
+    low1_ref,
+    high1_ref,
+    mixed_ref,
+    best_ref,
+    total_ref,
+):
+    device = lax.axis_index("seq")
+    samples = absorbed_ref.shape[0]
+    rows_of = absorbed_ref.shape[1] * GROUP // HEADS
+    pieces = ((own0_ref, low0_ref, high0_ref), (own1_ref, low1_ref, high1_ref))
+    for s in range(samples):
+        here = place(device, s)
+        for g in range(HEADS // GROUP):
+            rows = slice(rows_of * g, rows_of * (g + 1))
+            q = absorbed_ref[s, rows]
+            scores = [
+                piece_scores(q, piece[...], (bias0_ref, bias1_ref)[s], g, (here + step) % 4)
+                for piece, step in zip(pieces[s], (0, 3, 1))
+            ]
+            best = functools.reduce(
+                jnp.maximum, [jnp.max(c, axis=-1, keepdims=True) for c in scores]
+            )
+            total, mixed = 0.0, 0.0
+            for piece, c in zip(pieces[s], scores):
+                exponent = jnp.exp(c - best)
+                total = total + jnp.sum(exponent, axis=-1, keepdims=True)
+                mixed = mixed + dot(exponent.astype(BF16), piece[...])
+            mixed_ref[s, rows] = mixed
+            best_ref[s, rows] = jnp.broadcast_to(best, (rows_of, 128))
+            total_ref[s, rows] = jnp.broadcast_to(total, (rows_of, 128))
+
+
+def run_early(absorbed, bias0, bias1, pieces):
+    samples, rows, width = absorbed.shape
+    return pl.pallas_call(
+        early_kernel,
+        out_shape=(
+            jax.ShapeDtypeStruct((samples, rows, width), F32),
+            jax.ShapeDtypeStruct((samples, rows, 128), F32),
+            jax.ShapeDtypeStruct((samples, rows, 128), F32),
+        ),
+        in_specs=[vmem()] * (3 + len(pieces)),
+        out_specs=(vmem(),) * 3,
+        compiler_params=pltpu.CompilerParams(vmem_limit_bytes=26 * 2**20),
+        cost_estimate=cost(8_000_000_000),
+        name="early",
+    )(absorbed, bias0, bias1, *pieces)
+
+
+def late_kernel(
+    absorbed_ref,
+    bias0_ref,
+    bias1_ref,
+    far0_low_ref,
+    far0_high_ref,
+    far1_low_ref,
+    far1_high_ref,
+    mixed_ref,
+    best_ref,
+    total_ref,
+    tokact_ref,
+    mid_ref,
+    token_ref,
+    gain_ref,
+    keyval_hbm,
+    output_hbm,
+    gate_hbm,
+    down_hbm,
+    back_hbm,
+    atom_out_ref,
+    token_out_ref,
+    back_rows_ref,
+    value_ref,
+    output_ref,
+    gate_ref,
+    down_ref,
+    back_ref,
+    att_ref,
+    weight_sems,
+):
     samples, tokens, width = tokact_ref.shape
     head_size = width // HEADS
     device = lax.axis_index("seq")
-    mine = lax.axis_index("samp")
-
-    part_copies = []
-    for i, (part, at, sample, offset) in enumerate(plan):
-        target = pl.multiple_of(block_rows(*offset, tokens), 16)
-        copy = pltpu.make_async_copy(
-            parts[part].at[at : at + tokens],
-            all_ref.at[sample, pl.ds(target, tokens)],
-            part_sems.at[i],
-        )
-        copy.start()
-        part_copies.append(copy)
-    bias_copies = []
-    for i, (near, at, hop) in enumerate(bias_plan):
-        source = (mine // 2 + hop) % 4 * 2 + (mine % 2 if near else 1 - mine % 2)
-        heads = bias_ref.shape[0] // len(bias_plan)
-        copy = pltpu.make_async_copy(
-            (bias_near_hbm if near else bias_far_hbm).at[at],
-            bias_ref.at[pl.ds(source * heads, heads)],
-            bias_sems.at[i],
-        )
-        copy.start()
-        bias_copies.append(copy)
     weight_copies = []
     for i, (source, target) in enumerate(
         (
@@ -369,19 +434,22 @@
     lanes = GROUP * head_size
     head_of = lane_group(tokens, lanes, head_size)
     masks32 = [(head_of == h).astype(F32) for h in range(GROUP)]
-    for copy in part_copies:
-        copy.wait()
-    for copy in bias_copies:
-        copy.wait()
+    halves = ((far0_low_ref, far0_high_ref), (far1_low_ref, far1_high_ref))
     for s in range(samples):
+        far = (place(device, s) + 2) % 4
+        piece = jnp.concatenate([halves[s][0][...], halves[s][1][...]], axis=0)
         for g in range(HEADS // GROUP):
             columns = slice(lanes * g, lanes * (g + 1))
-            scores = dot_nt(absorbed_ref[s, columns], all_ref[s])
-            bias = bias_ref[GROUP * g : GROUP * (g + 1)].reshape(GROUP * tokens, -1)
-            scores = scores + bias.astype(F32)
-            exponent = jnp.exp(scores - jnp.max(scores, axis=-1, keepdims=True))
-            total = jnp.sum(exponent, axis=-1, keepdims=True)
-            mixed = dot(exponent.astype(BF16), all_ref[s]) / total
+            scores = piece_scores(absorbed_ref[s, columns], piece, (bias0_ref, bias1_ref)[s], g, far)
+            before = best_ref[s, columns][:, :1]
+            best = jnp.maximum(before, jnp.max(scores, axis=-1, keepdims=True))
+            exponent = jnp.exp(scores - best)
+            shrink = jnp.exp(before - best)
+            total = total_ref[s, columns][:, :1] * shrink + jnp.sum(
+                exponent, axis=-1, keepdims=True
+            )
+            mixed = mixed_ref[s, columns] * shrink + dot(exponent.astype(BF16), piece)
+            mixed = mixed / total
             if s == 0 and g == 0:
                 weight_copies[0].wait()
             valued = dot(mixed.astype(BF16), value_ref[:, columns])
@@ -414,113 +482,78 @@
         atom_out_ref[s] = (mid_ref[s].astype(F32) + gathered).astype(BF16)
 
 
-def run_tokens(plan, parts, bias_plan, bias_near, bias_far, absorbed, tokact, mid, token, gain, weights):
+def run_late(absorbed, bias0, bias1, far, early, tokact, mid, token, gain, weights):
     samples, tokens, width = tokact.shape
-    keys = bias_near.shape[-1]
     return pl.pallas_call(
-        functools.partial(token_kernel, plan, bias_plan, len(parts)),
+        late_kernel,
         out_shape=(
             jax.ShapeDtypeStruct(mid.shape, BF16),
             jax.ShapeDtypeStruct(tokact.shape, BF16),
             jax.ShapeDtypeStruct((samples, tokens, mid.shape[2]), BF16),
         ),
-        in_specs=[anywhere()] * (len(parts) + 2) + [vmem()] * 5 + [anywhere()] * 5,
+        in_specs=[vmem()] * 14 + [anywhere()] * 5,
         out_specs=(vmem(),) * 3,
-        scratch_shapes=[
-            pltpu.VMEM((samples, keys, width), BF16),
-            pltpu.VMEM((HEADS, tokens, keys), BF16),
-            pltpu.VMEM((width, width), BF16),
-        ]
+        scratch_shapes=[pltpu.VMEM((width, width), BF16)]
         + [pltpu.VMEM(w.shape, w.dtype) for w in weights[1:]]
         + [
             pltpu.VMEM((samples * tokens, width), BF16),
             pltpu.SemaphoreType.DMA((len(weights),)),
-            pltpu.SemaphoreType.DMA((len(plan),)),
-            pltpu.SemaphoreType.DMA((len(bias_plan),)),
         ],
-        compiler_params=pltpu.CompilerParams(vmem_limit_bytes=44 * 2**20),
-        cost_estimate=pl.CostEstimate(
-            flops=10_000_000_000, bytes_accessed=20_000_000, transcendentals=3_000_000
-        ),
-        name="tokens",
-    )(*parts, bias_near, bias_far, absorbed, tokact, mid, token, gain, *weights)
-
-
-def shifted(value, dx, dy, dz=0):
+        compiler_params=pltpu.CompilerParams(vmem_limit_bytes=28 * 2**20),
+        cost_estimate=cost(5_000_000_000),
+        name="late",
+    )(absorbed, bias0, bias1, *far, *early, tokact, mid, token, gain, *weights)
+
+
+def shifted(value, dx, dy):
     pairs = []
     for t in range(32):
         x, y, z = t // 8, (t // 2) % 4, t % 2
-        pairs.append((t, ((x + dx) % 4) * 8 + ((y + dy) % 4) * 2 + (z + dz) % 2))
+        pairs.append((t, ((x + dx) % 4) * 8 + ((y + dy) % 4) * 2 + z))
     return lax.ppermute(value, "seq", pairs)
 
 
-def line_of(value, dx, dy):
-    return [
-        value,
-        shifted(value, dx, dy),
-        shifted(value, -dx, -dy),
-        shifted(value, 2 * dx, 2 * dy),
-    ]
+def exchanged(value, bit):
+    return lax.ppermute(value, "seq", [(t, t ^ (1 << bit)) for t in range(32)])
+
+
+def join_kernel(bits, *refs):
+    count = len(bits)
+    device = lax.axis_index("seq")
+    for i, bit in enumerate(bits):
+        own, other, joined = refs[i], refs[count + i], refs[2 * count + i]
+        rows = joined.shape[0] // 2
+        where = (device // (1 << bit)) % 2
+        joined[pl.ds(pl.multiple_of(where * rows, 16), rows)] = own[...].reshape(rows, -1)
+        joined[pl.ds(pl.multiple_of((1 - where) * rows, 16), rows)] = other[...].reshape(rows, -1)
+
+
+def joined(own, other, bits):
+    rows, width = own[0].shape
+    shape = jax.ShapeDtypeStruct((2 * rows, width), BF16)
+    return pl.pallas_call(
+        functools.partial(join_kernel, bits),
+        out_shape=(shape,) * len(bits),
+        in_specs=[vmem()] * (2 * len(bits)),
+        out_specs=(vmem(),) * len(bits),
+        compiler_params=pltpu.CompilerParams(vmem_limit_bytes=16 * 2**20),
+        cost_estimate=cost(1_000_000),
+        name="join",
+    )(*own, *other)
 
 
 def spread(norm):
-    samples, tokens, _ = norm.shape
-    other = shifted(norm, 0, 0, 1)
-    parts, plan = [], []
-    for s in range(samples):
-        dx, dy = (0, 1) if s % 2 == 0 else (1, 0)
-        first = jnp.concatenate([norm[s], other[s]], axis=0)
-        line = line_of(first, dx, dy)
-        plane = line_of(jnp.concatenate(line, axis=0), dy, dx)
-        steps = (0, -1, 1, 2)
-        base = len(parts)
-        parts += plane
-        for piece, far in enumerate(steps):
-            for k in range(2 * len(steps)):
-                near = steps[k // 2]
-                offset = (near * dx + far * dy, near * dy + far * dx, k % 2)
-                plan.append((base + piece, k * tokens, s, offset))
-    return parts, plan, parts[1]
-
-
-def stack_kernel(count, *refs):
-    pieces, stacked, sems = refs[:count], refs[-2], refs[-1]
-    copies = []
-    for i, piece in enumerate(pieces):
-        copy = pltpu.make_async_copy(piece, stacked.at[i], sems.at[i])
-        copy.start()
-        copies.append(copy)
-    for copy in copies:
-        copy.wait()
-
-
-def run_stack(pieces, after):
-    count = len(pieces)
-    return pl.pallas_call(
-        functools.partial(stack_kernel, count),
-        out_shape=jax.ShapeDtypeStruct((count,) + pieces[0].shape, pieces[0].dtype),
-        in_specs=[anywhere()] * (count + 1),
-        out_specs=anywhere(),
-        scratch_shapes=[pltpu.SemaphoreType.DMA((count,))],
-        compiler_params=pltpu.CompilerParams(vmem_limit_bytes=60 * 2**20),
-        name="stack",
-    )(*pieces, after)
-
-
-BIAS_STEPS = (0, -1, 1, 2)
-
-
-def column_of(bias):
-    count = lax.axis_size("samp")
-
-    def hop(by):
-        return lax.ppermute(bias, "samp", [(i, (i + 2 * by) % count) for i in range(count)])
-
-    return [bias, hop(1), hop(-1), hop(2)]
-
-
-def other_core(value):
-    return lax.ppermute(value, "samp", [(i, i ^ 1) for i in range(lax.axis_size("samp"))])
+    other = exchanged(norm, 0)
+    lines = joined([norm[0], norm[1]], [other[0], other[1]], (0, 0))
+    for bits in ((1, 3), (2, 4)):
+        lines = joined(lines, [exchanged(v, b) for v, b in zip(lines, bits)], bits)
+    near, far = [], []
+    for value, dx, dy in ((lines[0], 1, 0), (lines[1], 0, 1)):
+        near.append((value, shifted(value, dx, dy), shifted(value, -dx, -dy)))
+    for (value, low, high), dx, dy in ((near[0], 1, 0), (near[1], 0, 1)):
+        half = value.shape[0] // 2
+        far += [shifted(low[:half], dx, dy), shifted(high[half:], -dx, -dy)]
+    return near, far
 
 
 def per_device(
@@ -551,13 +584,14 @@
     to_next = [(i, i + 1) for i in range(count - 1)]
     to_previous = [(i + 1, i) for i in range(count - 1)]
 
-    first, last = run_pack(key_range, atom_act, atom_bias)
+    ranges = key_range.T
+    first, last = run_pack(ranges, atom_act, atom_bias)
     after = lax.ppermute(first, "seq", to_previous)
     before = lax.ppermute(last, "seq", to_next)
-    column = column_of(pair_bias)
+    bias = lax.all_gather(pair_bias, "samp", axis=0, tiled=True)
     token_row = atom_token.reshape(1, atoms)
     atom_mid, token_act, token_norm = run_atoms(
-        key_range,
+        ranges,
         token_counts,
         before,
         after,
@@ -572,17 +606,15 @@
         gather_weight,
     )
     absorbed = run_queries(token_norm, token_query, token_keyval)
-    parts, plan, ready = spread(token_norm)
-    bias_near = run_stack(column, ready)
-    bias_far = other_core(bias_near)
-    bias_plan = [(side == 0, at, step) for side in range(2) for at, step in enumerate(BIAS_STEPS)]
-    atom_out, token_out, back_rows = run_tokens(
-        plan,
-        parts,
-        bias_plan,
-        bias_near,
-        bias_far,
+    near, far = spread(token_norm)
+    turned = run_reorder(bias, near[1][0])
+    early = run_early(absorbed, bias, turned, near[0] + near[1])
+    atom_out, token_out, back_rows = run_late(
         absorbed,
+        bias,
+        turned,
+        far,
+        early,
         token_act,
         atom_mid,
         token_row,

time: 182 us -> 139 us (0.76)
  the two profiles are of different devices: /device:TPU:6 before, /device:TPU:70 now
where the time goes in v3:
time: 139 us
  Pallas kernels  38.2 us (27%)
  waiting for transfers between devices  36.5 us (26%)
  starting transfers between devices  28.7 us (21%)
  local copies, waits for them, and re-layouts  19.1 us (14%)
  between operations  14.4 us (10%)
  other arithmetic  2.04 us (1%)
    ppermute x5, waiting for transfers between devices, exchanged(): return lax.ppermute(value, 'seq', [(t, t ^ 1 << bit) for t in range(32)])  23.2 us
    ppermute x8, starting transfers between devices, shifted(): return lax.ppermute(value, 'seq', pairs)  12.9 us
    unnamed x47, local copies, waits for them, and re-layouts  10.6 us
    pallas_call x1, Pallas kernels, run_atoms(): pl.pallas_call(atom_kernel, out_shape=(jax.ShapeDtypeStruct((samples, ato...  10.5 us
    pallas_call x1, Pallas kernels, run_early(): pl.pallas_call(early_kernel, out_shape=(jax.ShapeDtypeStruct((samples, ro...  10.5 us
    pallas_call x1, Pallas kernels, run_late(): pl.pallas_call(late_kernel, out_shape=(jax.ShapeDtypeStruct(mid.shape, BF...  10.5 us
    ppermute x1, starting transfers between devices, per_device(): after = lax.ppermute(first, 'seq', to_previous)  6.54 us
    ppermute x1, waiting for transfers between devices, per_device(): previous = lax.ppermute(back_rows[:, tokens - 1], 'seq', to_next)  5.82 us
  transfers between devices with their start and end apart: 17, of which 8 were waited for; matrix products, arithmetic and copies ran while one was open for 7% of the time, Pallas kernels for 20%

profile of v3, /device:TPU:70, one launch (start us, length us, event | category | flops | bytes accessed | tf_op | source)
XLA Modules:
  0.0 138.8 jit_solution(7691941654414869857)
XLA Ops:
  7.2 0.7 all-gather.2.cloned.1.call-update
  7.9 2.2 %pack.1 = (bf16[304,128]{1,0:T(8,128)(2,1)}, bf16[96,128]{1,0:T(8,128)(2,1)}) custom-call(s32[2,12]{1,0:T(2,128)} %bitcast.15, bf16[2,384,128]{2,1,0:T(8,128)(2,1)} %act_hbm.3, bf16[4,12,32,128]{3,2,1,0:T(8,128)(2,1)} %bias_hbm.3), custom_call_target="tpu_custom_call" | custom-call | tf_op jit(solution)/shard_map/pack/pallas_call | solution.py:83
  10.1 6.5 %collective-permute-start.1 = (bf16[304,128]{1,0:T(8,128)(2,1)}, bf16[304,128]{1,0:T(8,128)(2,1)S(1)}, u32[]{:S(2)}, u32[]{:S(2)}) collective-permute-start(bf16[304,128]{1,0:T(8,128)(2,1)} %get-tuple-element.20), channel_id=1, source_target_pairs={{1,0},{2,1},{3,2},{4,3},{5,4},{6,5},{7,6},{8,7},{9,8},{10,9},{11,1... | collective-permute-start | bytes 233480 | tf_op jit(solution)/shard_map/ppermute | solution.py:589
  16.7 1.9 %collective-permute-start = (bf16[96,128]{1,0:T(8,128)(2,1)}, bf16[96,128]{1,0:T(8,128)(2,1)S(1)}, u32[]{:S(2)}, u32[]{:S(2)}) collective-permute-start(bf16[96,128]{1,0:T(8,128)(2,1)} %get-tuple-element.19), channel_id=1, source_target_pairs={{0,1},{1,2},{2,3},{3,4},{4,5},{5,6},{6,7},{7,8},{8,9},{9,10},{10,1... | collective-permute-start | bytes 73736 | tf_op jit(solution)/shard_map/ppermute | solution.py:590
  18.6 1.2 reshape.20.token_ref
  19.8 1.3 reshape.21.token_gain_ref
  21.1 4.5 %collective-permute-done.before_ref = bf16[96,128]{1,0:T(8,128)(2,1)S(1)} collective-permute-done((bf16[96,128]{1,0:T(8,128)(2,1)}, bf16[96,128]{1,0:T(8,128)(2,1)S(1)}, u32[]{:S(2)}, u32[]{:S(2)}) %collective-permute-start) | collective-permute-done | bytes 24608 | tf_op jit(solution)/shard_map/ppermute | solution.py:590
  25.6 0.6 copy-done.20
  26.2 10.5 %atoms.1 = (bf16[2,384,128]{2,1,0:T(8,128)(2,1)}, bf16[2,48,768]{2,1,0:T(8,128)(2,1)}, bf16[2,48,768]{2,1,0:T(8,128)(2,1)}) custom-call(s32[2,12]{1,0:T(2,128)} %bitcast.16, s32[48]{0:T(128)} %count_ref.1, bf16[96,128]{1,0:T(8,128)(2,1)} %copy-done.20, bf16[304,128]{1,0:T(8,128)(2,1)} %copy-done.19, f32[1,128]{1,0:T(1,128)} %bitcast.17, ...), custom_call_target="tpu_custom_call" | custom-call | flops 5000000000 | bytes 1000 | tf_op jit(solution)/shard_map/atoms/pallas_call | solution.py:232
  36.9 1.1 slice_bitcast_fusion.2
  38.0 11.8 %collective-permute-done.2 = bf16[2,48,768]{2,1,0:T(8,128)(2,1)S(1)} collective-permute-done((bf16[2,48,768]{2,1,0:T(8,128)(2,1)}, bf16[2,48,768]{2,1,0:T(8,128)(2,1)S(1)}, u32[]{:S(2)}, u32[]{:S(2)}) %collective-permute-start.2) | collective-permute-done | bytes 147488 | tf_op jit(solution)/shard_map/ppermute | solution.py:517
  50.0 0.6 collective-permute-start.4
  50.6 4.5 %collective-permute-done.3.refs_2_ = bf16[96,768]{1,0:T(8,128)(2,1)S(1)} collective-permute-done((bf16[96,768]{1,0:T(8,128)(2,1)S(1)}, bf16[96,768]{1,0:T(8,128)(2,1)S(1)}, u32[]{:S(2)}, u32[]{:S(2)}) %collective-permute-start.3) | collective-permute-done | bytes 147488 | tf_op jit(solution)/shard_map/ppermute | solution.py:517
  55.1 0.1 collective-permute-done.4.refs_3_
  55.2 2.1 %collective-permute-start.5 = (bf16[192,768]{1,0:T(8,128)(2,1)S(1)}, bf16[192,768]{1,0:T(8,128)(2,1)S(1)}, u32[]{:S(2)}, u32[]{:S(2)}) collective-permute-start(bf16[192,768]{1,0:T(8,128)(2,1)S(1)} %get-tuple-element.24.refs_0_), channel_id=1, source_target_pairs={{0,4},{1,5},{2,6},{3,7},{4,0},{5,1},{6,2},{7,3},{8,12},{9,13},{10,... | collective-permute-start | bytes 884744 | tf_op jit(solution)/shard_map/ppermute | solution.py:517
  57.4 2.3 %collective-permute-start.6 = (bf16[192,768]{1,0:T(8,128)(2,1)S(1)}, bf16[192,768]{1,0:T(8,128)(2,1)S(1)}, u32[]{:S(2)}, u32[]{:S(2)}) collective-permute-start(bf16[192,768]{1,0:T(8,128)(2,1)S(1)} %get-tuple-element.25.refs_1_), channel_id=1, source_target_pairs={{0,16},{1,17},{2,18},{3,19},{4,20},{5,21},{6,22},{7,23},{8,24},{9,... | collective-permute-start | bytes 884744 | tf_op jit(solution)/shard_map/ppermute | solution.py:517
  59.7 3.9 %collective-permute-done.5.refs_2_ = bf16[192,768]{1,0:T(8,128)(2,1)S(1)} collective-permute-done((bf16[192,768]{1,0:T(8,128)(2,1)S(1)}, bf16[192,768]{1,0:T(8,128)(2,1)S(1)}, u32[]{:S(2)}, u32[]{:S(2)}) %collective-permute-start.5) | collective-permute-done | bytes 294944 | tf_op jit(solution)/shard_map/ppermute | solution.py:517
  63.7 2.9 %collective-permute-done.6.refs_3_ = bf16[192,768]{1,0:T(8,128)(2,1)S(1)} collective-permute-done((bf16[192,768]{1,0:T(8,128)(2,1)S(1)}, bf16[192,768]{1,0:T(8,128)(2,1)S(1)}, u32[]{:S(2)}, u32[]{:S(2)}) %collective-permute-start.6) | collective-permute-done | bytes 294944 | tf_op jit(solution)/shard_map/ppermute | solution.py:517
  66.5 1.1 join.5
  67.7 1.4 %collective-permute-start.9 = (bf16[384,768]{1,0:T(8,128)(2,1)}, bf16[384,768]{1,0:T(8,128)(2,1)S(1)}, u32[]{:S(2)}, u32[]{:S(2)}) collective-permute-start(bf16[384,768]{1,0:T(8,128)(2,1)} %get-tuple-element.27.own0_ref), channel_id=1, source_target_pairs={{0,24},{1,25},{2,26},{3,27},{4,28},{5,29},{6,30},{7,31},{8,0},{9,1... | collective-permute-start | bytes 1769480 | tf_op jit(solution)/shard_map/ppermute | solution.py:513
  69.1 0.1 collective-permute-start.11
  69.2 3.1 %collective-permute-start.13 = (bf16[384,768]{1,0:T(8,128)(2,1)}, bf16[384,768]{1,0:T(8,128)(2,1)}, u32[]{:S(2)}, u32[]{:S(2)}) collective-permute-start(bf16[384,768]{1,0:T(8,128)(2,1)} %get-tuple-element.26.after_hbm.own1_ref), channel_id=1, source_target_pairs={{0,6},{1,7},{2,0},{3,1},{4,2},{5,3},{6,4},{7,5},{8,14},{9,15},{10,... | collective-permute-start | bytes 1769480 | tf_op jit(solution)/shard_map/ppermute | solution.py:513
  72.3 1.8 %collective-permute-start.7 = (bf16[384,768]{1,0:T(8,128)(2,1)}, bf16[384,768]{1,0:T(8,128)(2,1)}, u32[]{:S(2)}, u32[]{:S(2)}) collective-permute-start(bf16[384,768]{1,0:T(8,128)(2,1)} %get-tuple-element.27.own0_ref), channel_id=1, source_target_pairs={{0,8},{1,9},{2,10},{3,11},{4,12},{5,13},{6,14},{7,15},{8,16},{9,17... | collective-permute-start | bytes 1769480 | tf_op jit(solution)/shard_map/ppermute | solution.py:513
  74.2 0.9 copy-done.14
  75.1 1.3 copy-done.17
  76.4 2.2 %queries.1.absorbed_ref = bf16[2,768,768]{2,1,0:T(8,128)(2,1)S(1)} custom-call(bf16[2,48,768]{2,1,0:T(8,128)(2,1)S(1)} %copy-done.14, bf16[768,768]{1,0:T(8,128)(2,1)S(1)} %copy-done.17, bf16[768,1536]{1,0:T(8,128)(2,1)S(1)} %copy-done), custom_call_target="tpu_custom_call" | custom-call | flops 2000000000 | bytes 1000 | tf_op jit(solution)/shard_map/queries/pallas_call | solution.py:277
  78.6 1.4 %copy-done.4 = bf16[2,768,768]{2,1,0:T(8,128)(2,1)} copy-done((bf16[2,768,768]{2,1,0:T(8,128)(2,1)}, bf16[2,768,768]{2,1,0:T(8,128)(2,1)S(1)}, u32[]{:S(2)}) %copy-start.4) | copy-done | bytes 2359320
  80.0 2.2 %collective-permute-done.9.high0_ref = bf16[384,768]{1,0:T(8,128)(2,1)S(1)} collective-permute-done((bf16[384,768]{1,0:T(8,128)(2,1)}, bf16[384,768]{1,0:T(8,128)(2,1)S(1)}, u32[]{:S(2)}, u32[]{:S(2)}) %collective-permute-start.9) | collective-permute-done | bytes 589856 | tf_op jit(solution)/shard_map/ppermute | solution.py:513
  82.2 0.8 slice.47
  82.9 0.9 copy-done.10
  83.8 0.8 slice.48
  84.6 0.3 collective-permute-start.12
  84.9 1.7 %slice.49 = bf16[192,768]{1,0:T(8,128)(2,1)} slice(bf16[384,768]{1,0:T(8,128)(2,1)} %collective-permute-done.13.high1_ref), slice={[192:384], [0:768]} | slice | bytes 589824 | tf_op jit(solution)/shard_map/slice | solution.py:555
  86.6 2.9 %collective-permute-start.14 = (bf16[192,768]{1,0:T(8,128)(2,1)}, bf16[192,768]{1,0:T(8,128)(2,1)S(1)}, u32[]{:S(2)}, u32[]{:S(2)}) collective-permute-start(bf16[192,768]{1,0:T(8,128)(2,1)} %slice.49), channel_id=1, source_target_pairs={{0,6},{1,7},{2,0},{3,1},{4,2},{5,3},{6,4},{7,5},{8,14},{9,15},{10,... | collective-permute-start | bytes 884744 | tf_op jit(solution)/shard_map/ppermute | solution.py:513
  89.5 1.7 %slice.46 = bf16[192,768]{1,0:T(8,128)(2,1)} slice(bf16[384,768]{1,0:T(8,128)(2,1)} %collective-permute-done.7.low0_ref), slice={[0:192], [0:768]} | slice | bytes 589824 | tf_op jit(solution)/shard_map/slice | solution.py:555
  91.2 3.2 %collective-permute-start.8 = (bf16[192,768]{1,0:T(8,128)(2,1)}, bf16[192,768]{1,0:T(8,128)(2,1)S(1)}, u32[]{:S(2)}, u32[]{:S(2)}) collective-permute-start(bf16[192,768]{1,0:T(8,128)(2,1)} %slice.46), channel_id=1, source_target_pairs={{0,8},{1,9},{2,10},{3,11},{4,12},{5,13},{6,14},{7,15},{8,16},{9,17... | collective-permute-start | bytes 884744 | tf_op jit(solution)/shard_map/ppermute | solution.py:513
  94.4 1.7 %copy-done.2 = bf16[16,48,1536]{2,1,0:T(8,128)(2,1)S(1)} copy-done((bf16[16,48,1536]{2,1,0:T(8,128)(2,1)S(1)}, bf16[16,48,1536]{2,1,0:T(8,128)(2,1)}, u32[]{:S(2)}) %copy-start.2) | copy-done | bytes 2359320
  96.1 1.0 reorder.1.bias1_ref
  97.1 0.7 copy-done.3
  97.8 0.1 copy-done.11
  97.9 2.0 %copy-done.5 = bf16[2,768,768]{2,1,0:T(8,128)(2,1)S(1)} copy-done((bf16[2,768,768]{2,1,0:T(8,128)(2,1)S(1)}, bf16[2,768,768]{2,1,0:T(8,128)(2,1)}, u32[]{:S(2)}) %copy-start.5) | copy-done | bytes 2359320
  99.9 1.1 copy-done.13
  101.0 10.5 %early.1 = (f32[2,768,768]{2,1,0:T(8,128)S(1)}, f32[2,768,128]{2,1,0:T(8,128)S(1)}, f32[2,768,128]{2,1,0:T(8,128)S(1)}) custom-call(bf16[2,768,768]{2,1,0:T(8,128)(2,1)S(1)} %copy-done.5, bf16[16,48,1536]{2,1,0:T(8,128)(2,1)S(1)} %copy-done.3, bf16[16,48,1536]{2,1,0:T(8,128)(2,1)S(1)} %reorder.1.bias1_ref, bf16[384,768]{1,0:T(8,128)(2,1)} %get-tuple-element.27.own0_ref, ...), custom_call_target="tpu_custom_call" | custom-call | flops 8000000000 | bytes 1000 | tf_op jit(solution)/shard_map/early/pallas_call | solution.py:371
  111.6 10.5 %late.1 = (bf16[2,384,128]{2,1,0:T(8,128)(2,1)}, bf16[2,48,768]{2,1,0:T(8,128)(2,1)}, bf16[2,48,128]{2,1,0:T(8,128)(2,1)S(1)}) custom-call(bf16[2,768,768]{2,1,0:T(8,128)(2,1)S(1)} %copy-done.6, bf16[16,48,1536]{2,1,0:T(8,128)(2,1)S(1)} %copy-done.3, bf16[16,48,1536]{2,1,0:T(8,128)(2,1)S(1)} %reorder.1.bias1_ref, ...), custom_call_target="tpu_custom_call" | custom-call | flops 5000000000 | bytes 1000 | tf_op jit(solution)/shard_map/late/pallas_call | solution.py:487
  122.2 1.9 %collective-permute-start.15 = (bf16[2,128]{1,0:T(2,128)(2,1)S(1)}, bf16[2,128]{1,0:T(2,128)(2,1)S(1)}, u32[]{:S(2)}, u32[]{:S(2)}) collective-permute-start(bf16[2,128]{1,0:T(2,128)(2,1)S(1)} %bitcast.18), channel_id=1, source_target_pairs={{0,1},{1,2},{2,3},{3,4},{4,5},{5,6},{6,7},{7,8},{8,9},{9,10},{10,1... | collective-permute-start | bytes 1544 | tf_op jit(solution)/shard_map/ppermute | solution.py:624
  124.1 0.7 slice_compare_fusion
  124.8 5.8 %collective-permute-done.15 = bf16[2,128]{1,0:T(2,128)(2,1)S(1)} collective-permute-done((bf16[2,128]{1,0:T(2,128)(2,1)S(1)}, bf16[2,128]{1,0:T(2,128)(2,1)S(1)}, u32[]{:S(2)}, u32[]{:S(2)}) %collective-permute-start.15) | collective-permute-done | bytes 544 | tf_op jit(solution)/shard_map/ppermute | solution.py:624
  130.6 1.4 fusion
  (57 shorter events, 0.5 us)
Async XLA Ops:
  7.2 87.3 %all-gather.2.cloned.1.call-start = ((), (), s32[]{:S(2)}) async-start(), calls=%async_computation | async-start | bytes 2654208 | tf_op jit(solution)/shard_map/all_gather | solution.py:591
  10.1 15.5 %collective-permute-start.1 = (bf16[304,128]{1,0:T(8,128)(2,1)}, bf16[304,128]{1,0:T(8,128)(2,1)S(1)}, u32[]{:S(2)}, u32[]{:S(2)}) collective-permute-start(bf16[304,128]{1,0:T(8,128)(2,1)} %get-tuple-element.20), channel_id=1, source_target_pairs={{1,0},{2,1},{3,2},{4,3},{5,4},{6,5},{7,6},{8,7},{9,8},{10,9},{11,1... | collective-permute-start | bytes 233480 | tf_op jit(solution)/shard_map/ppermute | solution.py:589
  16.7 8.9 %collective-permute-start = (bf16[96,128]{1,0:T(8,128)(2,1)}, bf16[96,128]{1,0:T(8,128)(2,1)S(1)}, u32[]{:S(2)}, u32[]{:S(2)}) collective-permute-start(bf16[96,128]{1,0:T(8,128)(2,1)} %get-tuple-element.19), channel_id=1, source_target_pairs={{0,1},{1,2},{2,3},{3,4},{4,5},{5,6},{6,7},{7,8},{8,9},{9,10},{10,1... | collective-permute-start | bytes 73736 | tf_op jit(solution)/shard_map/ppermute | solution.py:590
  25.6 0.6 copy-start.20
  25.6 0.6 copy-start.19
  36.8 37.4 %copy-start.18 = (f32[768]{0:T(1024)S(1)}, f32[768]{0:T(1024)}, u32[]{:S(2)}) copy-start(f32[768]{0:T(1024)} %param.34) | copy-start | bytes 9220
  36.8 37.4 %copy-start = (bf16[768,1536]{1,0:T(8,128)(2,1)S(1)}, bf16[768,1536]{1,0:T(8,128)(2,1)}, u32[]{:S(2)}) copy-start(bf16[768,1536]{1,0:T(8,128)(2,1)} %keyval_hbm.5) | copy-start | bytes 7077892
  36.8 13.0 %collective-permute-start.2 = (bf16[2,48,768]{2,1,0:T(8,128)(2,1)}, bf16[2,48,768]{2,1,0:T(8,128)(2,1)S(1)}, u32[]{:S(2)}, u32[]{:S(2)}) collective-permute-start(bf16[2,48,768]{2,1,0:T(8,128)(2,1)} %get-tuple-element.21.norm_ref), channel_id=1, source_target_pairs={{0,1},{1,0},{2,3},{3,2},{4,5},{5,4},{6,7},{7,6},{8,9},{9,8},{10,11... | collective-permute-start | bytes 442376 | tf_op jit(solution)/shard_map/ppermute | solution.py:517
  49.9 5.2 %collective-permute-start.3 = (bf16[96,768]{1,0:T(8,128)(2,1)S(1)}, bf16[96,768]{1,0:T(8,128)(2,1)S(1)}, u32[]{:S(2)}, u32[]{:S(2)}) collective-permute-start(bf16[96,768]{1,0:T(8,128)(2,1)S(1)} %get-tuple-element.22.refs_0_), channel_id=1, source_target_pairs={{0,2},{1,3},{2,0},{3,1},{4,6},{5,7},{6,4},{7,5},{8,10},{9,11},{10,... | collective-permute-start | bytes 442376 | tf_op jit(solution)/shard_map/ppermute | solution.py:517
  50.0 5.2 %collective-permute-start.4 = (bf16[96,768]{1,0:T(8,128)(2,1)S(1)}, bf16[96,768]{1,0:T(8,128)(2,1)S(1)}, u32[]{:S(2)}, u32[]{:S(2)}) collective-permute-start(bf16[96,768]{1,0:T(8,128)(2,1)S(1)} %get-tuple-element.23.refs_1_), channel_id=1, source_target_pairs={{0,8},{1,9},{2,10},{3,11},{4,12},{5,13},{6,14},{7,15},{8,0},{9,1},... | collective-permute-start | bytes 442376 | tf_op jit(solution)/shard_map/ppermute | solution.py:517
  55.2 8.4 %collective-permute-start.5 = (bf16[192,768]{1,0:T(8,128)(2,1)S(1)}, bf16[192,768]{1,0:T(8,128)(2,1)S(1)}, u32[]{:S(2)}, u32[]{:S(2)}) collective-permute-start(bf16[192,768]{1,0:T(8,128)(2,1)S(1)} %get-tuple-element.24.refs_0_), channel_id=1, source_target_pairs={{0,4},{1,5},{2,6},{3,7},{4,0},{5,1},{6,2},{7,3},{8,12},{9,13},{10,... | collective-permute-start | bytes 884744 | tf_op jit(solution)/shard_map/ppermute | solution.py:517
  57.4 9.2 %collective-permute-start.6 = (bf16[192,768]{1,0:T(8,128)(2,1)S(1)}, bf16[192,768]{1,0:T(8,128)(2,1)S(1)}, u32[]{:S(2)}, u32[]{:S(2)}) collective-permute-start(bf16[192,768]{1,0:T(8,128)(2,1)S(1)} %get-tuple-element.25.refs_1_), channel_id=1, source_target_pairs={{0,16},{1,17},{2,18},{3,19},{4,20},{5,21},{6,22},{7,23},{8,24},{9,... | collective-permute-start | bytes 884744 | tf_op jit(solution)/shard_map/ppermute | solution.py:517
  67.7 14.5 %collective-permute-start.9 = (bf16[384,768]{1,0:T(8,128)(2,1)}, bf16[384,768]{1,0:T(8,128)(2,1)S(1)}, u32[]{:S(2)}, u32[]{:S(2)}) collective-permute-start(bf16[384,768]{1,0:T(8,128)(2,1)} %get-tuple-element.27.own0_ref), channel_id=1, source_target_pairs={{0,24},{1,25},{2,26},{3,27},{4,28},{5,29},{6,30},{7,31},{8,0},{9,1... | collective-permute-start | bytes 1769480 | tf_op jit(solution)/shard_map/ppermute | solution.py:513
  69.1 14.7 %collective-permute-start.11 = (bf16[384,768]{1,0:T(8,128)(2,1)}, bf16[384,768]{1,0:T(8,128)(2,1)S(1)}, u32[]{:S(2)}, u32[]{:S(2)}) collective-permute-start(bf16[384,768]{1,0:T(8,128)(2,1)} %get-tuple-element.26.after_hbm.own1_ref), channel_id=1, source_target_pairs={{0,2},{1,3},{2,4},{3,5},{4,6},{5,7},{6,0},{7,1},{8,10},{9,11},{10,... | collective-permute-start | bytes 1769480 | tf_op jit(solution)/shard_map/ppermute | solution.py:513
  69.2 15.7 %collective-permute-start.13 = (bf16[384,768]{1,0:T(8,128)(2,1)}, bf16[384,768]{1,0:T(8,128)(2,1)}, u32[]{:S(2)}, u32[]{:S(2)}) collective-permute-start(bf16[384,768]{1,0:T(8,128)(2,1)} %get-tuple-element.26.after_hbm.own1_ref), channel_id=1, source_target_pairs={{0,6},{1,7},{2,0},{3,1},{4,2},{5,3},{6,4},{7,5},{8,14},{9,15},{10,... | collective-permute-start | bytes 1769480 | tf_op jit(solution)/shard_map/ppermute | solution.py:513
  72.3 17.2 %collective-permute-start.7 = (bf16[384,768]{1,0:T(8,128)(2,1)}, bf16[384,768]{1,0:T(8,128)(2,1)}, u32[]{:S(2)}, u32[]{:S(2)}) collective-permute-start(bf16[384,768]{1,0:T(8,128)(2,1)} %get-tuple-element.27.own0_ref), channel_id=1, source_target_pairs={{0,8},{1,9},{2,10},{3,11},{4,12},{5,13},{6,14},{7,15},{8,16},{9,17... | collective-permute-start | bytes 1769480 | tf_op jit(solution)/shard_map/ppermute | solution.py:513
  74.2 0.9 copy-start.14
  75.1 1.3 copy-start.17
  78.6 1.4 %copy-start.4 = (bf16[2,768,768]{2,1,0:T(8,128)(2,1)}, bf16[2,768,768]{2,1,0:T(8,128)(2,1)S(1)}, u32[]{:S(2)}) copy-start(bf16[2,768,768]{2,1,0:T(8,128)(2,1)S(1)} %queries.1.absorbed_ref) | copy-start | bytes 7077892
  82.9 0.9 copy-start.10
  83.8 27.7 %collective-permute-start.10 = (bf16[192,768]{1,0:T(8,128)(2,1)}, bf16[192,768]{1,0:T(8,128)(2,1)S(1)}, u32[]{:S(2)}, u32[]{:S(2)}) collective-permute-start(bf16[192,768]{1,0:T(8,128)(2,1)} %slice.47), channel_id=1, source_target_pairs={{0,24},{1,25},{2,26},{3,27},{4,28},{5,29},{6,30},{7,31},{8,0},{9,1... | collective-permute-start | bytes 884744 | tf_op jit(solution)/shard_map/ppermute | solution.py:513
  83.8 1.1 copy-start.12
  84.6 27.0 %collective-permute-start.12 = (bf16[192,768]{1,0:T(8,128)(2,1)}, bf16[192,768]{1,0:T(8,128)(2,1)S(1)}, u32[]{:S(2)}, u32[]{:S(2)}) collective-permute-start(bf16[192,768]{1,0:T(8,128)(2,1)} %slice.48), channel_id=1, source_target_pairs={{0,2},{1,3},{2,4},{3,5},{4,6},{5,7},{6,0},{7,1},{8,10},{9,11},{10,... | collective-permute-start | bytes 884744 | tf_op jit(solution)/shard_map/ppermute | solution.py:513
  86.6 25.0 %collective-permute-start.14 = (bf16[192,768]{1,0:T(8,128)(2,1)}, bf16[192,768]{1,0:T(8,128)(2,1)S(1)}, u32[]{:S(2)}, u32[]{:S(2)}) collective-permute-start(bf16[192,768]{1,0:T(8,128)(2,1)} %slice.49), channel_id=1, source_target_pairs={{0,6},{1,7},{2,0},{3,1},{4,2},{5,3},{6,4},{7,5},{8,14},{9,15},{10,... | collective-permute-start | bytes 884744 | tf_op jit(solution)/shard_map/ppermute | solution.py:513
  91.2 20.3 %collective-permute-start.8 = (bf16[192,768]{1,0:T(8,128)(2,1)}, bf16[192,768]{1,0:T(8,128)(2,1)S(1)}, u32[]{:S(2)}, u32[]{:S(2)}) collective-permute-start(bf16[192,768]{1,0:T(8,128)(2,1)} %slice.46), channel_id=1, source_target_pairs={{0,8},{1,9},{2,10},{3,11},{4,12},{5,13},{6,14},{7,15},{8,16},{9,17... | collective-permute-start | bytes 884744 | tf_op jit(solution)/shard_map/ppermute | solution.py:513
  94.4 1.7 %copy-start.2 = (bf16[16,48,1536]{2,1,0:T(8,128)(2,1)S(1)}, bf16[16,48,1536]{2,1,0:T(8,128)(2,1)}, u32[]{:S(2)}) copy-start(bf16[16,48,1536]{2,1,0:T(8,128)(2,1)} %all-gather.2.cloned.1.call-done.bias_ref.bias0_ref) | copy-start | bytes 7077892
  96.1 1.7 %copy-start.3 = (bf16[16,48,1536]{2,1,0:T(8,128)(2,1)S(1)}, bf16[16,48,1536]{2,1,0:T(8,128)(2,1)}, u32[]{:S(2)}) copy-start(bf16[16,48,1536]{2,1,0:T(8,128)(2,1)} %all-gather.2.cloned.1.call-done.bias_ref.bias0_ref) | copy-start | bytes 7077892
  96.1 1.8 %copy-start.11 = (bf16[384,768]{1,0:T(8,128)(2,1)S(1)}, bf16[384,768]{1,0:T(8,128)(2,1)}, u32[]{:S(2)}) copy-start(bf16[384,768]{1,0:T(8,128)(2,1)} %copy-done.10) | copy-start | bytes 1769476
  96.1 15.4 %slice-start = ((s8[4718592]{0:T(1024)(128)(4,1)}), s8[4194304]{0:T(1024)(128)(4,1)S(1)}, s32[]{:S(2)}) async-start(s8[4718592]{0:T(1024)(128)(4,1)} %bitcast.13), calls=%async_computation.1 | async-start | bytes 8388608
  97.9 2.0 %copy-start.5 = (bf16[2,768,768]{2,1,0:T(8,128)(2,1)S(1)}, bf16[2,768,768]{2,1,0:T(8,128)(2,1)}, u32[]{:S(2)}) copy-start(bf16[2,768,768]{2,1,0:T(8,128)(2,1)} %copy-done.4) | copy-start | bytes 7077892
  99.9 1.1 copy-start.13
  100.9 10.6 %slice-start.1 = ((s8[4718592]{0:T(1024)(128)(4,1)}), s8[524288]{0:T(1024)(128)(4,1)S(1)}, s32[]{:S(2)}) async-start(s8[4718592]{0:T(1024)(128)(4,1)} %bitcast.13), calls=%async_computation.2 | async-start | bytes 1048576
  100.9 10.7 %copy-start.1 = (bf16[1536,768]{1,0:T(8,128)(2,1)S(1)}, bf16[1536,768]{1,0:T(8,128)(2,1)}, u32[]{:S(2)}) copy-start(bf16[1536,768]{1,0:T(8,128)(2,1)} %down_hbm.1) | copy-start | bytes 7077892
  100.9 10.7 %copy-start.6 = (bf16[2,768,768]{2,1,0:T(8,128)(2,1)S(1)}, bf16[2,768,768]{2,1,0:T(8,128)(2,1)}, u32[]{:S(2)}) copy-start(bf16[2,768,768]{2,1,0:T(8,128)(2,1)} %copy-done.4) | copy-start | bytes 7077892
  100.9 10.7 %copy-start.7 = (bf16[768,768]{1,0:T(8,128)(2,1)S(1)}, bf16[768,768]{1,0:T(8,128)(2,1)}, u32[]{:S(2)}) copy-start(bf16[768,768]{1,0:T(8,128)(2,1)} %output_hbm.3) | copy-start | bytes 3538948
  100.9 10.7 %copy-start.8 = (bf16[768,128]{1,0:T(8,128)(2,1)S(1)}, bf16[768,128]{1,0:T(8,128)(2,1)}, u32[]{:S(2)}) copy-start(bf16[768,128]{1,0:T(8,128)(2,1)} %back_hbm.1) | copy-start | bytes 589828
  100.9 10.7 %copy-start.9 = (bf16[2,384,128]{2,1,0:T(8,128)(2,1)S(1)}, bf16[2,384,128]{2,1,0:T(8,128)(2,1)}, u32[]{:S(2)}) copy-start(bf16[2,384,128]{2,1,0:T(8,128)(2,1)} %get-tuple-element.32.mid_ref) | copy-start | bytes 589828
  101.0 10.7 %copy-start.15 = (bf16[2,48,768]{2,1,0:T(8,128)(2,1)S(1)}, bf16[2,48,768]{2,1,0:T(8,128)(2,1)}, u32[]{:S(2)}) copy-start(bf16[2,48,768]{2,1,0:T(8,128)(2,1)} %get-tuple-element.31.tokact_ref) | copy-start | bytes 442372
  101.0 10.7 %copy-start.16 = (s32[1,384]{1,0:T(1,128)S(1)}, s32[1,384]{1,0:T(1,128)}, u32[]{:S(2)}) copy-start(s32[1,384]{1,0:T(1,128)} %reshape.20.token_ref) | copy-start | bytes 4612
  122.2 8.4 %collective-permute-start.15 = (bf16[2,128]{1,0:T(2,128)(2,1)S(1)}, bf16[2,128]{1,0:T(2,128)(2,1)S(1)}, u32[]{:S(2)}, u32[]{:S(2)}) collective-permute-start(bf16[2,128]{1,0:T(2,128)(2,1)S(1)} %bitcast.18), channel_id=1, source_target_pairs={{0,1},{1,2},{2,3},{3,4},{4,5},{5,6},{6,7},{7,8},{8,9},{9,10},{10,1... | collective-permute-start | bytes 1544 | tf_op jit(solution)/shard_map/ppermute | solution.py:624
Sparse Core Ops, SparseCore 0:
  9.8 41.8 all-gather.1

commit v4 on v3

--- a/solution.py
+++ b/solution.py
@@ -244,7 +244,7 @@
             pltpu.SemaphoreType.DMA((len(arrays),)),
         ],
         compiler_params=pltpu.CompilerParams(vmem_limit_bytes=60 * 2**20),
-        cost_estimate=cost(5_000_000_000),
+        cost_estimate=cost(1_000_000),
         name="atoms",
     )(key_range, counts, before, after, gain, token, token_gain, *arrays)
 
@@ -285,33 +285,62 @@
             pltpu.SemaphoreType.DMA((2,)),
         ],
         compiler_params=pltpu.CompilerParams(vmem_limit_bytes=30 * 2**20),
-        cost_estimate=cost(2_000_000_000),
+        cost_estimate=cost(1_000_000),
         name="queries",
     )(norm, token_query, token_keyval)
 
 
-def reorder_kernel(bias_ref, after_hbm, out_ref):
-    heads, tokens, keys = bias_ref.shape
+def stack_kernel(steps, *refs):
+    column = lax.axis_index("samp") // 2
+    stacked = refs[-1]
+    for step, piece in zip(steps, refs):
+        stacked[(column + step) % len(steps)] = piece[...]
+
+
+def run_stack(pieces, steps, after):
+    count = len(pieces)
+    return pl.pallas_call(
+        functools.partial(stack_kernel, steps),
+        out_shape=jax.ShapeDtypeStruct((count,) + pieces[0].shape, pieces[0].dtype),
+        in_specs=[vmem()] * count + [anywhere()],
+        out_specs=vmem(),
+        compiler_params=pltpu.CompilerParams(vmem_limit_bytes=16 * 2**20),
+        cost_estimate=cost(1_000_000),
+        name="stack",
+    )(*pieces, after)
+
+
+def reorder_kernel(near_ref, far_ref, bias_ref, turned_ref):
+    columns, heads, _, keys = near_ref.shape
     line = keys // 4
     part = line // 4
-    for h in range(heads):
-        rows = bias_ref[h]
-        blocks = [
-            rows[:, line * x + part * y : line * x + part * (y + 1)] for y in range(4) for x in range(4)
-        ]
-        out_ref[h] = jnp.concatenate(blocks, axis=1)
-
-
-def run_reorder(bias, after):
+    core = lax.axis_index("samp") % 2
+    for source, which in ((near_ref, core), (far_ref, 1 - core)):
+        for column in range(columns):
+            for head in range(heads):
+                at = (2 * column + which) * heads + head
+                rows = source[column, head]
+                bias_ref[at] = rows
+                blocks = [
+                    rows[:, line * x + part * y : line * x + part * (y + 1)]
+                    for y in range(4)
+                    for x in range(4)
+                ]
+                turned_ref[at] = jnp.concatenate(blocks, axis=1)
+
+
+def run_reorder(near, far):
+    columns, heads, tokens, keys = near.shape
+    shape = jax.ShapeDtypeStruct((2 * columns * heads, tokens, keys), BF16)
     return pl.pallas_call(
         reorder_kernel,
-        out_shape=jax.ShapeDtypeStruct(bias.shape, BF16),
-        in_specs=[vmem(), anywhere()],
-        out_specs=vmem(),
+        out_shape=(shape, shape),
+        in_specs=[vmem(), vmem()],
+        out_specs=(vmem(), vmem()),
         compiler_params=pltpu.CompilerParams(vmem_limit_bytes=24 * 2**20),
         cost_estimate=cost(2_000_000_000),
         name="reorder",
-    )(bias, after)
+    )(near, far)
 
 
 def place(device, sample):
@@ -387,10 +416,8 @@
     absorbed_ref,
     bias0_ref,
     bias1_ref,
-    far0_low_ref,
-    far0_high_ref,
-    far1_low_ref,
-    far1_high_ref,
+    far0_ref,
+    far1_ref,
     mixed_ref,
     best_ref,
     total_ref,
@@ -434,10 +461,9 @@
     lanes = GROUP * head_size
     head_of = lane_group(tokens, lanes, head_size)
     masks32 = [(head_of == h).astype(F32) for h in range(GROUP)]
-    halves = ((far0_low_ref, far0_high_ref), (far1_low_ref, far1_high_ref))
     for s in range(samples):
         far = (place(device, s) + 2) % 4
-        piece = jnp.concatenate([halves[s][0][...], halves[s][1][...]], axis=0)
+        piece = (far0_ref, far1_ref)[s][...]
         for g in range(HEADS // GROUP):
             columns = slice(lanes * g, lanes * (g + 1))
             scores = piece_scores(absorbed_ref[s, columns], piece, (bias0_ref, bias1_ref)[s], g, far)
@@ -491,7 +517,7 @@
             jax.ShapeDtypeStruct(tokact.shape, BF16),
             jax.ShapeDtypeStruct((samples, tokens, mid.shape[2]), BF16),
         ),
-        in_specs=[vmem()] * 14 + [anywhere()] * 5,
+        in_specs=[vmem()] * 12 + [anywhere()] * 5,
         out_specs=(vmem(),) * 3,
         scratch_shapes=[pltpu.VMEM((width, width), BF16)]
         + [pltpu.VMEM(w.shape, w.dtype) for w in weights[1:]]
@@ -546,14 +572,29 @@
     other = exchanged(norm, 0)
     lines = joined([norm[0], norm[1]], [other[0], other[1]], (0, 0))
     for bits in ((1, 3), (2, 4)):
+        earlier = lines
         lines = joined(lines, [exchanged(v, b) for v, b in zip(lines, bits)], bits)
     near, far = [], []
     for value, dx, dy in ((lines[0], 1, 0), (lines[1], 0, 1)):
         near.append((value, shifted(value, dx, dy), shifted(value, -dx, -dy)))
-    for (value, low, high), dx, dy in ((near[0], 1, 0), (near[1], 0, 1)):
-        half = value.shape[0] // 2
-        far += [shifted(low[:half], dx, dy), shifted(high[half:], -dx, -dy)]
-    return near, far
+        far.append(shifted(value, 2 * dx, 2 * dy))
+    return near, far, earlier[1]
+
+
+BIAS_STEPS = (0, 3, 1, 2)
+
+
+def column_of(bias):
+    count = lax.axis_size("samp")
+
+    def hop(by):
+        return lax.ppermute(bias, "samp", [((i + 2 * by) % count, i) for i in range(count)])
+
+    return [bias] + [hop(step) for step in BIAS_STEPS[1:]]
+
+
+def other_core(value):
+    return lax.ppermute(value, "samp", [(i, i ^ 1) for i in range(lax.axis_size("samp"))])
 
 
 def per_device(
@@ -588,7 +629,7 @@
     first, last = run_pack(ranges, atom_act, atom_bias)
     after = lax.ppermute(first, "seq", to_previous)
     before = lax.ppermute(last, "seq", to_next)
-    bias = lax.all_gather(pair_bias, "samp", axis=0, tiled=True)
+    pieces = column_of(lax.optimization_barrier((pair_bias, first))[0])
     token_row = atom_token.reshape(1, atoms)
     atom_mid, token_act, token_norm = run_atoms(
         ranges,
@@ -606,8 +647,9 @@
         gather_weight,
     )
     absorbed = run_queries(token_norm, token_query, token_keyval)
-    near, far = spread(token_norm)
-    turned = run_reorder(bias, near[1][0])
+    near, far, ready = spread(token_norm)
+    bias_near = run_stack(pieces, BIAS_STEPS, ready)
+    bias, turned = run_reorder(bias_near, other_core(bias_near))
     early = run_early(absorbed, bias, turned, near[0] + near[1])
     atom_out, token_out, back_rows = run_late(
         absorbed,

time: 139 us -> 131 us (0.942)
  the two profiles are of different devices: /device:TPU:70 before, /device:TPU:6 now
where the time goes in v4:
time: 131 us
  Pallas kernels  42.6 us (33%)
  waiting for transfers between devices  41.7 us (32%)
  starting transfers between devices  38.5 us (29%)
  local copies, waits for them, and re-layouts  5.09 us (4%)
  other arithmetic  2.04 us (2%)
    ppermute x5, waiting for transfers between devices, exchanged(): return lax.ppermute(value, 'seq', [(t, t ^ 1 << bit) for t in range(32)])  20.5 us
    ppermute x6, waiting for transfers between devices, shifted(): return lax.ppermute(value, 'seq', pairs)  15.3 us
    pallas_call x1, Pallas kernels, run_early(): pl.pallas_call(early_kernel, out_shape=(jax.ShapeDtypeStruct((samples, ro...  10.9 us
    pallas_call x1, Pallas kernels, run_atoms(): pl.pallas_call(atom_kernel, out_shape=(jax.ShapeDtypeStruct((samples, ato...  10.5 us
    ppermute x3, starting transfers between devices, hop(): lax.ppermute(bias, 'samp', [((i + 2 * by) % count, i) for i in range(coun...  10.5 us
    pallas_call x1, Pallas kernels, run_late(): pl.pallas_call(late_kernel, out_shape=(jax.ShapeDtypeStruct(mid.shape, BF...  10.5 us
    ppermute x6, starting transfers between devices, shifted(): return lax.ppermute(value, 'seq', pairs)  9.82 us
    ppermute x5, starting transfers between devices, exchanged(): return lax.ppermute(value, 'seq', [(t, t ^ 1 << bit) for t in range(32)])  7.78 us
  transfers between devices with their start and end apart: 18, of which 8 were waited for; matrix products, arithmetic and copies ran while one was open for 3% of the time, Pallas kernels for 21%

profile of v4, /device:TPU:6, one launch (start us, length us, event | category | flops | bytes accessed | tf_op | source)
XLA Modules:
  0.0 130.9 jit_solution(16694275991625064731)
XLA Ops:
  0.6 0.0 copy-start.5
  0.6 2.3 %pack.1 = (bf16[304,128]{1,0:T(8,128)(2,1)}, bf16[96,128]{1,0:T(8,128)(2,1)}) custom-call(s32[2,12]{1,0:T(2,128)} %bitcast.15, bf16[2,384,128]{2,1,0:T(8,128)(2,1)} %act_hbm.3, bf16[4,12,32,128]{3,2,1,0:T(8,128)(2,1)} %bias_hbm.3), custom_call_target="tpu_custom_call" | custom-call | tf_op jit(solution)/shard_map/pack/pallas_call | solution.py:83
  3.0 6.5 %collective-permute-start.1 = (bf16[304,128]{1,0:T(8,128)(2,1)}, bf16[304,128]{1,0:T(8,128)(2,1)S(1)}, u32[]{:S(2)}, u32[]{:S(2)}) collective-permute-start(bf16[304,128]{1,0:T(8,128)(2,1)} %get-tuple-element.23), channel_id=1, source_target_pairs={{1,0},{2,1},{3,2},{4,3},{5,4},{6,5},{7,6},{8,7},{9,8},{10,9},{11,1... | collective-permute-start | bytes 233480 | tf_op jit(solution)/shard_map/ppermute | solution.py:630
  9.5 1.9 %collective-permute-start = (bf16[96,128]{1,0:T(8,128)(2,1)}, bf16[96,128]{1,0:T(8,128)(2,1)S(1)}, u32[]{:S(2)}, u32[]{:S(2)}) collective-permute-start(bf16[96,128]{1,0:T(8,128)(2,1)} %get-tuple-element.22), channel_id=1, source_target_pairs={{0,1},{1,2},{2,3},{3,4},{4,5},{5,6},{6,7},{7,8},{8,9},{9,10},{10,1... | collective-permute-start | bytes 73736 | tf_op jit(solution)/shard_map/ppermute | solution.py:631
  11.5 3.3 %collective-permute-start.2 = (bf16[2,48,1536]{2,1,0:T(8,128)(2,1)}, bf16[2,48,1536]{2,1,0:T(8,128)(2,1)}, u32[]{:S(2)}, u32[]{:S(2)}) collective-permute-start(bf16[2,48,1536]{2,1,0:T(8,128)(2,1)} %refs_0_), channel_id=1, source_target_pairs={{192,0},{224,32},{0,64},{32,96},{64,128},{96,160},{128,192},{160,2... | collective-permute-start | bytes 884744 | tf_op jit(solution)/shard_map/ppermute | solution.py:591
  14.8 2.2 %collective-permute-start.3 = (bf16[2,48,1536]{2,1,0:T(8,128)(2,1)}, bf16[2,48,1536]{2,1,0:T(8,128)(2,1)}, u32[]{:S(2)}, u32[]{:S(2)}) collective-permute-start(bf16[2,48,1536]{2,1,0:T(8,128)(2,1)} %refs_0_), channel_id=1, source_target_pairs={{64,0},{96,32},{128,64},{160,96},{192,128},{224,160},{0,192},{32,2... | collective-permute-start | bytes 884744 | tf_op jit(solution)/shard_map/ppermute | solution.py:591
  17.0 4.9 %collective-permute-start.4 = (bf16[2,48,1536]{2,1,0:T(8,128)(2,1)}, bf16[2,48,1536]{2,1,0:T(8,128)(2,1)}, u32[]{:S(2)}, u32[]{:S(2)}) collective-permute-start(bf16[2,48,1536]{2,1,0:T(8,128)(2,1)} %refs_0_), channel_id=1, source_target_pairs={{128,0},{160,32},{192,64},{224,96},{0,128},{32,160},{64,192},{96,2... | collective-permute-start | bytes 884744 | tf_op jit(solution)/shard_map/ppermute | solution.py:591
  22.0 1.2 reshape.20.token_ref
  23.2 1.3 reshape.21.token_gain_ref
  24.5 0.6 copy-done.11
  25.1 0.0 copy-done.10
  25.1 10.5 %atoms.1 = (bf16[2,384,128]{2,1,0:T(8,128)(2,1)}, bf16[2,48,768]{2,1,0:T(8,128)(2,1)}, bf16[2,48,768]{2,1,0:T(8,128)(2,1)}) custom-call(s32[2,12]{1,0:T(2,128)} %bitcast.16, s32[48]{0:T(128)} %count_ref.1, bf16[96,128]{1,0:T(8,128)(2,1)} %copy-done.11, bf16[304,128]{1,0:T(8,128)(2,1)} %copy-done.10, f32[1,128]{1,0:T(1,128)} %bitcast.17, ...), custom_call_target="tpu_custom_call" | custom-call | flops 1000000 | bytes 1000 | tf_op jit(solution)/shard_map/atoms/pallas_call | solution.py:232
  35.6 0.3 collective-permute-start.5
  35.9 1.0 slice_bitcast_fusion.2
  36.9 8.8 %collective-permute-done.5 = bf16[2,48,768]{2,1,0:T(8,128)(2,1)S(1)} collective-permute-done((bf16[2,48,768]{2,1,0:T(8,128)(2,1)}, bf16[2,48,768]{2,1,0:T(8,128)(2,1)S(1)}, u32[]{:S(2)}, u32[]{:S(2)}) %collective-permute-start.5) | collective-permute-done | bytes 147488 | tf_op jit(solution)/shard_map/ppermute | solution.py:543
  45.7 0.0 copy-start.12
  45.8 0.0 copy-start.2
  45.8 1.2 collective-permute-start.6
  47.1 0.8 collective-permute-start.7
  47.9 3.2 %collective-permute-done.6.refs_2_ = bf16[96,768]{1,0:T(8,128)(2,1)S(1)} collective-permute-done((bf16[96,768]{1,0:T(8,128)(2,1)S(1)}, bf16[96,768]{1,0:T(8,128)(2,1)S(1)}, u32[]{:S(2)}, u32[]{:S(2)}) %collective-permute-start.6) | collective-permute-done | bytes 147488 | tf_op jit(solution)/shard_map/ppermute | solution.py:543
  51.1 1.1 collective-permute-done.7.refs_3_
  52.2 0.1 join.4
  52.3 2.3 %stack.1.near_ref = bf16[4,2,48,1536]{3,2,1,0:T(8,128)(2,1)} custom-call(bf16[2,48,1536]{2,1,0:T(8,128)(2,1)S(1)} %copy-done.5, bf16[2,48,1536]{2,1,0:T(8,128)(2,1)} %collective-permute-done.2.refs_1_, bf16[2,48,1536]{2,1,0:T(8,128)(2,1)} %collective-permute-done.3.refs_2_, bf16[2,48,1536]{2,1,0:T(8,128)(2,1)} %collective-permute-done.4.refs_3_, ...), custom_call_target="tpu_custom_call" | custom-call | flops 1000000 | bytes 1000 | tf_op jit(solution)/shard_map/stack/pallas_call | solution.py:302
  54.6 1.4 %collective-permute-start.10 = (bf16[192,768]{1,0:T(8,128)(2,1)S(1)}, bf16[192,768]{1,0:T(8,128)(2,1)S(1)}, u32[]{:S(2)}, u32[]{:S(2)}) collective-permute-start(bf16[192,768]{1,0:T(8,128)(2,1)S(1)} %get-tuple-element.28.refs_4_.refs_1_), channel_id=1, source_target_pairs={{0,16},{1,17},{2,18},{3,19},{4,20},{5,21},{6,22},{7,23},{8,24},{9,... | collective-permute-start | bytes 884744 | tf_op jit(solution)/shard_map/ppermute | solution.py:543
  56.0 4.0 %collective-permute-start.9 = (bf16[192,768]{1,0:T(8,128)(2,1)S(1)}, bf16[192,768]{1,0:T(8,128)(2,1)S(1)}, u32[]{:S(2)}, u32[]{:S(2)}) collective-permute-start(bf16[192,768]{1,0:T(8,128)(2,1)S(1)} %get-tuple-element.31.refs_0_), channel_id=1, source_target_pairs={{0,4},{1,5},{2,6},{3,7},{4,0},{5,1},{6,2},{7,3},{8,12},{9,13},{10,... | collective-permute-start | bytes 884744 | tf_op jit(solution)/shard_map/ppermute | solution.py:543
  60.0 5.5 %collective-permute-done.10.refs_3_ = bf16[192,768]{1,0:T(8,128)(2,1)S(1)} collective-permute-done((bf16[192,768]{1,0:T(8,128)(2,1)S(1)}, bf16[192,768]{1,0:T(8,128)(2,1)S(1)}, u32[]{:S(2)}, u32[]{:S(2)}) %collective-permute-start.10) | collective-permute-done | bytes 294944 | tf_op jit(solution)/shard_map/ppermute | solution.py:543
  65.5 1.9 %collective-permute-done.9.refs_2_ = bf16[192,768]{1,0:T(8,128)(2,1)S(1)} collective-permute-done((bf16[192,768]{1,0:T(8,128)(2,1)S(1)}, bf16[192,768]{1,0:T(8,128)(2,1)S(1)}, u32[]{:S(2)}, u32[]{:S(2)}) %collective-permute-start.9) | collective-permute-done | bytes 294944 | tf_op jit(solution)/shard_map/ppermute | solution.py:543
  67.4 1.1 join.5
  68.5 2.1 %collective-permute-start.13 = (bf16[384,768]{1,0:T(8,128)(2,1)}, bf16[384,768]{1,0:T(8,128)(2,1)}, u32[]{:S(2)}, u32[]{:S(2)}) collective-permute-start(bf16[384,768]{1,0:T(8,128)(2,1)} %get-tuple-element.32.own0_ref), channel_id=1, source_target_pairs={{0,8},{1,9},{2,10},{3,11},{4,12},{5,13},{6,14},{7,15},{8,16},{9,17... | collective-permute-start | bytes 1769480 | tf_op jit(solution)/shard_map/ppermute | solution.py:539
  70.6 0.1 collective-permute-start.15
  70.7 3.1 %collective-permute-start.16 = (bf16[384,768]{1,0:T(8,128)(2,1)}, bf16[384,768]{1,0:T(8,128)(2,1)}, u32[]{:S(2)}, u32[]{:S(2)}) collective-permute-start(bf16[384,768]{1,0:T(8,128)(2,1)} %get-tuple-element.33.own1_ref), channel_id=1, source_target_pairs={{0,6},{1,7},{2,0},{3,1},{4,2},{5,3},{6,4},{7,5},{8,14},{9,15},{10,... | collective-permute-start | bytes 1769480 | tf_op jit(solution)/shard_map/ppermute | solution.py:539
  73.9 0.9 copy-done.4
  74.8 2.2 %queries.1.absorbed_ref = bf16[2,768,768]{2,1,0:T(8,128)(2,1)S(1)} custom-call(bf16[2,48,768]{2,1,0:T(8,128)(2,1)S(1)} %copy-done.4, bf16[768,768]{1,0:T(8,128)(2,1)S(1)} %copy-done.2, bf16[768,1536]{1,0:T(8,128)(2,1)S(1)} %copy-done), custom_call_target="tpu_custom_call" | custom-call | flops 1000000 | bytes 1000 | tf_op jit(solution)/shard_map/queries/pallas_call | solution.py:277
  77.0 1.6 %collective-permute-start.11 = (bf16[384,768]{1,0:T(8,128)(2,1)}, bf16[384,768]{1,0:T(8,128)(2,1)S(1)}, u32[]{:S(2)}, u32[]{:S(2)}) collective-permute-start(bf16[384,768]{1,0:T(8,128)(2,1)} %get-tuple-element.32.own0_ref), channel_id=1, source_target_pairs={{0,16},{1,17},{2,18},{3,19},{4,20},{5,21},{6,22},{7,23},{8,24},{9,... | collective-permute-start | bytes 1769480 | tf_op jit(solution)/shard_map/ppermute | solution.py:539
  78.6 2.6 %reorder.1 = (bf16[16,48,1536]{2,1,0:T(8,128)(2,1)S(1)}, bf16[16,48,1536]{2,1,0:T(8,128)(2,1)S(1)}) custom-call(bf16[4,2,48,1536]{3,2,1,0:T(8,128)(2,1)} %stack.1.near_ref, bf16[4,2,48,1536]{3,2,1,0:T(8,128)(2,1)} %collective-permute-done.8.far_ref), custom_call_target="tpu_custom_call" | custom-call | flops 2000000000 | bytes 1000 | tf_op jit(solution)/shard_map/reorder/pallas_call | solution.py:335
  81.2 14.9 %collective-permute-done.13.low0_ref = bf16[384,768]{1,0:T(8,128)(2,1)} collective-permute-done((bf16[384,768]{1,0:T(8,128)(2,1)}, bf16[384,768]{1,0:T(8,128)(2,1)}, u32[]{:S(2)}, u32[]{:S(2)}) %collective-permute-start.13) | collective-permute-done | bytes 589856 | tf_op jit(solution)/shard_map/ppermute | solution.py:539
  96.1 2.9 %collective-permute-start.12 = (bf16[384,768]{1,0:T(8,128)(2,1)}, bf16[384,768]{1,0:T(8,128)(2,1)S(1)}, u32[]{:S(2)}, u32[]{:S(2)}) collective-permute-start(bf16[384,768]{1,0:T(8,128)(2,1)} %get-tuple-element.33.own1_ref), channel_id=1, source_target_pairs={{0,4},{1,5},{2,6},{3,7},{4,0},{5,1},{6,2},{7,3},{8,12},{9,13},{10,... | collective-permute-start | bytes 1769480 | tf_op jit(solution)/shard_map/ppermute | solution.py:539
  99.0 0.4 collective-permute-done.14.high0_ref
  99.5 0.0 copy-start.1
  99.5 0.0 copy-start.3
  99.5 0.0 copy-start.7
  99.6 0.0 copy-start.8
  99.6 10.9 %early.1 = (f32[2,768,768]{2,1,0:T(8,128)S(1)}, f32[2,768,128]{2,1,0:T(8,128)S(1)}, f32[2,768,128]{2,1,0:T(8,128)S(1)}) custom-call(bf16[2,768,768]{2,1,0:T(8,128)(2,1)S(1)} %queries.1.absorbed_ref, bf16[16,48,1536]{2,1,0:T(8,128)(2,1)S(1)} %get-tuple-element.29.bias0_ref, bf16[16,48,1536]{2,1,0:T(8,128)(2,1)S(1)} %get-tuple-element.30.bias1_ref, ...), custom_call_target="tpu_custom_call" | custom-call | flops 8000000000 | bytes 1000 | tf_op jit(solution)/shard_map/early/pallas_call | solution.py:400
  110.6 10.5 %late.1 = (bf16[2,384,128]{2,1,0:T(8,128)(2,1)}, bf16[2,48,768]{2,1,0:T(8,128)(2,1)}, bf16[2,48,128]{2,1,0:T(8,128)(2,1)S(1)}) custom-call(bf16[2,768,768]{2,1,0:T(8,128)(2,1)S(1)} %queries.1.absorbed_ref, bf16[16,48,1536]{2,1,0:T(8,128)(2,1)S(1)} %get-tuple-element.29.bias0_ref, bf16[16,48,1536]{2,1,0:T(8,128)(2,1)S(1)} %get-tuple-element.30.bias1_ref, ...), custom_call_target="tpu_custom_call" | custom-call | flops 5000000000 | bytes 1000 | tf_op jit(solution)/shard_map/late/pallas_call | solution.py:513
  121.1 1.9 %collective-permute-start.17 = (bf16[2,128]{1,0:T(2,128)(2,1)S(1)}, bf16[2,128]{1,0:T(2,128)(2,1)S(1)}, u32[]{:S(2)}, u32[]{:S(2)}) collective-permute-start(bf16[2,128]{1,0:T(2,128)(2,1)S(1)} %bitcast.18), channel_id=1, source_target_pairs={{0,1},{1,2},{2,3},{3,4},{4,5},{5,6},{6,7},{7,8},{8,9},{9,10},{10,1... | collective-permute-start | bytes 1544 | tf_op jit(solution)/shard_map/ppermute | solution.py:666
  123.0 0.7 slice_compare_fusion
  123.7 5.8 %collective-permute-done.17 = bf16[2,128]{1,0:T(2,128)(2,1)S(1)} collective-permute-done((bf16[2,128]{1,0:T(2,128)(2,1)S(1)}, bf16[2,128]{1,0:T(2,128)(2,1)S(1)}, u32[]{:S(2)}, u32[]{:S(2)}) %collective-permute-start.17) | collective-permute-done | bytes 544 | tf_op jit(solution)/shard_map/ppermute | solution.py:666
  129.6 1.4 %fusion = bf16[2,384,128]{2,1,0:T(8,128)(2,1)} fusion(bf16[2,384,128]{2,1,0:T(8,128)(2,1)} %get-tuple-element.39, f32[2,128]{1,0:T(2,128)S(1)} %convert_element_type.11, pred[8]{0:T(512)(128)(4,1)S(1)} %slice_compare_fusion), kind=kLoop, calls=%fused_computation.5 | loop fusion | flops 8192 | bytes 9224 | tf_op jit(solution)/shard_map/dynamic_update_slice | solution.py:670
  (39 shorter events, 0.1 us)
Async XLA Ops:
  0.6 51.7 %copy-start.5 = (bf16[2,48,1536]{2,1,0:T(8,128)(2,1)S(1)}, bf16[2,48,1536]{2,1,0:T(8,128)(2,1)}, u32[]{:S(2)}) copy-start(bf16[2,48,1536]{2,1,0:T(8,128)(2,1)} %refs_0_) | copy-start | bytes 884740
  3.0 21.5 %collective-permute-start.1 = (bf16[304,128]{1,0:T(8,128)(2,1)}, bf16[304,128]{1,0:T(8,128)(2,1)S(1)}, u32[]{:S(2)}, u32[]{:S(2)}) collective-permute-start(bf16[304,128]{1,0:T(8,128)(2,1)} %get-tuple-element.23), channel_id=1, source_target_pairs={{1,0},{2,1},{3,2},{4,3},{5,4},{6,5},{7,6},{8,7},{9,8},{10,9},{11,1... | collective-permute-start | bytes 233480 | tf_op jit(solution)/shard_map/ppermute | solution.py:630
  9.5 14.9 %collective-permute-start = (bf16[96,128]{1,0:T(8,128)(2,1)}, bf16[96,128]{1,0:T(8,128)(2,1)S(1)}, u32[]{:S(2)}, u32[]{:S(2)}) collective-permute-start(bf16[96,128]{1,0:T(8,128)(2,1)} %get-tuple-element.22), channel_id=1, source_target_pairs={{0,1},{1,2},{2,3},{3,4},{4,5},{5,6},{6,7},{7,8},{8,9},{9,10},{10,1... | collective-permute-start | bytes 73736 | tf_op jit(solution)/shard_map/ppermute | solution.py:631
  11.5 40.8 %collective-permute-start.2 = (bf16[2,48,1536]{2,1,0:T(8,128)(2,1)}, bf16[2,48,1536]{2,1,0:T(8,128)(2,1)}, u32[]{:S(2)}, u32[]{:S(2)}) collective-permute-start(bf16[2,48,1536]{2,1,0:T(8,128)(2,1)} %refs_0_), channel_id=1, source_target_pairs={{192,0},{224,32},{0,64},{32,96},{64,128},{96,160},{128,192},{160,2... | collective-permute-start | bytes 884744 | tf_op jit(solution)/shard_map/ppermute | solution.py:591
  14.8 37.5 %collective-permute-start.3 = (bf16[2,48,1536]{2,1,0:T(8,128)(2,1)}, bf16[2,48,1536]{2,1,0:T(8,128)(2,1)}, u32[]{:S(2)}, u32[]{:S(2)}) collective-permute-start(bf16[2,48,1536]{2,1,0:T(8,128)(2,1)} %refs_0_), channel_id=1, source_target_pairs={{64,0},{96,32},{128,64},{160,96},{192,128},{224,160},{0,192},{32,2... | collective-permute-start | bytes 884744 | tf_op jit(solution)/shard_map/ppermute | solution.py:591
  17.0 35.2 %collective-permute-start.4 = (bf16[2,48,1536]{2,1,0:T(8,128)(2,1)}, bf16[2,48,1536]{2,1,0:T(8,128)(2,1)}, u32[]{:S(2)}, u32[]{:S(2)}) collective-permute-start(bf16[2,48,1536]{2,1,0:T(8,128)(2,1)} %refs_0_), channel_id=1, source_target_pairs={{128,0},{160,32},{192,64},{224,96},{0,128},{32,160},{64,192},{96,2... | collective-permute-start | bytes 884744 | tf_op jit(solution)/shard_map/ppermute | solution.py:591
  24.5 0.6 copy-start.11
  24.5 0.6 copy-start.10
  35.6 10.1 %collective-permute-start.5 = (bf16[2,48,768]{2,1,0:T(8,128)(2,1)}, bf16[2,48,768]{2,1,0:T(8,128)(2,1)S(1)}, u32[]{:S(2)}, u32[]{:S(2)}) collective-permute-start(bf16[2,48,768]{2,1,0:T(8,128)(2,1)} %get-tuple-element.24.norm_ref), channel_id=1, source_target_pairs={{0,1},{1,0},{2,3},{3,2},{4,5},{5,4},{6,7},{7,6},{8,9},{9,8},{10,11... | collective-permute-start | bytes 442376 | tf_op jit(solution)/shard_map/ppermute | solution.py:543
  45.7 28.1 %copy-start.12 = (f32[768]{0:T(1024)S(1)}, f32[768]{0:T(1024)}, u32[]{:S(2)}) copy-start(f32[768]{0:T(1024)} %param.34) | copy-start | bytes 9220
  45.8 28.1 %copy-start = (bf16[768,1536]{1,0:T(8,128)(2,1)S(1)}, bf16[768,1536]{1,0:T(8,128)(2,1)}, u32[]{:S(2)}) copy-start(bf16[768,1536]{1,0:T(8,128)(2,1)} %keyval_hbm.5) | copy-start | bytes 7077892
  45.8 28.1 %copy-start.2 = (bf16[768,768]{1,0:T(8,128)(2,1)S(1)}, bf16[768,768]{1,0:T(8,128)(2,1)}, u32[]{:S(2)}) copy-start(bf16[768,768]{1,0:T(8,128)(2,1)} %query_hbm.3) | copy-start | bytes 3538948
  45.8 5.2 %collective-permute-start.6 = (bf16[96,768]{1,0:T(8,128)(2,1)S(1)}, bf16[96,768]{1,0:T(8,128)(2,1)S(1)}, u32[]{:S(2)}, u32[]{:S(2)}) collective-permute-start(bf16[96,768]{1,0:T(8,128)(2,1)S(1)} %get-tuple-element.26.refs_0_), channel_id=1, source_target_pairs={{0,2},{1,3},{2,0},{3,1},{4,6},{5,7},{6,4},{7,5},{8,10},{9,11},{10,... | collective-permute-start | bytes 442376 | tf_op jit(solution)/shard_map/ppermute | solution.py:543
  47.1 5.1 %collective-permute-start.7 = (bf16[96,768]{1,0:T(8,128)(2,1)S(1)}, bf16[96,768]{1,0:T(8,128)(2,1)S(1)}, u32[]{:S(2)}, u32[]{:S(2)}) collective-permute-start(bf16[96,768]{1,0:T(8,128)(2,1)S(1)} %get-tuple-element.27.refs_1_), channel_id=1, source_target_pairs={{0,8},{1,9},{2,10},{3,11},{4,12},{5,13},{6,14},{7,15},{8,0},{9,1},... | collective-permute-start | bytes 442376 | tf_op jit(solution)/shard_map/ppermute | solution.py:543
  54.6 22.4 %collective-permute-start.8 = (bf16[4,2,48,1536]{3,2,1,0:T(8,128)(2,1)}, bf16[4,2,48,1536]{3,2,1,0:T(8,128)(2,1)}, u32[]{:S(2)}, u32[]{:S(2)}) collective-permute-start(bf16[4,2,48,1536]{3,2,1,0:T(8,128)(2,1)} %stack.1.near_ref), channel_id=1, source_target_pairs={{0,32},{32,0},{64,96},{96,64},{128,160},{160,128},{192,224},{224,1... | collective-permute-start | bytes 3538952 | tf_op jit(solution)/shard_map/ppermute | solution.py:597
  54.6 10.9 %collective-permute-start.10 = (bf16[192,768]{1,0:T(8,128)(2,1)S(1)}, bf16[192,768]{1,0:T(8,128)(2,1)S(1)}, u32[]{:S(2)}, u32[]{:S(2)}) collective-permute-start(bf16[192,768]{1,0:T(8,128)(2,1)S(1)} %get-tuple-element.28.refs_4_.refs_1_), channel_id=1, source_target_pairs={{0,16},{1,17},{2,18},{3,19},{4,20},{5,21},{6,22},{7,23},{8,24},{9,... | collective-permute-start | bytes 884744 | tf_op jit(solution)/shard_map/ppermute | solution.py:543
  56.0 11.4 %collective-permute-start.9 = (bf16[192,768]{1,0:T(8,128)(2,1)S(1)}, bf16[192,768]{1,0:T(8,128)(2,1)S(1)}, u32[]{:S(2)}, u32[]{:S(2)}) collective-permute-start(bf16[192,768]{1,0:T(8,128)(2,1)S(1)} %get-tuple-element.31.refs_0_), channel_id=1, source_target_pairs={{0,4},{1,5},{2,6},{3,7},{4,0},{5,1},{6,2},{7,3},{8,12},{9,13},{10,... | collective-permute-start | bytes 884744 | tf_op jit(solution)/shard_map/ppermute | solution.py:543
  68.5 27.6 %collective-permute-start.13 = (bf16[384,768]{1,0:T(8,128)(2,1)}, bf16[384,768]{1,0:T(8,128)(2,1)}, u32[]{:S(2)}, u32[]{:S(2)}) collective-permute-start(bf16[384,768]{1,0:T(8,128)(2,1)} %get-tuple-element.32.own0_ref), channel_id=1, source_target_pairs={{0,8},{1,9},{2,10},{3,11},{4,12},{5,13},{6,14},{7,15},{8,16},{9,17... | collective-permute-start | bytes 1769480 | tf_op jit(solution)/shard_map/ppermute | solution.py:539
  70.6 28.8 %collective-permute-start.14 = (bf16[384,768]{1,0:T(8,128)(2,1)}, bf16[384,768]{1,0:T(8,128)(2,1)}, u32[]{:S(2)}, u32[]{:S(2)}) collective-permute-start(bf16[384,768]{1,0:T(8,128)(2,1)} %get-tuple-element.32.own0_ref), channel_id=1, source_target_pairs={{0,24},{1,25},{2,26},{3,27},{4,28},{5,29},{6,30},{7,31},{8,0},{9,1... | collective-permute-start | bytes 1769480 | tf_op jit(solution)/shard_map/ppermute | solution.py:539
  70.6 28.8 %collective-permute-start.15 = (bf16[384,768]{1,0:T(8,128)(2,1)}, bf16[384,768]{1,0:T(8,128)(2,1)}, u32[]{:S(2)}, u32[]{:S(2)}) collective-permute-start(bf16[384,768]{1,0:T(8,128)(2,1)} %get-tuple-element.33.own1_ref), channel_id=1, source_target_pairs={{0,2},{1,3},{2,4},{3,5},{4,6},{5,7},{6,0},{7,1},{8,10},{9,11},{10,... | collective-permute-start | bytes 1769480 | tf_op jit(solution)/shard_map/ppermute | solution.py:539
  70.7 28.8 %collective-permute-start.16 = (bf16[384,768]{1,0:T(8,128)(2,1)}, bf16[384,768]{1,0:T(8,128)(2,1)}, u32[]{:S(2)}, u32[]{:S(2)}) collective-permute-start(bf16[384,768]{1,0:T(8,128)(2,1)} %get-tuple-element.33.own1_ref), channel_id=1, source_target_pairs={{0,6},{1,7},{2,0},{3,1},{4,2},{5,3},{6,4},{7,5},{8,14},{9,15},{10,... | collective-permute-start | bytes 1769480 | tf_op jit(solution)/shard_map/ppermute | solution.py:539
  73.9 0.9 copy-start.4
  77.0 33.5 %collective-permute-start.11 = (bf16[384,768]{1,0:T(8,128)(2,1)}, bf16[384,768]{1,0:T(8,128)(2,1)S(1)}, u32[]{:S(2)}, u32[]{:S(2)}) collective-permute-start(bf16[384,768]{1,0:T(8,128)(2,1)} %get-tuple-element.32.own0_ref), channel_id=1, source_target_pairs={{0,16},{1,17},{2,18},{3,19},{4,20},{5,21},{6,22},{7,23},{8,24},{9,... | collective-permute-start | bytes 1769480 | tf_op jit(solution)/shard_map/ppermute | solution.py:539
  96.1 14.4 %collective-permute-start.12 = (bf16[384,768]{1,0:T(8,128)(2,1)}, bf16[384,768]{1,0:T(8,128)(2,1)S(1)}, u32[]{:S(2)}, u32[]{:S(2)}) collective-permute-start(bf16[384,768]{1,0:T(8,128)(2,1)} %get-tuple-element.33.own1_ref), channel_id=1, source_target_pairs={{0,4},{1,5},{2,6},{3,7},{4,0},{5,1},{6,2},{7,3},{8,12},{9,13},{10,... | collective-permute-start | bytes 1769480 | tf_op jit(solution)/shard_map/ppermute | solution.py:539
  99.5 11.0 %slice-start = ((s8[4718592]{0:T(1024)(128)(4,1)}), s8[4194304]{0:T(1024)(128)(4,1)S(1)}, s32[]{:S(2)}) async-start(s8[4718592]{0:T(1024)(128)(4,1)} %bitcast.13), calls=%async_computation | async-start | bytes 8388608
  99.5 11.0 %slice-start.1 = ((s8[4718592]{0:T(1024)(128)(4,1)}), s8[524288]{0:T(1024)(128)(4,1)S(1)}, s32[]{:S(2)}) async-start(s8[4718592]{0:T(1024)(128)(4,1)} %bitcast.13), calls=%async_computation.1 | async-start | bytes 1048576
  99.5 11.0 %copy-start.1 = (bf16[1536,768]{1,0:T(8,128)(2,1)S(1)}, bf16[1536,768]{1,0:T(8,128)(2,1)}, u32[]{:S(2)}) copy-start(bf16[1536,768]{1,0:T(8,128)(2,1)} %down_hbm.1) | copy-start | bytes 7077892
  99.5 11.0 %copy-start.3 = (bf16[768,768]{1,0:T(8,128)(2,1)S(1)}, bf16[768,768]{1,0:T(8,128)(2,1)}, u32[]{:S(2)}) copy-start(bf16[768,768]{1,0:T(8,128)(2,1)} %output_hbm.3) | copy-start | bytes 3538948
  99.5 11.0 %copy-start.6 = (bf16[768,128]{1,0:T(8,128)(2,1)S(1)}, bf16[768,128]{1,0:T(8,128)(2,1)}, u32[]{:S(2)}) copy-start(bf16[768,128]{1,0:T(8,128)(2,1)} %back_hbm.1) | copy-start | bytes 589828
  99.5 11.0 %copy-start.7 = (bf16[2,384,128]{2,1,0:T(8,128)(2,1)S(1)}, bf16[2,384,128]{2,1,0:T(8,128)(2,1)}, u32[]{:S(2)}) copy-start(bf16[2,384,128]{2,1,0:T(8,128)(2,1)} %get-tuple-element.38.mid_ref) | copy-start | bytes 589828
  99.6 11.0 %copy-start.8 = (bf16[2,48,768]{2,1,0:T(8,128)(2,1)S(1)}, bf16[2,48,768]{2,1,0:T(8,128)(2,1)}, u32[]{:S(2)}) copy-start(bf16[2,48,768]{2,1,0:T(8,128)(2,1)} %get-tuple-element.37.tokact_ref) | copy-start | bytes 442372
  99.6 11.0 %copy-start.9 = (s32[1,384]{1,0:T(1,128)S(1)}, s32[1,384]{1,0:T(1,128)}, u32[]{:S(2)}) copy-start(s32[1,384]{1,0:T(1,128)} %reshape.20.token_ref) | copy-start | bytes 4612
  121.1 8.4 %collective-permute-start.17 = (bf16[2,128]{1,0:T(2,128)(2,1)S(1)}, bf16[2,128]{1,0:T(2,128)(2,1)S(1)}, u32[]{:S(2)}, u32[]{:S(2)}) collective-permute-start(bf16[2,128]{1,0:T(2,128)(2,1)S(1)} %bitcast.18), channel_id=1, source_target_pairs={{0,1},{1,2},{2,3},{3,4},{4,5},{5,6},{6,7},{7,8},{8,9},{9,10},{10,1... | collective-permute-start | bytes 1544 | tf_op jit(solution)/shard_map/ppermute | solution.py:666

commit v5 on v4

--- a/solution.py
+++ b/solution.py
@@ -49,6 +49,10 @@
     centred = widened - jnp.mean(widened, axis=-1, keepdims=True)
     variance = jnp.mean(centred * centred, axis=-1, keepdims=True)
     return (centred * lax.rsqrt(variance + EPSILON) * gain).astype(BF16)
+
+
+def one_row(flat):
+    return jnp.concatenate([flat[i : i + 1] for i in range(flat.shape[0])], axis=1)
 
 
 def lane_group(rows, lanes, width):
@@ -141,6 +145,7 @@
     scale = 1.0 / math.sqrt(head_width)
     device = lax.axis_index("seq")
     gain = gain_ref[...]
+    token_gain = one_row(token_gain_ref[...])
     bias_at = samples * AFTER
     meta_at = bias_at + AH * WQ
 
@@ -153,7 +158,7 @@
     indexf = index.astype(F32)
     valid_after = (indexf >= meta[0:1, :]) & (indexf < meta[1:2, :])
 
-    slot = token_ref[...] - device * tokens
+    slot = one_row(token_ref[...]) - device * tokens
     own_table = (lax.broadcasted_iota(jnp.int32, (tokens, atoms), 0) == slot).astype(F32)
     own_counts = jnp.sum(own_table, axis=1, keepdims=True)
     own_table = own_table.astype(BF16)
@@ -179,10 +184,12 @@
         normed = layer_norm(extended, gain)
         queries = dot(normed, query_ref[...]).astype(BF16)
         keyvals = dot(normed, keyval_ref[...]).astype(BF16)
+        values_ones = jnp.concatenate(
+            [keyvals[:, channels:], jnp.ones((keyvals.shape[0], channels), BF16)], axis=1
+        )
         for w in range(windows + 1):
             q = queries[BEFORE + WQ * w : BEFORE + WQ * (w + 1), :]
             keys = keyvals[WQ * w : WQ * w + WK, :channels]
-            values = keyvals[WQ * w : WQ * w + WK, channels:]
             stacked = jnp.concatenate([q * m for m in masks], axis=0)
             scores = dot_nt(stacked, keys) * scale
             if w < windows:
@@ -194,8 +201,8 @@
                 valid = valid_after
             scores = jnp.where(valid, scores + bias.astype(F32), NEGATIVE)
             exponent = jnp.exp(scores - jnp.max(scores, axis=-1, keepdims=True))
-            total = jnp.sum(exponent, axis=-1, keepdims=True)
-            mixed = dot(exponent.astype(BF16), values) / total
+            sums = dot(exponent.astype(BF16), values_ones[WQ * w : WQ * w + WK])
+            mixed = sums[:, :channels] / sums[:, channels:]
             attended = mixed[:WQ] * masks32[0]
             for h in range(1, AH):
                 attended = attended + mixed[WQ * h : WQ * (h + 1)] * masks32[h]
@@ -210,7 +217,7 @@
         sums = dot(own_table, hidden[:atoms]) + dot(after_table, hidden[atoms:])
         token_act = (sums / counts).astype(BF16)
         tokact_ref[s] = token_act
-        norm_ref[s] = layer_norm(token_act.astype(F32), token_gain_ref[...])
+        norm_ref[s] = layer_norm(token_act.astype(F32), token_gain)
 
 
 def vmem():
@@ -288,26 +295,6 @@
         cost_estimate=cost(1_000_000),
         name="queries",
     )(norm, token_query, token_keyval)
-
-
-def stack_kernel(steps, *refs):
-    column = lax.axis_index("samp") // 2
-    stacked = refs[-1]
-    for step, piece in zip(steps, refs):
-        stacked[(column + step) % len(steps)] = piece[...]
-
-
-def run_stack(pieces, steps, after):
-    count = len(pieces)
-    return pl.pallas_call(
-        functools.partial(stack_kernel, steps),
-        out_shape=jax.ShapeDtypeStruct((count,) + pieces[0].shape, pieces[0].dtype),
-        in_specs=[vmem()] * count + [anywhere()],
-        out_specs=vmem(),
-        compiler_params=pltpu.CompilerParams(vmem_limit_bytes=16 * 2**20),
-        cost_estimate=cost(1_000_000),
-        name="stack",
-    )(*pieces, after)
 
 
 def reorder_kernel(near_ref, far_ref, bias_ref, turned_ref):
@@ -488,7 +475,7 @@
     merged = dot(att_ref[...], output_ref[...])
     token_act = tokact_ref[...].reshape(samples * tokens, width).astype(F32)
     token_mid = (token_act + merged).astype(BF16).astype(F32)
-    trans = layer_norm(token_mid, gain_ref[...])
+    trans = layer_norm(token_mid, one_row(gain_ref[...]))
     weight_copies[2].wait()
     hidden_width = down_ref.shape[0]
     gate = dot(trans, gate_ref[:, :hidden_width])
@@ -501,7 +488,7 @@
     back_rows = dot(token_out, back_ref[...]).astype(BF16)
     back_rows_ref[...] = back_rows.reshape(samples, tokens, -1)
     atoms = mid_ref.shape[1]
-    slot = token_ref[...] - device * tokens
+    slot = one_row(token_ref[...]) - device * tokens
     table = (lax.broadcasted_iota(jnp.int32, (tokens, atoms), 0) == slot).astype(BF16)
     for s in range(samples):
         gathered = dot_tn(table, back_rows[tokens * s : tokens * (s + 1)])
@@ -539,62 +526,56 @@
     return lax.ppermute(value, "seq", pairs)
 
 
-def exchanged(value, bit):
-    return lax.ppermute(value, "seq", [(t, t ^ (1 << bit)) for t in range(32)])
-
-
-def join_kernel(bits, *refs):
+def exchanged(value, axis, bit):
+    return lax.ppermute(value, axis, [(t, t ^ (1 << bit)) for t in range(lax.axis_size(axis))])
+
+
+def join_kernel(axis, bits, *refs):
     count = len(bits)
-    device = lax.axis_index("seq")
-    for i, bit in enumerate(bits):
-        own, other, joined = refs[i], refs[count + i], refs[2 * count + i]
+    device = lax.axis_index(axis)
+    for own, other, joined, bit in zip(refs, refs[count:], refs[-count:], bits):
         rows = joined.shape[0] // 2
         where = (device // (1 << bit)) % 2
-        joined[pl.ds(pl.multiple_of(where * rows, 16), rows)] = own[...].reshape(rows, -1)
-        joined[pl.ds(pl.multiple_of((1 - where) * rows, 16), rows)] = other[...].reshape(rows, -1)
-
-
-def joined(own, other, bits):
+        joined[pl.ds(pl.multiple_of(where * rows, 16), rows)] = own[...]
+        joined[pl.ds(pl.multiple_of((1 - where) * rows, 16), rows)] = other[...]
+
+
+def joined(own, other, axis, bits, after=()):
     rows, width = own[0].shape
     shape = jax.ShapeDtypeStruct((2 * rows, width), BF16)
     return pl.pallas_call(
-        functools.partial(join_kernel, bits),
+        functools.partial(join_kernel, axis, bits),
         out_shape=(shape,) * len(bits),
-        in_specs=[vmem()] * (2 * len(bits)),
+        in_specs=[vmem()] * (2 * len(bits)) + [anywhere()] * len(after),
         out_specs=(vmem(),) * len(bits),
         compiler_params=pltpu.CompilerParams(vmem_limit_bytes=16 * 2**20),
         cost_estimate=cost(1_000_000),
         name="join",
-    )(*own, *other)
+    )(*own, *other, *after)
 
 
 def spread(norm):
-    other = exchanged(norm, 0)
-    lines = joined([norm[0], norm[1]], [other[0], other[1]], (0, 0))
+    other = exchanged(norm, "seq", 0)
+    lines = joined([norm[0], norm[1]], [other[0], other[1]], "seq", (0, 0))
+    steps = [other]
     for bits in ((1, 3), (2, 4)):
-        earlier = lines
-        lines = joined(lines, [exchanged(v, b) for v, b in zip(lines, bits)], bits)
+        lines = joined(lines, [exchanged(v, "seq", b) for v, b in zip(lines, bits)], "seq", bits)
+        steps.append(lines[1])
     near, far = [], []
     for value, dx, dy in ((lines[0], 1, 0), (lines[1], 0, 1)):
-        near.append((value, shifted(value, dx, dy), shifted(value, -dx, -dy)))
-        far.append(shifted(value, 2 * dx, 2 * dy))
-    return near, far, earlier[1]
-
-
-BIAS_STEPS = (0, 3, 1, 2)
-
-
-def column_of(bias):
-    count = lax.axis_size("samp")
-
-    def hop(by):
-        return lax.ppermute(bias, "samp", [((i + 2 * by) % count, i) for i in range(count)])
-
-    return [bias] + [hop(step) for step in BIAS_STEPS[1:]]
-
-
-def other_core(value):
-    return lax.ppermute(value, "samp", [(i, i ^ 1) for i in range(lax.axis_size("samp"))])
+        low = shifted(value, dx, dy)
+        near.append((value, low, shifted(value, -dx, -dy)))
+        far.append(shifted(low, dx, dy))
+    return near, far, steps
+
+
+def all_heads(bias, steps):
+    heads, tokens, keys = bias.shape
+    rows = bias.reshape(heads * tokens, keys)
+    for bit, after in zip((1, 2), (steps[0], steps[-1])):
+        (rows,) = joined([rows], [exchanged(rows, "samp", bit)], "samp", (bit,), (after,))
+    shape = (lax.axis_size("samp") // 2, heads, tokens, keys)
+    return rows.reshape(shape), exchanged(rows, "samp", 0).reshape(shape)
 
 
 def per_device(
@@ -629,8 +610,7 @@
     first, last = run_pack(ranges, atom_act, atom_bias)
     after = lax.ppermute(first, "seq", to_previous)
     before = lax.ppermute(last, "seq", to_next)
-    pieces = column_of(lax.optimization_barrier((pair_bias, first))[0])
-    token_row = atom_token.reshape(1, atoms)
+    token_row = atom_token.reshape(-1, 128)
     atom_mid, token_act, token_norm = run_atoms(
         ranges,
         token_counts,
@@ -638,7 +618,7 @@
         after,
         atom_gain.reshape(1, -1),
         token_row,
-        token_gain.reshape(1, -1),
+        token_gain.reshape(-1, 128),
         atom_act,
         atom_query,
         atom_keyval,
@@ -647,9 +627,8 @@
         gather_weight,
     )
     absorbed = run_queries(token_norm, token_query, token_keyval)
-    near, far, ready = spread(token_norm)
-    bias_near = run_stack(pieces, BIAS_STEPS, ready)
-    bias, turned = run_reorder(bias_near, other_core(bias_near))
+    near, far, steps = spread(token_norm)
+    bias, turned = run_reorder(*all_heads(pair_bias, steps))
     early = run_early(absorbed, bias, turned, near[0] + near[1])
     atom_out, token_out, back_rows = run_late(
         absorbed,
@@ -660,7 +639,7 @@
         token_act,
         atom_mid,
         token_row,
-        trans_gain.reshape(1, -1),
+        trans_gain.reshape(-1, 128),
         [token_keyval, token_output, trans_gate_up, trans_down, back_weight],
     )
     previous = lax.ppermute(back_rows[:, tokens - 1], "seq", to_next)

time: 131 us -> 120 us (0.916); the launches traced: 131 us -> 118 us
  starting transfers between devices: 38.5 us -> 27.5 us
  Pallas kernels: 42.6 us -> 38.5 us
  waiting for transfers between devices: 41.7 us -> 45.7 us
  local copies, waits for them, and re-layouts: 5.09 us -> 3.55 us
    ppermute x9 -> x8, starting transfers between devices: 18.3 us -> 5.35 us  [exchanged(): lax.ppermute(value, axis, [(t, t ^ 1 << bit) for t in range(lax.axis_size...]
    ppermute x1, waiting for transfers between devices: 0.01 us -> 11.8 us  [per_device(): before = lax.ppermute(last, 'seq', to_next)]
    ppermute x6, waiting for transfers between devices: 15.3 us -> 10.3 us  [shifted(): return lax.ppermute(value, 'seq', pairs)]
    ppermute x1, starting transfers between devices: 1.92 us -> 6.92 us  [per_device(): previous = lax.ppermute(back_rows[:, tokens - 1], 'seq', to_next)]
    ppermute x1, waiting for transfers between devices: 5.82 us -> 2.51 us  [per_device(): previous = lax.ppermute(back_rows[:, tokens - 1], 'seq', to_next)]
    ppermute x6, starting transfers between devices: 9.82 us -> 6.75 us  [shifted(): return lax.ppermute(value, 'seq', pairs)]
    pallas_call x1, Pallas kernels: 10.5 us -> 7.63 us  [run_atoms(): pl.pallas_call(atom_kernel, out_shape=(jax.ShapeDtypeStruct((samples, ato...]
    reshape x3 -> x0, local copies, waits for them, and re-layouts: 2.5 us -> none  [the longest x1 1.27 us: per_device(): token_gain.reshape(1, -1)]
  transfers between devices with their start and end apart: 18 -> 17, of which waited for: 8 -> 9; matrix products, arithmetic and copies ran while one was open for 3% -> 1% of each run, Pallas kernels for 21% -> 21%
where the time goes in v5:
time: 120 us; the launch traced here: 118 us
  waiting for transfers between devices  45.7 us (38%)
  Pallas kernels  38.5 us (32%)
  starting transfers between devices  27.5 us (23%)
  local copies, waits for them, and re-layouts  3.55 us (3%)
  other arithmetic  1.36 us (1%)
    ppermute x8, waiting for transfers between devices, exchanged(): lax.ppermute(value, axis, [(t, t ^ 1 << bit) for t in range(lax.axis_size...  21.1 us
    ppermute x1, waiting for transfers between devices, per_device(): before = lax.ppermute(last, 'seq', to_next)  11.8 us
    pallas_call x1, Pallas kernels, run_early(): pl.pallas_call(early_kernel, out_shape=(jax.ShapeDtypeStruct((samples, ro...  10.9 us
    pallas_call x1, Pallas kernels, run_late(): pl.pallas_call(late_kernel, out_shape=(jax.ShapeDtypeStruct(mid.shape, BF...  10.5 us
    ppermute x6, waiting for transfers between devices, shifted(): return lax.ppermute(value, 'seq', pairs)  10.3 us
    pallas_call x1, Pallas kernels, run_atoms(): pl.pallas_call(atom_kernel, out_shape=(jax.ShapeDtypeStruct((samples, ato...  7.63 us
    ppermute x1, starting transfers between devices, per_device(): previous = lax.ppermute(back_rows[:, tokens - 1], 'seq', to_next)  6.92 us
    ppermute x6, starting transfers between devices, shifted(): return lax.ppermute(value, 'seq', pairs)  6.75 us
  transfers between devices with their start and end apart: 17, of which 9 were waited for; matrix products, arithmetic and copies ran while one was open for 1% of the time, Pallas kernels for 21%

profile of v5, /device:TPU:6, one launch (start us, length us, event | category | flops | bytes accessed | tf_op | source)
XLA Modules:
  0.0 117.6 jit_solution(404306643950076088)
XLA Ops:
  0.6 2.2 %pack.1 = (bf16[304,128]{1,0:T(8,128)(2,1)}, bf16[96,128]{1,0:T(8,128)(2,1)}) custom-call(s32[2,12]{1,0:T(2,128)} %bitcast.27, bf16[2,384,128]{2,1,0:T(8,128)(2,1)} %act_hbm.3, bf16[4,12,32,128]{3,2,1,0:T(8,128)(2,1)} %bias_hbm.3), custom_call_target="tpu_custom_call" | custom-call | tf_op jit(solution)/shard_map/pack/pallas_call | solution.py:87
  2.8 6.5 %collective-permute-start.1 = (bf16[304,128]{1,0:T(8,128)(2,1)}, bf16[304,128]{1,0:T(8,128)(2,1)S(1)}, u32[]{:S(2)}, u32[]{:S(2)}) collective-permute-start(bf16[304,128]{1,0:T(8,128)(2,1)} %get-tuple-element.22), channel_id=1, source_target_pairs={{1,0},{2,1},{3,2},{4,3},{5,4},{6,5},{7,6},{8,7},{9,8},{10,9},{11,1... | collective-permute-start | bytes 233480 | tf_op jit(solution)/shard_map/ppermute | solution.py:611
  9.4 3.4 %collective-permute-start.2 = (bf16[96,1536]{1,0:T(8,128)(2,1)}, bf16[96,1536]{1,0:T(8,128)(2,1)S(1)}, u32[]{:S(2)}, u32[]{:S(2)}) collective-permute-start(bf16[96,1536]{1,0:T(8,128)(2,1)} %bitcast.21), channel_id=1, source_target_pairs={{0,64},{32,96},{64,0},{96,32},{128,192},{160,224},{192,128},{224,1... | collective-permute-start | bytes 884744 | tf_op jit(solution)/shard_map/ppermute | solution.py:530
  12.8 1.9 %collective-permute-start = (bf16[96,128]{1,0:T(8,128)(2,1)}, bf16[96,128]{1,0:T(8,128)(2,1)S(1)}, u32[]{:S(2)}, u32[]{:S(2)}) collective-permute-start(bf16[96,128]{1,0:T(8,128)(2,1)} %get-tuple-element.21), channel_id=1, source_target_pairs={{0,1},{1,2},{2,3},{3,4},{4,5},{5,6},{6,7},{7,8},{8,9},{9,10},{10,1... | collective-permute-start | bytes 73736 | tf_op jit(solution)/shard_map/ppermute | solution.py:612
  14.7 11.8 %collective-permute-done.before_ref = bf16[96,128]{1,0:T(8,128)(2,1)S(1)} collective-permute-done((bf16[96,128]{1,0:T(8,128)(2,1)}, bf16[96,128]{1,0:T(8,128)(2,1)S(1)}, u32[]{:S(2)}, u32[]{:S(2)}) %collective-permute-start) | collective-permute-done | bytes 24608 | tf_op jit(solution)/shard_map/ppermute | solution.py:612
  26.5 0.6 copy-done.12
  27.1 0.0 copy-done.11
  27.1 7.6 %atoms.1 = (bf16[2,384,128]{2,1,0:T(8,128)(2,1)}, bf16[2,48,768]{2,1,0:T(8,128)(2,1)}, bf16[2,48,768]{2,1,0:T(8,128)(2,1)}) custom-call(s32[2,12]{1,0:T(2,128)} %bitcast.28, s32[48]{0:T(128)} %count_ref.1, bf16[96,128]{1,0:T(8,128)(2,1)} %copy-done.12, bf16[304,128]{1,0:T(8,128)(2,1)} %copy-done.11, f32[1,128]{1,0:T(1,128)} %bitcast.29, s32[3,128]{1,0:T(4,128)} %bitcast.23, ...), custom_call_target="tpu_custom_call" | custom-call | flops 1000000 | bytes 1000 | tf_op jit(solution)/shard_map/atoms/pallas_call | solution.py:239
  34.7 0.1 collective-permute-start.3
  34.8 1.0 slice_bitcast_fusion.2
  35.8 4.4 %collective-permute-done.3.refs_2_ = bf16[2,48,768]{2,1,0:T(8,128)(2,1)S(1)} collective-permute-done((bf16[2,48,768]{2,1,0:T(8,128)(2,1)}, bf16[2,48,768]{2,1,0:T(8,128)(2,1)S(1)}, u32[]{:S(2)}, u32[]{:S(2)}) %collective-permute-start.3) | collective-permute-done | bytes 147488 | tf_op jit(solution)/shard_map/ppermute | solution.py:530
  40.2 1.0 copy-done.5
  41.1 0.1 join.5.refs_0_
  41.2 0.1 collective-permute-start.4
  41.4 0.1 collective-permute-start.5
  41.5 0.0 copy-start
  41.5 0.0 copy-start.3
  41.5 0.6 collective-permute-start.6
  42.1 5.8 %collective-permute-done.5.refs_2_ = bf16[96,768]{1,0:T(8,128)(2,1)S(1)} collective-permute-done((bf16[96,768]{1,0:T(8,128)(2,1)S(1)}, bf16[96,768]{1,0:T(8,128)(2,1)S(1)}, u32[]{:S(2)}, u32[]{:S(2)}) %collective-permute-start.5) | collective-permute-done | bytes 147488 | tf_op jit(solution)/shard_map/ppermute | solution.py:530
  47.9 0.1 join.7
  48.0 0.1 collective-permute-start.7
  48.1 1.0 collective-permute-start.8
  49.1 7.2 %collective-permute-done.7.refs_2_ = bf16[192,768]{1,0:T(8,128)(2,1)S(1)} collective-permute-done((bf16[192,768]{1,0:T(8,128)(2,1)S(1)}, bf16[192,768]{1,0:T(8,128)(2,1)S(1)}, u32[]{:S(2)}, u32[]{:S(2)}) %collective-permute-start.7) | collective-permute-done | bytes 294944 | tf_op jit(solution)/shard_map/ppermute | solution.py:530
  56.3 0.1 collective-permute-done.8.refs_3_
  56.4 1.1 join.8
  57.6 3.6 %collective-permute-done.4.refs_1_ = bf16[192,1536]{1,0:T(8,128)(2,1)S(1)} collective-permute-done((bf16[192,1536]{1,0:T(8,128)(2,1)S(1)}, bf16[192,1536]{1,0:T(8,128)(2,1)S(1)}, u32[]{:S(2)}, u32[]{:S(2)}) %collective-permute-start.4) | collective-permute-done | bytes 589856 | tf_op jit(solution)/shard_map/ppermute | solution.py:530
  61.1 1.1 join.9
  62.3 2.0 %collective-permute-start.14 = (bf16[384,768]{1,0:T(8,128)(2,1)}, bf16[384,768]{1,0:T(8,128)(2,1)}, u32[]{:S(2)}, u32[]{:S(2)}) collective-permute-start(bf16[384,768]{1,0:T(8,128)(2,1)} %get-tuple-element.31.own0_ref), channel_id=1, source_target_pairs={{0,24},{1,25},{2,26},{3,27},{4,28},{5,29},{6,30},{7,31},{8,0},{9,1... | collective-permute-start | bytes 1769480 | tf_op jit(solution)/shard_map/ppermute | solution.py:526
  64.3 3.2 %collective-permute-start.15 = (bf16[384,768]{1,0:T(8,128)(2,1)}, bf16[384,768]{1,0:T(8,128)(2,1)}, u32[]{:S(2)}, u32[]{:S(2)}) collective-permute-start(bf16[384,768]{1,0:T(8,128)(2,1)} %get-tuple-element.28.refs_2_.own1_ref), channel_id=1, source_target_pairs={{0,6},{1,7},{2,0},{3,1},{4,2},{5,3},{6,4},{7,5},{8,14},{9,15},{10,... | collective-permute-start | bytes 1769480 | tf_op jit(solution)/shard_map/ppermute | solution.py:526
  67.6 0.9 copy-done.4
  68.5 2.2 %queries.1.absorbed_ref = bf16[2,768,768]{2,1,0:T(8,128)(2,1)S(1)} custom-call(bf16[2,48,768]{2,1,0:T(8,128)(2,1)S(1)} %copy-done.4, bf16[768,768]{1,0:T(8,128)(2,1)S(1)} %copy-done.3, bf16[768,1536]{1,0:T(8,128)(2,1)S(1)} %copy-done), custom_call_target="tpu_custom_call" | custom-call | flops 1000000 | bytes 1000 | tf_op jit(solution)/shard_map/queries/pallas_call | solution.py:284
  70.7 7.7 %collective-permute-done.10.low0_ref = bf16[384,768]{1,0:T(8,128)(2,1)} collective-permute-done((bf16[384,768]{1,0:T(8,128)(2,1)}, bf16[384,768]{1,0:T(8,128)(2,1)}, u32[]{:S(2)}, u32[]{:S(2)}) %collective-permute-start.10) | collective-permute-done | bytes 589856 | tf_op jit(solution)/shard_map/ppermute | solution.py:526
  78.3 1.5 %collective-permute-start.11 = (bf16[384,768]{1,0:T(8,128)(2,1)}, bf16[384,768]{1,0:T(8,128)(2,1)S(1)}, u32[]{:S(2)}, u32[]{:S(2)}) collective-permute-start(bf16[384,768]{1,0:T(8,128)(2,1)} %collective-permute-done.10.low0_ref), channel_id=1, source_target_pairs={{0,8},{1,9},{2,10},{3,11},{4,12},{5,13},{6,14},{7,15},{8,16},{9,17... | collective-permute-start | bytes 1769480 | tf_op jit(solution)/shard_map/ppermute | solution.py:526
  79.8 2.7 %reorder.1 = (bf16[16,48,1536]{2,1,0:T(8,128)(2,1)S(1)}, bf16[16,48,1536]{2,1,0:T(8,128)(2,1)S(1)}) custom-call(bf16[4,2,48,1536]{3,2,1,0:T(8,128)(2,1)} %bitcast.9.near_ref, bf16[4,2,48,1536]{3,2,1,0:T(8,128)(2,1)} %bitcast.10.far_ref), custom_call_target="tpu_custom_call" | custom-call | flops 2000000000 | bytes 1000 | tf_op jit(solution)/shard_map/reorder/pallas_call | solution.py:322
  82.5 0.0 slice-start
  82.5 0.0 copy-start.1
  82.6 0.0 copy-start.2
  82.6 0.0 copy-start.6
  82.6 0.0 copy-start.7
  82.6 0.0 copy-start.8
  82.6 0.0 copy-start.9
  82.6 0.0 copy-start.10
  82.6 10.9 %early.1 = (f32[2,768,768]{2,1,0:T(8,128)S(1)}, f32[2,768,128]{2,1,0:T(8,128)S(1)}, f32[2,768,128]{2,1,0:T(8,128)S(1)}) custom-call(bf16[2,768,768]{2,1,0:T(8,128)(2,1)S(1)} %queries.1.absorbed_ref, bf16[16,48,1536]{2,1,0:T(8,128)(2,1)S(1)} %get-tuple-element.29.bias0_ref, bf16[16,48,1536]{2,1,0:T(8,128)(2,1)S(1)} %get-tuple-element.30.bias1_ref, ...), custom_call_target="tpu_custom_call" | custom-call | flops 8000000000 | bytes 1000 | tf_op jit(solution)/shard_map/early/pallas_call | solution.py:387
  93.5 2.6 %collective-permute-done.13.far1_ref = bf16[384,768]{1,0:T(8,128)(2,1)S(1)} collective-permute-done((bf16[384,768]{1,0:T(8,128)(2,1)}, bf16[384,768]{1,0:T(8,128)(2,1)S(1)}, u32[]{:S(2)}, u32[]{:S(2)}) %collective-permute-start.13) | collective-permute-done | bytes 589856 | tf_op jit(solution)/shard_map/ppermute | solution.py:526
  96.2 10.5 %late.1 = (bf16[2,384,128]{2,1,0:T(8,128)(2,1)}, bf16[2,48,768]{2,1,0:T(8,128)(2,1)}, bf16[2,48,128]{2,1,0:T(8,128)(2,1)S(1)}) custom-call(bf16[2,768,768]{2,1,0:T(8,128)(2,1)S(1)} %queries.1.absorbed_ref, bf16[16,48,1536]{2,1,0:T(8,128)(2,1)S(1)} %get-tuple-element.29.bias0_ref, bf16[16,48,1536]{2,1,0:T(8,128)(2,1)S(1)} %get-tuple-element.30.bias1_ref, ...), custom_call_target="tpu_custom_call" | custom-call | flops 5000000000 | bytes 1000 | tf_op jit(solution)/shard_map/late/pallas_call | solution.py:500
  106.7 6.9 %collective-permute-start.16 = (bf16[2,128]{1,0:T(2,128)(2,1)S(1)}, bf16[2,128]{1,0:T(2,128)(2,1)S(1)}, u32[]{:S(2)}, u32[]{:S(2)}) collective-permute-start(bf16[2,128]{1,0:T(2,128)(2,1)S(1)} %bitcast.30), channel_id=1, source_target_pairs={{0,1},{1,2},{2,3},{3,4},{4,5},{5,6},{6,7},{7,8},{8,9},{9,10},{10,1... | collective-permute-start | bytes 1544 | tf_op jit(solution)/shard_map/ppermute | solution.py:645
  113.7 2.5 %collective-permute-done.16 = bf16[2,128]{1,0:T(2,128)(2,1)S(1)} collective-permute-done((bf16[2,128]{1,0:T(2,128)(2,1)S(1)}, bf16[2,128]{1,0:T(2,128)(2,1)S(1)}, u32[]{:S(2)}, u32[]{:S(2)}) %collective-permute-start.16) | collective-permute-done | bytes 544 | tf_op jit(solution)/shard_map/ppermute | solution.py:645
  116.2 1.4 %fusion = bf16[2,384,128]{2,1,0:T(8,128)(2,1)} fusion(bf16[2,384,128]{2,1,0:T(8,128)(2,1)} %get-tuple-element.37, f32[2,128]{1,0:T(2,128)S(1)} %convert_element_type.11, pred[8]{0:T(512)(128)(4,1)S(1)} %slice_compare_fusion), kind=kLoop, calls=%fused_computation.5 | loop fusion | flops 8192 | bytes 9224 | tf_op jit(solution)/shard_map/dynamic_update_slice | solution.py:649
  (35 shorter events, 0.1 us)
Async XLA Ops:
  2.8 23.6 %collective-permute-start.1 = (bf16[304,128]{1,0:T(8,128)(2,1)}, bf16[304,128]{1,0:T(8,128)(2,1)S(1)}, u32[]{:S(2)}, u32[]{:S(2)}) collective-permute-start(bf16[304,128]{1,0:T(8,128)(2,1)} %get-tuple-element.22), channel_id=1, source_target_pairs={{1,0},{2,1},{3,2},{4,3},{5,4},{6,5},{7,6},{8,7},{9,8},{10,9},{11,1... | collective-permute-start | bytes 233480 | tf_op jit(solution)/shard_map/ppermute | solution.py:611
  9.4 30.8 %collective-permute-start.2 = (bf16[96,1536]{1,0:T(8,128)(2,1)}, bf16[96,1536]{1,0:T(8,128)(2,1)S(1)}, u32[]{:S(2)}, u32[]{:S(2)}) collective-permute-start(bf16[96,1536]{1,0:T(8,128)(2,1)} %bitcast.21), channel_id=1, source_target_pairs={{0,64},{32,96},{64,0},{96,32},{128,192},{160,224},{192,128},{224,1... | collective-permute-start | bytes 884744 | tf_op jit(solution)/shard_map/ppermute | solution.py:530
  12.8 13.7 %collective-permute-start = (bf16[96,128]{1,0:T(8,128)(2,1)}, bf16[96,128]{1,0:T(8,128)(2,1)S(1)}, u32[]{:S(2)}, u32[]{:S(2)}) collective-permute-start(bf16[96,128]{1,0:T(8,128)(2,1)} %get-tuple-element.21), channel_id=1, source_target_pairs={{0,1},{1,2},{2,3},{3,4},{4,5},{5,6},{6,7},{7,8},{8,9},{9,10},{10,1... | collective-permute-start | bytes 73736 | tf_op jit(solution)/shard_map/ppermute | solution.py:612
  26.5 0.6 copy-start.12
  26.5 0.6 copy-start.11
  34.7 5.4 %collective-permute-start.3 = (bf16[2,48,768]{2,1,0:T(8,128)(2,1)}, bf16[2,48,768]{2,1,0:T(8,128)(2,1)S(1)}, u32[]{:S(2)}, u32[]{:S(2)}) collective-permute-start(bf16[2,48,768]{2,1,0:T(8,128)(2,1)} %get-tuple-element.23.norm_ref), channel_id=1, source_target_pairs={{0,1},{1,0},{2,3},{3,2},{4,5},{5,4},{6,7},{7,6},{8,9},{9,8},{10,11... | collective-permute-start | bytes 442376 | tf_op jit(solution)/shard_map/ppermute | solution.py:530
  40.2 1.0 copy-start.5
  41.2 19.9 %collective-permute-start.4 = (bf16[192,1536]{1,0:T(8,128)(2,1)S(1)}, bf16[192,1536]{1,0:T(8,128)(2,1)S(1)}, u32[]{:S(2)}, u32[]{:S(2)}) collective-permute-start(bf16[192,1536]{1,0:T(8,128)(2,1)S(1)} %join.5.refs_0_), channel_id=1, source_target_pairs={{0,128},{32,160},{64,192},{96,224},{128,0},{160,32},{192,64},{224,... | collective-permute-start | bytes 1769480 | tf_op jit(solution)/shard_map/ppermute | solution.py:530
  41.4 6.6 %collective-permute-start.5 = (bf16[96,768]{1,0:T(8,128)(2,1)S(1)}, bf16[96,768]{1,0:T(8,128)(2,1)S(1)}, u32[]{:S(2)}, u32[]{:S(2)}) collective-permute-start(bf16[96,768]{1,0:T(8,128)(2,1)S(1)} %get-tuple-element.24.refs_0_), channel_id=1, source_target_pairs={{0,2},{1,3},{2,0},{3,1},{4,6},{5,7},{6,4},{7,5},{8,10},{9,11},{10,... | collective-permute-start | bytes 442376 | tf_op jit(solution)/shard_map/ppermute | solution.py:530
  41.5 26.1 %copy-start = (bf16[768,1536]{1,0:T(8,128)(2,1)S(1)}, bf16[768,1536]{1,0:T(8,128)(2,1)}, u32[]{:S(2)}) copy-start(bf16[768,1536]{1,0:T(8,128)(2,1)} %keyval_hbm.5) | copy-start | bytes 7077892
  41.5 26.1 %copy-start.3 = (bf16[768,768]{1,0:T(8,128)(2,1)S(1)}, bf16[768,768]{1,0:T(8,128)(2,1)}, u32[]{:S(2)}) copy-start(bf16[768,768]{1,0:T(8,128)(2,1)} %query_hbm.3) | copy-start | bytes 3538948
  41.5 6.5 %collective-permute-start.6 = (bf16[96,768]{1,0:T(8,128)(2,1)S(1)}, bf16[96,768]{1,0:T(8,128)(2,1)S(1)}, u32[]{:S(2)}, u32[]{:S(2)}) collective-permute-start(bf16[96,768]{1,0:T(8,128)(2,1)S(1)} %get-tuple-element.25.refs_1_), channel_id=1, source_target_pairs={{0,8},{1,9},{2,10},{3,11},{4,12},{5,13},{6,14},{7,15},{8,0},{9,1},... | collective-permute-start | bytes 442376 | tf_op jit(solution)/shard_map/ppermute | solution.py:530
  48.0 8.3 %collective-permute-start.7 = (bf16[192,768]{1,0:T(8,128)(2,1)S(1)}, bf16[192,768]{1,0:T(8,128)(2,1)S(1)}, u32[]{:S(2)}, u32[]{:S(2)}) collective-permute-start(bf16[192,768]{1,0:T(8,128)(2,1)S(1)} %get-tuple-element.26.refs_0_), channel_id=1, source_target_pairs={{0,4},{1,5},{2,6},{3,7},{4,0},{5,1},{6,2},{7,3},{8,12},{9,13},{10,... | collective-permute-start | bytes 884744 | tf_op jit(solution)/shard_map/ppermute | solution.py:530
  48.1 8.3 %collective-permute-start.8 = (bf16[192,768]{1,0:T(8,128)(2,1)S(1)}, bf16[192,768]{1,0:T(8,128)(2,1)S(1)}, u32[]{:S(2)}, u32[]{:S(2)}) collective-permute-start(bf16[192,768]{1,0:T(8,128)(2,1)S(1)} %get-tuple-element.27.refs_1_), channel_id=1, source_target_pairs={{0,16},{1,17},{2,18},{3,19},{4,20},{5,21},{6,22},{7,23},{8,24},{9,... | collective-permute-start | bytes 884744 | tf_op jit(solution)/shard_map/ppermute | solution.py:530
  62.3 17.6 %collective-permute-start.9 = (bf16[384,1536]{1,0:T(8,128)(2,1)}, bf16[384,1536]{1,0:T(8,128)(2,1)}, u32[]{:S(2)}, u32[]{:S(2)}) collective-permute-start(bf16[384,1536]{1,0:T(8,128)(2,1)} %join.9), channel_id=1, source_target_pairs={{0,32},{32,0},{64,96},{96,64},{128,160},{160,128},{192,224},{224,1... | collective-permute-start | bytes 3538952 | tf_op jit(solution)/shard_map/ppermute | solution.py:530
  62.3 16.1 %collective-permute-start.10 = (bf16[384,768]{1,0:T(8,128)(2,1)}, bf16[384,768]{1,0:T(8,128)(2,1)}, u32[]{:S(2)}, u32[]{:S(2)}) collective-permute-start(bf16[384,768]{1,0:T(8,128)(2,1)} %get-tuple-element.31.own0_ref), channel_id=1, source_target_pairs={{0,8},{1,9},{2,10},{3,11},{4,12},{5,13},{6,14},{7,15},{8,16},{9,17... | collective-permute-start | bytes 1769480 | tf_op jit(solution)/shard_map/ppermute | solution.py:526
  62.3 17.6 %collective-permute-start.12 = (bf16[384,768]{1,0:T(8,128)(2,1)}, bf16[384,768]{1,0:T(8,128)(2,1)}, u32[]{:S(2)}, u32[]{:S(2)}) collective-permute-start(bf16[384,768]{1,0:T(8,128)(2,1)} %get-tuple-element.28.refs_2_.own1_ref), channel_id=1, source_target_pairs={{0,2},{1,3},{2,4},{3,5},{4,6},{5,7},{6,0},{7,1},{8,10},{9,11},{10,... | collective-permute-start | bytes 1769480 | tf_op jit(solution)/shard_map/ppermute | solution.py:526
  62.3 20.2 %collective-permute-start.14 = (bf16[384,768]{1,0:T(8,128)(2,1)}, bf16[384,768]{1,0:T(8,128)(2,1)}, u32[]{:S(2)}, u32[]{:S(2)}) collective-permute-start(bf16[384,768]{1,0:T(8,128)(2,1)} %get-tuple-element.31.own0_ref), channel_id=1, source_target_pairs={{0,24},{1,25},{2,26},{3,27},{4,28},{5,29},{6,30},{7,31},{8,0},{9,1... | collective-permute-start | bytes 1769480 | tf_op jit(solution)/shard_map/ppermute | solution.py:526
  64.3 18.2 %collective-permute-start.15 = (bf16[384,768]{1,0:T(8,128)(2,1)}, bf16[384,768]{1,0:T(8,128)(2,1)}, u32[]{:S(2)}, u32[]{:S(2)}) collective-permute-start(bf16[384,768]{1,0:T(8,128)(2,1)} %get-tuple-element.28.refs_2_.own1_ref), channel_id=1, source_target_pairs={{0,6},{1,7},{2,0},{3,1},{4,2},{5,3},{6,4},{7,5},{8,14},{9,15},{10,... | collective-permute-start | bytes 1769480 | tf_op jit(solution)/shard_map/ppermute | solution.py:526
  67.5 0.9 copy-start.4
  78.3 15.2 %collective-permute-start.11 = (bf16[384,768]{1,0:T(8,128)(2,1)}, bf16[384,768]{1,0:T(8,128)(2,1)S(1)}, u32[]{:S(2)}, u32[]{:S(2)}) collective-permute-start(bf16[384,768]{1,0:T(8,128)(2,1)} %collective-permute-done.10.low0_ref), channel_id=1, source_target_pairs={{0,8},{1,9},{2,10},{3,11},{4,12},{5,13},{6,14},{7,15},{8,16},{9,17... | collective-permute-start | bytes 1769480 | tf_op jit(solution)/shard_map/ppermute | solution.py:526
  79.8 16.3 %collective-permute-start.13 = (bf16[384,768]{1,0:T(8,128)(2,1)}, bf16[384,768]{1,0:T(8,128)(2,1)S(1)}, u32[]{:S(2)}, u32[]{:S(2)}) collective-permute-start(bf16[384,768]{1,0:T(8,128)(2,1)} %collective-permute-done.12.low1_ref), channel_id=1, source_target_pairs={{0,2},{1,3},{2,4},{3,5},{4,6},{5,7},{6,0},{7,1},{8,10},{9,11},{10,... | collective-permute-start | bytes 1769480 | tf_op jit(solution)/shard_map/ppermute | solution.py:526
  82.5 13.6 %slice-start = ((s8[4718592]{0:T(1024)(128)(4,1)}), s8[4194304]{0:T(1024)(128)(4,1)S(1)}, s32[]{:S(2)}) async-start(s8[4718592]{0:T(1024)(128)(4,1)} %bitcast.19), calls=%async_computation | async-start | bytes 8388608
  82.5 13.6 %slice-start.1 = ((s8[4718592]{0:T(1024)(128)(4,1)}), s8[524288]{0:T(1024)(128)(4,1)S(1)}, s32[]{:S(2)}) async-start(s8[4718592]{0:T(1024)(128)(4,1)} %bitcast.19), calls=%async_computation.1 | async-start | bytes 1048576
  82.5 13.6 %copy-start.1 = (bf16[1536,768]{1,0:T(8,128)(2,1)S(1)}, bf16[1536,768]{1,0:T(8,128)(2,1)}, u32[]{:S(2)}) copy-start(bf16[1536,768]{1,0:T(8,128)(2,1)} %down_hbm.1) | copy-start | bytes 7077892
  82.6 13.6 %copy-start.2 = (bf16[768,768]{1,0:T(8,128)(2,1)S(1)}, bf16[768,768]{1,0:T(8,128)(2,1)}, u32[]{:S(2)}) copy-start(bf16[768,768]{1,0:T(8,128)(2,1)} %output_hbm.3) | copy-start | bytes 3538948
  82.6 13.6 %copy-start.6 = (bf16[768,128]{1,0:T(8,128)(2,1)S(1)}, bf16[768,128]{1,0:T(8,128)(2,1)}, u32[]{:S(2)}) copy-start(bf16[768,128]{1,0:T(8,128)(2,1)} %back_hbm.1) | copy-start | bytes 589828
  82.6 13.6 %copy-start.7 = (bf16[2,384,128]{2,1,0:T(8,128)(2,1)S(1)}, bf16[2,384,128]{2,1,0:T(8,128)(2,1)}, u32[]{:S(2)}) copy-start(bf16[2,384,128]{2,1,0:T(8,128)(2,1)} %get-tuple-element.36.mid_ref) | copy-start | bytes 589828
  82.6 13.6 %copy-start.8 = (bf16[2,48,768]{2,1,0:T(8,128)(2,1)S(1)}, bf16[2,48,768]{2,1,0:T(8,128)(2,1)}, u32[]{:S(2)}) copy-start(bf16[2,48,768]{2,1,0:T(8,128)(2,1)} %get-tuple-element.35.tokact_ref) | copy-start | bytes 442372
  82.6 13.6 %copy-start.9 = (s32[384]{0:T(512)S(1)}, s32[384]{0:T(512)}, u32[]{:S(2)}) copy-start(s32[384]{0:T(512)} %param.26) | copy-start | bytes 4612
  82.6 13.6 %copy-start.10 = (f32[768]{0:T(1024)S(1)}, f32[768]{0:T(1024)}, u32[]{:S(2)}) copy-start(f32[768]{0:T(1024)} %param.34) | copy-start | bytes 9220
  106.7 9.5 %collective-permute-start.16 = (bf16[2,128]{1,0:T(2,128)(2,1)S(1)}, bf16[2,128]{1,0:T(2,128)(2,1)S(1)}, u32[]{:S(2)}, u32[]{:S(2)}) collective-permute-start(bf16[2,128]{1,0:T(2,128)(2,1)S(1)} %bitcast.30), channel_id=1, source_target_pairs={{0,1},{1,2},{2,3},{3,4},{4,5},{5,6},{6,7},{7,8},{8,9},{9,10},{10,1... | collective-permute-start | bytes 1544 | tf_op jit(solution)/shard_map/ppermute | solution.py:645

commit v6 on v5

--- a/solution.py
+++ b/solution.py
@@ -256,26 +256,20 @@
     )(key_range, counts, before, after, gain, token, token_gain, *arrays)
 
 
-def query_kernel(norm_ref, query_hbm, keyval_hbm, absorbed_ref, query_ref, key_ref, sems):
+def query_kernel(norm_ref, query_ref, keyval_ref, absorbed_ref):
     samples, tokens, width = norm_ref.shape
-    first = pltpu.make_async_copy(query_hbm, query_ref, sems.at[0])
-    second = pltpu.make_async_copy(keyval_hbm.at[:, :width], key_ref, sems.at[1])
-    first.start()
-    second.start()
     head_size = width // HEADS
     scale = 1.0 / math.sqrt(head_size)
     lanes = GROUP * head_size
     head_of = lane_group(tokens, lanes, head_size)
     masks = [(head_of == h).astype(BF16) for h in range(GROUP)]
-    first.wait()
     queries = dot(norm_ref[...].reshape(samples * tokens, width), query_ref[...]).astype(BF16)
-    second.wait()
     for s in range(samples):
         for g in range(HEADS // GROUP):
             columns = slice(lanes * g, lanes * (g + 1))
             q = queries[tokens * s : tokens * (s + 1), columns]
             stacked = jnp.concatenate([q * m for m in masks], axis=0)
-            absorbed = dot_nt(stacked, key_ref[:, columns]) * scale
+            absorbed = dot_nt(stacked, keyval_ref[:, columns]) * scale
             absorbed_ref[s, lanes * g : lanes * (g + 1)] = absorbed.astype(BF16)
 
 
@@ -284,14 +278,9 @@
     return pl.pallas_call(
         query_kernel,
         out_shape=jax.ShapeDtypeStruct((samples, HEADS * tokens, width), BF16),
-        in_specs=[vmem(), anywhere(), anywhere()],
+        in_specs=[vmem()] * 3,
         out_specs=vmem(),
-        scratch_shapes=[
-            pltpu.VMEM((width, width), BF16),
-            pltpu.VMEM((width, width), BF16),
-            pltpu.SemaphoreType.DMA((2,)),
-        ],
-        compiler_params=pltpu.CompilerParams(vmem_limit_bytes=30 * 2**20),
+        compiler_params=pltpu.CompilerParams(vmem_limit_bytes=16 * 2**20),
         cost_estimate=cost(1_000_000),
         name="queries",
     )(norm, token_query, token_keyval)
@@ -393,7 +382,7 @@
         ),
         in_specs=[vmem()] * (3 + len(pieces)),
         out_specs=(vmem(),) * 3,
-        compiler_params=pltpu.CompilerParams(vmem_limit_bytes=26 * 2**20),
+        compiler_params=pltpu.CompilerParams(vmem_limit_bytes=18 * 2**20),
         cost_estimate=cost(8_000_000_000),
         name="early",
     )(absorbed, bias0, bias1, *pieces)
@@ -412,39 +401,19 @@
     mid_ref,
     token_ref,
     gain_ref,
-    keyval_hbm,
-    output_hbm,
-    gate_hbm,
-    down_hbm,
-    back_hbm,
-    atom_out_ref,
-    token_out_ref,
-    back_rows_ref,
-    value_ref,
+    keyval_ref,
     output_ref,
     gate_ref,
     down_ref,
     back_ref,
+    atom_out_ref,
+    token_out_ref,
+    back_rows_ref,
     att_ref,
-    weight_sems,
 ):
     samples, tokens, width = tokact_ref.shape
     head_size = width // HEADS
     device = lax.axis_index("seq")
-    weight_copies = []
-    for i, (source, target) in enumerate(
-        (
-            (keyval_hbm.at[:, width:], value_ref),
-            (output_hbm, output_ref),
-            (gate_hbm, gate_ref),
-            (down_hbm, down_ref),
-            (back_hbm, back_ref),
-        )
-    ):
-        copy = pltpu.make_async_copy(source, target, weight_sems.at[i])
-        copy.start()
-        weight_copies.append(copy)
-
     lanes = GROUP * head_size
     head_of = lane_group(tokens, lanes, head_size)
     masks32 = [(head_of == h).astype(F32) for h in range(GROUP)]
@@ -463,28 +432,23 @@
             )
             mixed = mixed_ref[s, columns] * shrink + dot(exponent.astype(BF16), piece)
             mixed = mixed / total
-            if s == 0 and g == 0:
-                weight_copies[0].wait()
-            valued = dot(mixed.astype(BF16), value_ref[:, columns])
+            value_at = slice(width + lanes * g, width + lanes * (g + 1))
+            valued = dot(mixed.astype(BF16), keyval_ref[:, value_at])
             attended = valued[:tokens] * masks32[0]
             for h in range(1, GROUP):
                 attended = attended + valued[tokens * h : tokens * (h + 1)] * masks32[h]
             att_ref[tokens * s : tokens * (s + 1), columns] = attended.astype(BF16)
 
-    weight_copies[1].wait()
     merged = dot(att_ref[...], output_ref[...])
     token_act = tokact_ref[...].reshape(samples * tokens, width).astype(F32)
     token_mid = (token_act + merged).astype(BF16).astype(F32)
     trans = layer_norm(token_mid, one_row(gain_ref[...]))
-    weight_copies[2].wait()
     hidden_width = down_ref.shape[0]
     gate = dot(trans, gate_ref[:, :hidden_width])
     up = dot(trans, gate_ref[:, hidden_width:])
     hidden = (gate / (1.0 + jnp.exp(-gate)) * up).astype(BF16)
-    weight_copies[3].wait()
     token_out = (token_mid + dot(hidden, down_ref[...])).astype(BF16)
     token_out_ref[...] = token_out.reshape(samples, tokens, width)
-    weight_copies[4].wait()
     back_rows = dot(token_out, back_ref[...]).astype(BF16)
     back_rows_ref[...] = back_rows.reshape(samples, tokens, -1)
     atoms = mid_ref.shape[1]
@@ -504,15 +468,10 @@
             jax.ShapeDtypeStruct(tokact.shape, BF16),
             jax.ShapeDtypeStruct((samples, tokens, mid.shape[2]), BF16),
         ),
-        in_specs=[vmem()] * 12 + [anywhere()] * 5,
+        in_specs=[vmem()] * 17,
         out_specs=(vmem(),) * 3,
-        scratch_shapes=[pltpu.VMEM((width, width), BF16)]
-        + [pltpu.VMEM(w.shape, w.dtype) for w in weights[1:]]
-        + [
-            pltpu.VMEM((samples * tokens, width), BF16),
-            pltpu.SemaphoreType.DMA((len(weights),)),
-        ],
-        compiler_params=pltpu.CompilerParams(vmem_limit_bytes=28 * 2**20),
+        scratch_shapes=[pltpu.VMEM((samples * tokens, width), BF16)],
+        compiler_params=pltpu.CompilerParams(vmem_limit_bytes=18 * 2**20),
         cost_estimate=cost(5_000_000_000),
         name="late",
     )(absorbed, bias0, bias1, *far, *early, tokact, mid, token, gain, *weights)
@@ -554,25 +513,78 @@
     )(*own, *other, *after)
 
 
+STEPS = (0, 3, 1, 2)
+
+
+def line_kernel(*refs):
+    count = 2 * len(STEPS)
+    device = lax.axis_index("seq")
+    for s, line in enumerate(refs[count:]):
+        at = place(device, s + 1)
+        for step, piece in zip(STEPS, refs[len(STEPS) * s :]):
+            rows = piece.shape[0]
+            start = pl.multiple_of((at + step) % 4 * rows, 16)
+            line[pl.ds(start, rows)] = piece[...]
+
+
+def lines_of(first, second):
+    rows, width = first[0].shape
+    shape = jax.ShapeDtypeStruct((4 * rows, width), BF16)
+    return pl.pallas_call(
+        line_kernel,
+        out_shape=(shape, shape),
+        in_specs=[vmem()] * 8,
+        out_specs=(vmem(),) * 2,
+        compiler_params=pltpu.CompilerParams(vmem_limit_bytes=16 * 2**20),
+        cost_estimate=cost(1_000_000),
+        name="lines",
+    )(*first, *second)
+
+
+def pair_kernel(own_ref, other_ref, first_ref, second_ref):
+    rows = own_ref.shape[1]
+    where = lax.axis_index("seq") % 2
+    for s, pair in enumerate((first_ref, second_ref)):
+        pair[pl.ds(pl.multiple_of(where * rows, 16), rows)] = own_ref[s]
+        pair[pl.ds(pl.multiple_of((1 - where) * rows, 16), rows)] = other_ref[s]
+
+
+def pairs_of(own, other):
+    _, rows, width = own.shape
+    shape = jax.ShapeDtypeStruct((2 * rows, width), BF16)
+    return pl.pallas_call(
+        pair_kernel,
+        out_shape=(shape, shape),
+        in_specs=[vmem()] * 2,
+        out_specs=(vmem(),) * 2,
+        compiler_params=pltpu.CompilerParams(vmem_limit_bytes=16 * 2**20),
+        cost_estimate=cost(1_000_000),
+        name="pairs",
+    )(own, other)
+
+
 def spread(norm):
     other = exchanged(norm, "seq", 0)
-    lines = joined([norm[0], norm[1]], [other[0], other[1]], "seq", (0, 0))
-    steps = [other]
-    for bits in ((1, 3), (2, 4)):
-        lines = joined(lines, [exchanged(v, "seq", b) for v, b in zip(lines, bits)], "seq", bits)
-        steps.append(lines[1])
+    pairs = pairs_of(norm, other)
+    around = []
+    for value, dx, dy in ((pairs[0], 0, 1), (pairs[1], 1, 0)):
+        around.append(
+            [value]
+            + [shifted(value, by * dx, by * dy) for by in (1, -1, 2)]
+        )
+    lines = lines_of(*around)
     near, far = [], []
     for value, dx, dy in ((lines[0], 1, 0), (lines[1], 0, 1)):
         low = shifted(value, dx, dy)
         near.append((value, low, shifted(value, -dx, -dy)))
         far.append(shifted(low, dx, dy))
-    return near, far, steps
+    return near, far, other
 
 
 def all_heads(bias, steps):
     heads, tokens, keys = bias.shape
     rows = bias.reshape(heads * tokens, keys)
-    for bit, after in zip((1, 2), (steps[0], steps[-1])):
+    for bit, after in zip((1, 2), steps):
         (rows,) = joined([rows], [exchanged(rows, "samp", bit)], "samp", (bit,), (after,))
     shape = (lax.axis_size("samp") // 2, heads, tokens, keys)
     return rows.reshape(shape), exchanged(rows, "samp", 0).reshape(shape)
@@ -627,8 +639,8 @@
         gather_weight,
     )
     absorbed = run_queries(token_norm, token_query, token_keyval)
-    near, far, steps = spread(token_norm)
-    bias, turned = run_reorder(*all_heads(pair_bias, steps))
+    near, far, ready = spread(token_norm)
+    bias, turned = run_reorder(*all_heads(pair_bias, (ready, near[1][0])))
     early = run_early(absorbed, bias, turned, near[0] + near[1])
     atom_out, token_out, back_rows = run_late(
         absorbed,

time: 120 us -> 125 us (1.042)
  starting transfers between devices: 27.5 us -> 46.9 us
  waiting for transfers between devices: 45.7 us -> 34.7 us
  Pallas kernels: 38.5 us -> 36.4 us
    ppermute x6 -> x12, starting transfers between devices: 6.75 us -> 26.7 us  [shifted(): return lax.ppermute(value, 'seq', pairs)]
    ppermute x8 -> x4, waiting for transfers between devices: 21.1 us -> 5.35 us  [exchanged(): lax.ppermute(value, axis, [(t, t ^ 1 << bit) for t in range(lax.axis_size...]
    ppermute x6 -> x12, waiting for transfers between devices: 10.3 us -> 15.8 us  [shifted(): return lax.ppermute(value, 'seq', pairs)]
    ppermute x1, starting transfers between devices: 6.92 us -> 1.92 us  [per_device(): previous = lax.ppermute(back_rows[:, tokens - 1], 'seq', to_next)]
    ppermute x1, waiting for transfers between devices: 11.8 us -> 7.01 us  [per_device(): before = lax.ppermute(last, 'seq', to_next)]
    ppermute x8 -> x4, starting transfers between devices: 5.35 us -> 9.8 us  [exchanged(): lax.ppermute(value, axis, [(t, t ^ 1 << bit) for t in range(lax.axis_size...]
    ppermute x1, waiting for transfers between devices: 2.51 us -> 6.5 us  [per_device(): previous = lax.ppermute(back_rows[:, tokens - 1], 'seq', to_next)]
    pallas_call x1, Pallas kernels: 10.5 us -> 8.97 us  [run_late(): pl.pallas_call(late_kernel, out_shape=(jax.ShapeDtypeStruct(mid.shape, BF...]
  transfers between devices with their start and end apart: 17 -> 19, of which waited for: 9 -> 9; matrix products, arithmetic and copies ran while one was open for 1% -> 0% of each run, Pallas kernels for 21% -> 21%
where the time goes in v6:
time: 125 us; the launch traced here: 124 us
  starting transfers between devices  46.9 us (38%)
  Pallas kernels  36.4 us (29%)
  waiting for transfers between devices  34.7 us (28%)
  local copies, waits for them, and re-layouts  3.49 us (3%)
  other arithmetic  1.36 us (1%)
    ppermute x12, starting transfers between devices, shifted(): return lax.ppermute(value, 'seq', pairs)  26.7 us
    ppermute x12, waiting for transfers between devices, shifted(): return lax.ppermute(value, 'seq', pairs)  15.8 us
    pallas_call x1, Pallas kernels, run_early(): pl.pallas_call(early_kernel, out_shape=(jax.ShapeDtypeStruct((samples, ro...  10.9 us
    ppermute x4, starting transfers between devices, exchanged(): lax.ppermute(value, axis, [(t, t ^ 1 << bit) for t in range(lax.axis_size...  9.8 us
    pallas_call x1, Pallas kernels, run_late(): pl.pallas_call(late_kernel, out_shape=(jax.ShapeDtypeStruct(mid.shape, BF...  8.97 us
    pallas_call x1, Pallas kernels, run_atoms(): pl.pallas_call(atom_kernel, out_shape=(jax.ShapeDtypeStruct((samples, ato...  7.63 us
    ppermute x1, waiting for transfers between devices, per_device(): before = lax.ppermute(last, 'seq', to_next)  7.01 us
    ppermute x1, starting transfers between devices, per_device(): after = lax.ppermute(first, 'seq', to_previous)  6.54 us
  transfers between devices with their start and end apart: 19, of which 9 were waited for; matrix products, arithmetic and copies ran while one was open for 0% of the time, Pallas kernels for 21%

profile of v6, /device:TPU:6, one launch (start us, length us, event | category | flops | bytes accessed | tf_op | source)
XLA Modules:
  0.0 123.7 jit_solution(18335405005559930834)
XLA Ops:
  0.6 3.4 %collective-permute-start.2 = (bf16[96,1536]{1,0:T(8,128)(2,1)}, bf16[96,1536]{1,0:T(8,128)(2,1)S(1)}, u32[]{:S(2)}, u32[]{:S(2)}) collective-permute-start(bf16[96,1536]{1,0:T(8,128)(2,1)} %bitcast.13), channel_id=1, source_target_pairs={{0,64},{32,96},{64,0},{96,32},{128,192},{160,224},{192,128},{224,1... | collective-permute-start | bytes 884744 | tf_op jit(solution)/shard_map/ppermute | solution.py:489
  4.0 2.2 %pack.1 = (bf16[304,128]{1,0:T(8,128)(2,1)}, bf16[96,128]{1,0:T(8,128)(2,1)}) custom-call(s32[2,12]{1,0:T(2,128)} %bitcast.19, bf16[2,384,128]{2,1,0:T(8,128)(2,1)} %act_hbm.3, bf16[4,12,32,128]{3,2,1,0:T(8,128)(2,1)} %bias_hbm.3), custom_call_target="tpu_custom_call" | custom-call | tf_op jit(solution)/shard_map/pack/pallas_call | solution.py:87
  6.2 6.5 %collective-permute-start.1 = (bf16[304,128]{1,0:T(8,128)(2,1)}, bf16[304,128]{1,0:T(8,128)(2,1)S(1)}, u32[]{:S(2)}, u32[]{:S(2)}) collective-permute-start(bf16[304,128]{1,0:T(8,128)(2,1)} %get-tuple-element.20), channel_id=1, source_target_pairs={{1,0},{2,1},{3,2},{4,3},{5,4},{6,5},{7,6},{8,7},{9,8},{10,9},{11,1... | collective-permute-start | bytes 233480 | tf_op jit(solution)/shard_map/ppermute | solution.py:623
  12.7 1.9 %collective-permute-start = (bf16[96,128]{1,0:T(8,128)(2,1)}, bf16[96,128]{1,0:T(8,128)(2,1)S(1)}, u32[]{:S(2)}, u32[]{:S(2)}) collective-permute-start(bf16[96,128]{1,0:T(8,128)(2,1)} %get-tuple-element.19), channel_id=1, source_target_pairs={{0,1},{1,2},{2,3},{3,4},{4,5},{5,6},{6,7},{7,8},{8,9},{9,10},{10,1... | collective-permute-start | bytes 73736 | tf_op jit(solution)/shard_map/ppermute | solution.py:624
  14.7 7.0 %collective-permute-done.before_ref = bf16[96,128]{1,0:T(8,128)(2,1)S(1)} collective-permute-done((bf16[96,128]{1,0:T(8,128)(2,1)}, bf16[96,128]{1,0:T(8,128)(2,1)S(1)}, u32[]{:S(2)}, u32[]{:S(2)}) %collective-permute-start) | collective-permute-done | bytes 24608 | tf_op jit(solution)/shard_map/ppermute | solution.py:624
  21.7 0.6 copy-done.13
  22.3 0.0 copy-done.12
  22.3 7.6 %atoms.1 = (bf16[2,384,128]{2,1,0:T(8,128)(2,1)}, bf16[2,48,768]{2,1,0:T(8,128)(2,1)}, bf16[2,48,768]{2,1,0:T(8,128)(2,1)}) custom-call(s32[2,12]{1,0:T(2,128)} %bitcast.20, s32[48]{0:T(128)} %count_ref.1, bf16[96,128]{1,0:T(8,128)(2,1)} %copy-done.13, bf16[304,128]{1,0:T(8,128)(2,1)} %copy-done.12, f32[1,128]{1,0:T(1,128)} %bitcast.21, s32[3,128]{1,0:T(4,128)} %bitcast.15, ...), custom_call_target="tpu_custom_call" | custom-call | flops 1000000 | bytes 1000 | tf_op jit(solution)/shard_map/atoms/pallas_call | solution.py:239
  30.0 0.1 collective-permute-start.3
  30.1 5.3 %collective-permute-done.3.refs_2_.other_ref = bf16[2,48,768]{2,1,0:T(8,128)(2,1)S(1)} collective-permute-done((bf16[2,48,768]{2,1,0:T(8,128)(2,1)}, bf16[2,48,768]{2,1,0:T(8,128)(2,1)S(1)}, u32[]{:S(2)}, u32[]{:S(2)}) %collective-permute-start.3) | collective-permute-done | bytes 147488 | tf_op jit(solution)/shard_map/ppermute | solution.py:489
  35.4 1.0 copy-done.6
  36.4 0.1 join.2.refs_0_
  36.4 0.0 copy-start
  36.5 0.0 copy-start.3
  36.5 6.4 %collective-permute-start.4 = (bf16[192,1536]{1,0:T(8,128)(2,1)S(1)}, bf16[192,1536]{1,0:T(8,128)(2,1)S(1)}, u32[]{:S(2)}, u32[]{:S(2)}) collective-permute-start(bf16[192,1536]{1,0:T(8,128)(2,1)S(1)} %join.2.refs_0_), channel_id=1, source_target_pairs={{0,128},{32,160},{64,192},{96,224},{128,0},{160,32},{192,64},{224,... | collective-permute-start | bytes 1769480 | tf_op jit(solution)/shard_map/ppermute | solution.py:489
  42.8 0.9 copy-done.4
  43.8 1.2 collective-permute-start.10
  45.0 11.6 %collective-permute-start.5 = (bf16[96,768]{1,0:T(8,128)(2,1)S(1)}, bf16[96,768]{1,0:T(8,128)(2,1)S(1)}, u32[]{:S(2)}, u32[]{:S(2)}) collective-permute-start(bf16[96,768]{1,0:T(8,128)(2,1)S(1)} %get-tuple-element.22.refs_0_), channel_id=1, source_target_pairs={{0,2},{1,3},{2,4},{3,5},{4,6},{5,7},{6,0},{7,1},{8,10},{9,11},{10,... | collective-permute-start | bytes 442376 | tf_op jit(solution)/shard_map/ppermute | solution.py:485
  56.6 0.4 collective-permute-start.6
  57.0 3.3 %collective-permute-start.7 = (bf16[96,768]{1,0:T(8,128)(2,1)S(1)}, bf16[96,768]{1,0:T(8,128)(2,1)S(1)}, u32[]{:S(2)}, u32[]{:S(2)}) collective-permute-start(bf16[96,768]{1,0:T(8,128)(2,1)S(1)} %get-tuple-element.22.refs_0_), channel_id=1, source_target_pairs={{0,4},{1,5},{2,6},{3,7},{4,0},{5,1},{6,2},{7,3},{8,12},{9,13},{10,... | collective-permute-start | bytes 442376 | tf_op jit(solution)/shard_map/ppermute | solution.py:485
  60.3 2.1 %collective-permute-start.8 = (bf16[96,768]{1,0:T(8,128)(2,1)S(1)}, bf16[96,768]{1,0:T(8,128)(2,1)S(1)}, u32[]{:S(2)}, u32[]{:S(2)}) collective-permute-start(bf16[96,768]{1,0:T(8,128)(2,1)S(1)} %get-tuple-element.23.refs_4_), channel_id=1, source_target_pairs={{0,8},{1,9},{2,10},{3,11},{4,12},{5,13},{6,14},{7,15},{8,16},{9,17... | collective-permute-start | bytes 442376 | tf_op jit(solution)/shard_map/ppermute | solution.py:485
  62.4 0.7 collective-permute-done.6.refs_2_
  63.0 1.8 %collective-permute-done.7.refs_3_ = bf16[96,768]{1,0:T(8,128)(2,1)S(1)} collective-permute-done((bf16[96,768]{1,0:T(8,128)(2,1)S(1)}, bf16[96,768]{1,0:T(8,128)(2,1)S(1)}, u32[]{:S(2)}, u32[]{:S(2)}) %collective-permute-start.7) | collective-permute-done | bytes 147488 | tf_op jit(solution)/shard_map/ppermute | solution.py:485
  64.8 0.6 collective-permute-done.8.refs_5_
  65.4 3.3 %collective-permute-done.9.refs_6_ = bf16[96,768]{1,0:T(8,128)(2,1)S(1)} collective-permute-done((bf16[96,768]{1,0:T(8,128)(2,1)S(1)}, bf16[96,768]{1,0:T(8,128)(2,1)S(1)}, u32[]{:S(2)}, u32[]{:S(2)}) %collective-permute-start.9) | collective-permute-done | bytes 147488 | tf_op jit(solution)/shard_map/ppermute | solution.py:485
  68.7 1.1 lines.1
  69.8 1.1 join.3
  71.0 1.6 %collective-permute-start.14 = (bf16[384,768]{1,0:T(8,128)(2,1)}, bf16[384,768]{1,0:T(8,128)(2,1)}, u32[]{:S(2)}, u32[]{:S(2)}) collective-permute-start(bf16[384,768]{1,0:T(8,128)(2,1)} %get-tuple-element.24.refs_2_.own1_ref), channel_id=1, source_target_pairs={{0,2},{1,3},{2,4},{3,5},{4,6},{5,7},{6,0},{7,1},{8,10},{9,11},{10,... | collective-permute-start | bytes 1769480 | tf_op jit(solution)/shard_map/ppermute | solution.py:485
  72.6 1.1 collective-permute-start.16
  73.8 2.5 %collective-permute-start.17 = (bf16[384,768]{1,0:T(8,128)(2,1)}, bf16[384,768]{1,0:T(8,128)(2,1)}, u32[]{:S(2)}, u32[]{:S(2)}) collective-permute-start(bf16[384,768]{1,0:T(8,128)(2,1)} %get-tuple-element.24.refs_2_.own1_ref), channel_id=1, source_target_pairs={{0,6},{1,7},{2,0},{3,1},{4,2},{5,3},{6,4},{7,5},{8,14},{9,15},{10,... | collective-permute-start | bytes 1769480 | tf_op jit(solution)/shard_map/ppermute | solution.py:485
  76.2 0.9 copy-done.5
  77.1 1.6 %queries.1.absorbed_ref = bf16[2,768,768]{2,1,0:T(8,128)(2,1)S(1)} custom-call(bf16[2,48,768]{2,1,0:T(8,128)(2,1)S(1)} %copy-done.5, bf16[768,768]{1,0:T(8,128)(2,1)S(1)} %copy-done.3, bf16[768,1536]{1,0:T(8,128)(2,1)S(1)} %copy-done), custom_call_target="tpu_custom_call" | custom-call | flops 1000000 | bytes 1000 | tf_op jit(solution)/shard_map/queries/pallas_call | solution.py:278
  78.8 8.2 %collective-permute-done.12.low0_ref = bf16[384,768]{1,0:T(8,128)(2,1)} collective-permute-done((bf16[384,768]{1,0:T(8,128)(2,1)}, bf16[384,768]{1,0:T(8,128)(2,1)}, u32[]{:S(2)}, u32[]{:S(2)}) %collective-permute-start.12) | collective-permute-done | bytes 589856 | tf_op jit(solution)/shard_map/ppermute | solution.py:485
  87.0 1.5 %collective-permute-start.13 = (bf16[384,768]{1,0:T(8,128)(2,1)}, bf16[384,768]{1,0:T(8,128)(2,1)S(1)}, u32[]{:S(2)}, u32[]{:S(2)}) collective-permute-start(bf16[384,768]{1,0:T(8,128)(2,1)} %collective-permute-done.12.low0_ref), channel_id=1, source_target_pairs={{0,8},{1,9},{2,10},{3,11},{4,12},{5,13},{6,14},{7,15},{8,16},{9,17... | collective-permute-start | bytes 1769480 | tf_op jit(solution)/shard_map/ppermute | solution.py:485
  88.5 1.4 %collective-permute-start.15 = (bf16[384,768]{1,0:T(8,128)(2,1)}, bf16[384,768]{1,0:T(8,128)(2,1)S(1)}, u32[]{:S(2)}, u32[]{:S(2)}) collective-permute-start(bf16[384,768]{1,0:T(8,128)(2,1)} %collective-permute-done.14.low1_ref), channel_id=1, source_target_pairs={{0,2},{1,3},{2,4},{3,5},{4,6},{5,7},{6,0},{7,1},{8,10},{9,11},{10,... | collective-permute-start | bytes 1769480 | tf_op jit(solution)/shard_map/ppermute | solution.py:485
  89.9 2.6 %reorder.1 = (bf16[16,48,1536]{2,1,0:T(8,128)(2,1)S(1)}, bf16[16,48,1536]{2,1,0:T(8,128)(2,1)S(1)}) custom-call(bf16[4,2,48,1536]{3,2,1,0:T(8,128)(2,1)} %bitcast.5.near_ref, bf16[4,2,48,1536]{3,2,1,0:T(8,128)(2,1)} %bitcast.6.far_ref), custom_call_target="tpu_custom_call" | custom-call | flops 2000000000 | bytes 1000 | tf_op jit(solution)/shard_map/reorder/pallas_call | solution.py:311
  92.6 0.0 slice-start
  92.6 0.0 copy-start.1
  92.6 0.0 copy-start.2
  92.6 0.0 copy-start.7
  92.6 0.0 copy-start.9
  92.6 0.0 copy-start.10
  92.7 10.9 %early.1 = (f32[2,768,768]{2,1,0:T(8,128)S(1)}, f32[2,768,128]{2,1,0:T(8,128)S(1)}, f32[2,768,128]{2,1,0:T(8,128)S(1)}) custom-call(bf16[2,768,768]{2,1,0:T(8,128)(2,1)S(1)} %queries.1.absorbed_ref, bf16[16,48,1536]{2,1,0:T(8,128)(2,1)S(1)} %get-tuple-element.25.bias0_ref, bf16[16,48,1536]{2,1,0:T(8,128)(2,1)S(1)} %get-tuple-element.26.bias1_ref, ...), custom_call_target="tpu_custom_call" | custom-call | flops 8000000000 | bytes 1000 | tf_op jit(solution)/shard_map/early/pallas_call | solution.py:376
  103.6 1.2 collective-permute-done.15.far1_ref
  104.9 9.0 %late.1 = (bf16[2,384,128]{2,1,0:T(8,128)(2,1)}, bf16[2,48,768]{2,1,0:T(8,128)(2,1)}, bf16[2,48,128]{2,1,0:T(8,128)(2,1)S(1)}) custom-call(bf16[2,768,768]{2,1,0:T(8,128)(2,1)S(1)} %queries.1.absorbed_ref, bf16[16,48,1536]{2,1,0:T(8,128)(2,1)S(1)} %get-tuple-element.25.bias0_ref, bf16[16,48,1536]{2,1,0:T(8,128)(2,1)S(1)} %get-tuple-element.26.bias1_ref, ...), custom_call_target="tpu_custom_call" | custom-call | flops 5000000000 | bytes 1000 | tf_op jit(solution)/shard_map/late/pallas_call | solution.py:464
  113.9 1.9 %collective-permute-start.18 = (bf16[2,128]{1,0:T(2,128)(2,1)S(1)}, bf16[2,128]{1,0:T(2,128)(2,1)S(1)}, u32[]{:S(2)}, u32[]{:S(2)}) collective-permute-start(bf16[2,128]{1,0:T(2,128)(2,1)S(1)} %bitcast.22), channel_id=1, source_target_pairs={{0,1},{1,2},{2,3},{3,4},{4,5},{5,6},{6,7},{7,8},{8,9},{9,10},{10,1... | collective-permute-start | bytes 1544 | tf_op jit(solution)/shard_map/ppermute | solution.py:657
  115.8 6.5 %collective-permute-done.18 = bf16[2,128]{1,0:T(2,128)(2,1)S(1)} collective-permute-done((bf16[2,128]{1,0:T(2,128)(2,1)S(1)}, bf16[2,128]{1,0:T(2,128)(2,1)S(1)}, u32[]{:S(2)}, u32[]{:S(2)}) %collective-permute-start.18) | collective-permute-done | bytes 544 | tf_op jit(solution)/shard_map/ppermute | solution.py:657
  122.3 1.4 %fusion = bf16[2,384,128]{2,1,0:T(8,128)(2,1)} fusion(bf16[2,384,128]{2,1,0:T(8,128)(2,1)} %get-tuple-element.33, f32[2,128]{1,0:T(2,128)S(1)} %convert_element_type.11, pred[8]{0:T(512)(128)(4,1)S(1)} %slice_compare_fusion), kind=kLoop, calls=%fused_computation.1 | loop fusion | flops 8192 | bytes 9224 | tf_op jit(solution)/shard_map/dynamic_update_slice | solution.py:661
  (38 shorter events, 0.1 us)
Async XLA Ops:
  0.6 34.8 %collective-permute-start.2 = (bf16[96,1536]{1,0:T(8,128)(2,1)}, bf16[96,1536]{1,0:T(8,128)(2,1)S(1)}, u32[]{:S(2)}, u32[]{:S(2)}) collective-permute-start(bf16[96,1536]{1,0:T(8,128)(2,1)} %bitcast.13), channel_id=1, source_target_pairs={{0,64},{32,96},{64,0},{96,32},{128,192},{160,224},{192,128},{224,1... | collective-permute-start | bytes 884744 | tf_op jit(solution)/shard_map/ppermute | solution.py:489
  6.2 15.5 %collective-permute-start.1 = (bf16[304,128]{1,0:T(8,128)(2,1)}, bf16[304,128]{1,0:T(8,128)(2,1)S(1)}, u32[]{:S(2)}, u32[]{:S(2)}) collective-permute-start(bf16[304,128]{1,0:T(8,128)(2,1)} %get-tuple-element.20), channel_id=1, source_target_pairs={{1,0},{2,1},{3,2},{4,3},{5,4},{6,5},{7,6},{8,7},{9,8},{10,9},{11,1... | collective-permute-start | bytes 233480 | tf_op jit(solution)/shard_map/ppermute | solution.py:623
  12.7 8.9 %collective-permute-start = (bf16[96,128]{1,0:T(8,128)(2,1)}, bf16[96,128]{1,0:T(8,128)(2,1)S(1)}, u32[]{:S(2)}, u32[]{:S(2)}) collective-permute-start(bf16[96,128]{1,0:T(8,128)(2,1)} %get-tuple-element.19), channel_id=1, source_target_pairs={{0,1},{1,2},{2,3},{3,4},{4,5},{5,6},{6,7},{7,8},{8,9},{9,10},{10,1... | collective-permute-start | bytes 73736 | tf_op jit(solution)/shard_map/ppermute | solution.py:624
  21.7 0.6 copy-start.13
  21.7 0.6 copy-start.12
  30.0 5.4 %collective-permute-start.3 = (bf16[2,48,768]{2,1,0:T(8,128)(2,1)}, bf16[2,48,768]{2,1,0:T(8,128)(2,1)S(1)}, u32[]{:S(2)}, u32[]{:S(2)}) collective-permute-start(bf16[2,48,768]{2,1,0:T(8,128)(2,1)} %get-tuple-element.21.norm_ref.own_ref), channel_id=1, source_target_pairs={{0,1},{1,0},{2,3},{3,2},{4,5},{5,4},{6,7},{7,6},{8,9},{9,8},{10,11... | collective-permute-start | bytes 442376 | tf_op jit(solution)/shard_map/ppermute | solution.py:489
  35.4 1.0 copy-start.6
  36.4 39.8 %copy-start = (bf16[768,1536]{1,0:T(8,128)(2,1)S(1)}, bf16[768,1536]{1,0:T(8,128)(2,1)}, u32[]{:S(2)}) copy-start(bf16[768,1536]{1,0:T(8,128)(2,1)} %keyval_ref.3) | copy-start | bytes 7077892
  36.5 39.8 %copy-start.3 = (bf16[768,768]{1,0:T(8,128)(2,1)S(1)}, bf16[768,768]{1,0:T(8,128)(2,1)}, u32[]{:S(2)}) copy-start(bf16[768,768]{1,0:T(8,128)(2,1)} %query_ref.1) | copy-start | bytes 3538948
  36.5 33.4 %collective-permute-start.4 = (bf16[192,1536]{1,0:T(8,128)(2,1)S(1)}, bf16[192,1536]{1,0:T(8,128)(2,1)S(1)}, u32[]{:S(2)}, u32[]{:S(2)}) collective-permute-start(bf16[192,1536]{1,0:T(8,128)(2,1)S(1)} %join.2.refs_0_), channel_id=1, source_target_pairs={{0,128},{32,160},{64,192},{96,224},{128,0},{160,32},{192,64},{224,... | collective-permute-start | bytes 1769480 | tf_op jit(solution)/shard_map/ppermute | solution.py:489
  42.8 0.9 copy-start.4
  43.8 16.5 %collective-permute-start.10 = (bf16[96,768]{1,0:T(8,128)(2,1)S(1)}, bf16[96,768]{1,0:T(8,128)(2,1)S(1)}, u32[]{:S(2)}, u32[]{:S(2)}) collective-permute-start(bf16[96,768]{1,0:T(8,128)(2,1)S(1)} %get-tuple-element.23.refs_4_), channel_id=1, source_target_pairs={{0,16},{1,17},{2,18},{3,19},{4,20},{5,21},{6,22},{7,23},{8,24},{9,... | collective-permute-start | bytes 442376 | tf_op jit(solution)/shard_map/ppermute | solution.py:485
  45.0 17.4 %collective-permute-start.5 = (bf16[96,768]{1,0:T(8,128)(2,1)S(1)}, bf16[96,768]{1,0:T(8,128)(2,1)S(1)}, u32[]{:S(2)}, u32[]{:S(2)}) collective-permute-start(bf16[96,768]{1,0:T(8,128)(2,1)S(1)} %get-tuple-element.22.refs_0_), channel_id=1, source_target_pairs={{0,2},{1,3},{2,4},{3,5},{4,6},{5,7},{6,0},{7,1},{8,10},{9,11},{10,... | collective-permute-start | bytes 442376 | tf_op jit(solution)/shard_map/ppermute | solution.py:485
  56.6 6.5 %collective-permute-start.6 = (bf16[96,768]{1,0:T(8,128)(2,1)S(1)}, bf16[96,768]{1,0:T(8,128)(2,1)S(1)}, u32[]{:S(2)}, u32[]{:S(2)}) collective-permute-start(bf16[96,768]{1,0:T(8,128)(2,1)S(1)} %get-tuple-element.22.refs_0_), channel_id=1, source_target_pairs={{0,6},{1,7},{2,0},{3,1},{4,2},{5,3},{6,4},{7,5},{8,14},{9,15},{10,... | collective-permute-start | bytes 442376 | tf_op jit(solution)/shard_map/ppermute | solution.py:485
  57.0 7.9 %collective-permute-start.7 = (bf16[96,768]{1,0:T(8,128)(2,1)S(1)}, bf16[96,768]{1,0:T(8,128)(2,1)S(1)}, u32[]{:S(2)}, u32[]{:S(2)}) collective-permute-start(bf16[96,768]{1,0:T(8,128)(2,1)S(1)} %get-tuple-element.22.refs_0_), channel_id=1, source_target_pairs={{0,4},{1,5},{2,6},{3,7},{4,0},{5,1},{6,2},{7,3},{8,12},{9,13},{10,... | collective-permute-start | bytes 442376 | tf_op jit(solution)/shard_map/ppermute | solution.py:485
  60.3 5.1 %collective-permute-start.8 = (bf16[96,768]{1,0:T(8,128)(2,1)S(1)}, bf16[96,768]{1,0:T(8,128)(2,1)S(1)}, u32[]{:S(2)}, u32[]{:S(2)}) collective-permute-start(bf16[96,768]{1,0:T(8,128)(2,1)S(1)} %get-tuple-element.23.refs_4_), channel_id=1, source_target_pairs={{0,8},{1,9},{2,10},{3,11},{4,12},{5,13},{6,14},{7,15},{8,16},{9,17... | collective-permute-start | bytes 442376 | tf_op jit(solution)/shard_map/ppermute | solution.py:485
  62.4 6.4 %collective-permute-start.9 = (bf16[96,768]{1,0:T(8,128)(2,1)S(1)}, bf16[96,768]{1,0:T(8,128)(2,1)S(1)}, u32[]{:S(2)}, u32[]{:S(2)}) collective-permute-start(bf16[96,768]{1,0:T(8,128)(2,1)S(1)} %get-tuple-element.23.refs_4_), channel_id=1, source_target_pairs={{0,24},{1,25},{2,26},{3,27},{4,28},{5,29},{6,30},{7,31},{8,0},{9,1... | collective-permute-start | bytes 442376 | tf_op jit(solution)/shard_map/ppermute | solution.py:485
  71.0 18.9 %collective-permute-start.11 = (bf16[384,1536]{1,0:T(8,128)(2,1)}, bf16[384,1536]{1,0:T(8,128)(2,1)}, u32[]{:S(2)}, u32[]{:S(2)}) collective-permute-start(bf16[384,1536]{1,0:T(8,128)(2,1)} %join.3), channel_id=1, source_target_pairs={{0,32},{32,0},{64,96},{96,64},{128,160},{160,128},{192,224},{224,1... | collective-permute-start | bytes 3538952 | tf_op jit(solution)/shard_map/ppermute | solution.py:489
  71.0 16.1 %collective-permute-start.12 = (bf16[384,768]{1,0:T(8,128)(2,1)}, bf16[384,768]{1,0:T(8,128)(2,1)}, u32[]{:S(2)}, u32[]{:S(2)}) collective-permute-start(bf16[384,768]{1,0:T(8,128)(2,1)} %get-tuple-element.27.own0_ref), channel_id=1, source_target_pairs={{0,8},{1,9},{2,10},{3,11},{4,12},{5,13},{6,14},{7,15},{8,16},{9,17... | collective-permute-start | bytes 1769480 | tf_op jit(solution)/shard_map/ppermute | solution.py:485
  71.0 17.6 %collective-permute-start.14 = (bf16[384,768]{1,0:T(8,128)(2,1)}, bf16[384,768]{1,0:T(8,128)(2,1)}, u32[]{:S(2)}, u32[]{:S(2)}) collective-permute-start(bf16[384,768]{1,0:T(8,128)(2,1)} %get-tuple-element.24.refs_2_.own1_ref), channel_id=1, source_target_pairs={{0,2},{1,3},{2,4},{3,5},{4,6},{5,7},{6,0},{7,1},{8,10},{9,11},{10,... | collective-permute-start | bytes 1769480 | tf_op jit(solution)/shard_map/ppermute | solution.py:485
  72.6 19.9 %collective-permute-start.16 = (bf16[384,768]{1,0:T(8,128)(2,1)}, bf16[384,768]{1,0:T(8,128)(2,1)}, u32[]{:S(2)}, u32[]{:S(2)}) collective-permute-start(bf16[384,768]{1,0:T(8,128)(2,1)} %get-tuple-element.27.own0_ref), channel_id=1, source_target_pairs={{0,24},{1,25},{2,26},{3,27},{4,28},{5,29},{6,30},{7,31},{8,0},{9,1... | collective-permute-start | bytes 1769480 | tf_op jit(solution)/shard_map/ppermute | solution.py:485
  73.8 18.8 %collective-permute-start.17 = (bf16[384,768]{1,0:T(8,128)(2,1)}, bf16[384,768]{1,0:T(8,128)(2,1)}, u32[]{:S(2)}, u32[]{:S(2)}) collective-permute-start(bf16[384,768]{1,0:T(8,128)(2,1)} %get-tuple-element.24.refs_2_.own1_ref), channel_id=1, source_target_pairs={{0,6},{1,7},{2,0},{3,1},{4,2},{5,3},{6,4},{7,5},{8,14},{9,15},{10,... | collective-permute-start | bytes 1769480 | tf_op jit(solution)/shard_map/ppermute | solution.py:485
  76.2 0.9 copy-start.5
  87.0 16.6 %collective-permute-start.13 = (bf16[384,768]{1,0:T(8,128)(2,1)}, bf16[384,768]{1,0:T(8,128)(2,1)S(1)}, u32[]{:S(2)}, u32[]{:S(2)}) collective-permute-start(bf16[384,768]{1,0:T(8,128)(2,1)} %collective-permute-done.12.low0_ref), channel_id=1, source_target_pairs={{0,8},{1,9},{2,10},{3,11},{4,12},{5,13},{6,14},{7,15},{8,16},{9,17... | collective-permute-start | bytes 1769480 | tf_op jit(solution)/shard_map/ppermute | solution.py:485
  88.5 16.3 %collective-permute-start.15 = (bf16[384,768]{1,0:T(8,128)(2,1)}, bf16[384,768]{1,0:T(8,128)(2,1)S(1)}, u32[]{:S(2)}, u32[]{:S(2)}) collective-permute-start(bf16[384,768]{1,0:T(8,128)(2,1)} %collective-permute-done.14.low1_ref), channel_id=1, source_target_pairs={{0,2},{1,3},{2,4},{3,5},{4,6},{5,7},{6,0},{7,1},{8,10},{9,11},{10,... | collective-permute-start | bytes 1769480 | tf_op jit(solution)/shard_map/ppermute | solution.py:485
  92.6 12.3 %slice-start = ((s8[4718592]{0:T(1024)(128)(4,1)}), s8[4194304]{0:T(1024)(128)(4,1)S(1)}, s32[]{:S(2)}) async-start(s8[4718592]{0:T(1024)(128)(4,1)} %bitcast.11), calls=%async_computation | async-start | bytes 8388608
  92.6 12.3 %slice-start.1 = ((s8[4718592]{0:T(1024)(128)(4,1)}), s8[524288]{0:T(1024)(128)(4,1)S(1)}, s32[]{:S(2)}) async-start(s8[4718592]{0:T(1024)(128)(4,1)} %bitcast.11), calls=%async_computation.1 | async-start | bytes 1048576
  92.6 12.2 %copy-start.1 = (bf16[1536,768]{1,0:T(8,128)(2,1)S(1)}, bf16[1536,768]{1,0:T(8,128)(2,1)}, u32[]{:S(2)}) copy-start(bf16[1536,768]{1,0:T(8,128)(2,1)} %down_ref.1) | copy-start | bytes 7077892
  92.6 12.2 %copy-start.2 = (bf16[768,768]{1,0:T(8,128)(2,1)S(1)}, bf16[768,768]{1,0:T(8,128)(2,1)}, u32[]{:S(2)}) copy-start(bf16[768,768]{1,0:T(8,128)(2,1)} %output_ref.1) | copy-start | bytes 3538948
  92.6 12.2 %copy-start.7 = (bf16[768,128]{1,0:T(8,128)(2,1)S(1)}, bf16[768,128]{1,0:T(8,128)(2,1)}, u32[]{:S(2)}) copy-start(bf16[768,128]{1,0:T(8,128)(2,1)} %back_ref.1) | copy-start | bytes 589828
  92.6 12.2 %copy-start.8 = (bf16[2,384,128]{2,1,0:T(8,128)(2,1)S(1)}, bf16[2,384,128]{2,1,0:T(8,128)(2,1)}, u32[]{:S(2)}) copy-start(bf16[2,384,128]{2,1,0:T(8,128)(2,1)} %get-tuple-element.32.mid_ref) | copy-start | bytes 589828
  92.6 12.2 %copy-start.9 = (bf16[2,48,768]{2,1,0:T(8,128)(2,1)S(1)}, bf16[2,48,768]{2,1,0:T(8,128)(2,1)}, u32[]{:S(2)}) copy-start(bf16[2,48,768]{2,1,0:T(8,128)(2,1)} %get-tuple-element.31.tokact_ref) | copy-start | bytes 442372
  92.6 12.2 %copy-start.10 = (s32[384]{0:T(512)S(1)}, s32[384]{0:T(512)}, u32[]{:S(2)}) copy-start(s32[384]{0:T(512)} %param.26) | copy-start | bytes 4612
  92.7 12.2 %copy-start.11 = (f32[768]{0:T(1024)S(1)}, f32[768]{0:T(1024)}, u32[]{:S(2)}) copy-start(f32[768]{0:T(1024)} %param.34) | copy-start | bytes 9220
  113.9 8.4 %collective-permute-start.18 = (bf16[2,128]{1,0:T(2,128)(2,1)S(1)}, bf16[2,128]{1,0:T(2,128)(2,1)S(1)}, u32[]{:S(2)}, u32[]{:S(2)}) collective-permute-start(bf16[2,128]{1,0:T(2,128)(2,1)S(1)} %bitcast.22), channel_id=1, source_target_pairs={{0,1},{1,2},{2,3},{3,4},{4,5},{5,6},{6,7},{7,8},{8,9},{9,10},{10,1... | collective-permute-start | bytes 1544 | tf_op jit(solution)/shard_map/ppermute | solution.py:657

commit v7 on v6

--- a/solution.py
+++ b/solution.py
@@ -256,7 +256,7 @@
     )(key_range, counts, before, after, gain, token, token_gain, *arrays)
 
 
-def query_kernel(norm_ref, query_ref, keyval_ref, absorbed_ref):
+def query_kernel(norm_ref, query_ref, keyval_ref, after_hbm, absorbed_ref):
     samples, tokens, width = norm_ref.shape
     head_size = width // HEADS
     scale = 1.0 / math.sqrt(head_size)
@@ -273,28 +273,34 @@
             absorbed_ref[s, lanes * g : lanes * (g + 1)] = absorbed.astype(BF16)
 
 
-def run_queries(norm, token_query, token_keyval):
+def run_queries(norm, token_query, token_keyval, after):
     samples, tokens, width = norm.shape
     return pl.pallas_call(
         query_kernel,
         out_shape=jax.ShapeDtypeStruct((samples, HEADS * tokens, width), BF16),
-        in_specs=[vmem()] * 3,
+        in_specs=[vmem()] * 3 + [anywhere()],
         out_specs=vmem(),
         compiler_params=pltpu.CompilerParams(vmem_limit_bytes=16 * 2**20),
-        cost_estimate=cost(1_000_000),
+        cost_estimate=cost(1000000),
         name="queries",
-    )(norm, token_query, token_keyval)
-
-
-def reorder_kernel(near_ref, far_ref, bias_ref, turned_ref):
+    )(norm, token_query, token_keyval, after)
+
+
+def reorder_kernel(near_ref, near_far_ref, other_ref, other_far_ref, bias_ref, turned_ref):
     columns, heads, _, keys = near_ref.shape
     line = keys // 4
     part = line // 4
-    core = lax.axis_index("samp") % 2
-    for source, which in ((near_ref, core), (far_ref, 1 - core)):
+    place_of = lax.axis_index("samp")
+    core, upper = place_of % 2, place_of // (2 * columns)
+    for source, which, half in (
+        (near_ref, core, upper),
+        (near_far_ref, core, 1 - upper),
+        (other_ref, 1 - core, upper),
+        (other_far_ref, 1 - core, 1 - upper),
+    ):
         for column in range(columns):
             for head in range(heads):
-                at = (2 * column + which) * heads + head
+                at = (2 * (columns * half + column) + which) * heads + head
                 rows = source[column, head]
                 bias_ref[at] = rows
                 blocks = [
@@ -305,18 +311,18 @@
                 turned_ref[at] = jnp.concatenate(blocks, axis=1)
 
 
-def run_reorder(near, far):
-    columns, heads, tokens, keys = near.shape
-    shape = jax.ShapeDtypeStruct((2 * columns * heads, tokens, keys), BF16)
+def run_reorder(parts):
+    columns, heads, tokens, keys = parts[0].shape
+    shape = jax.ShapeDtypeStruct((4 * columns * heads, tokens, keys), BF16)
     return pl.pallas_call(
         reorder_kernel,
         out_shape=(shape, shape),
-        in_specs=[vmem(), vmem()],
+        in_specs=[vmem()] * 4,
         out_specs=(vmem(), vmem()),
         compiler_params=pltpu.CompilerParams(vmem_limit_bytes=24 * 2**20),
-        cost_estimate=cost(2_000_000_000),
+        cost_estimate=cost(4000000000),
         name="reorder",
-    )(near, far)
+    )(*parts)
 
 
 def place(device, sample):
@@ -383,7 +389,7 @@
         in_specs=[vmem()] * (3 + len(pieces)),
         out_specs=(vmem(),) * 3,
         compiler_params=pltpu.CompilerParams(vmem_limit_bytes=18 * 2**20),
-        cost_estimate=cost(8_000_000_000),
+        cost_estimate=cost(8000000000),
         name="early",
     )(absorbed, bias0, bias1, *pieces)
 
@@ -513,66 +519,11 @@
     )(*own, *other, *after)
 
 
-STEPS = (0, 3, 1, 2)
-
-
-def line_kernel(*refs):
-    count = 2 * len(STEPS)
-    device = lax.axis_index("seq")
-    for s, line in enumerate(refs[count:]):
-        at = place(device, s + 1)
-        for step, piece in zip(STEPS, refs[len(STEPS) * s :]):
-            rows = piece.shape[0]
-            start = pl.multiple_of((at + step) % 4 * rows, 16)
-            line[pl.ds(start, rows)] = piece[...]
-
-
-def lines_of(first, second):
-    rows, width = first[0].shape
-    shape = jax.ShapeDtypeStruct((4 * rows, width), BF16)
-    return pl.pallas_call(
-        line_kernel,
-        out_shape=(shape, shape),
-        in_specs=[vmem()] * 8,
-        out_specs=(vmem(),) * 2,
-        compiler_params=pltpu.CompilerParams(vmem_limit_bytes=16 * 2**20),
-        cost_estimate=cost(1_000_000),
-        name="lines",
-    )(*first, *second)
-
-
-def pair_kernel(own_ref, other_ref, first_ref, second_ref):
-    rows = own_ref.shape[1]
-    where = lax.axis_index("seq") % 2
-    for s, pair in enumerate((first_ref, second_ref)):
-        pair[pl.ds(pl.multiple_of(where * rows, 16), rows)] = own_ref[s]
-        pair[pl.ds(pl.multiple_of((1 - where) * rows, 16), rows)] = other_ref[s]
-
-
-def pairs_of(own, other):
-    _, rows, width = own.shape
-    shape = jax.ShapeDtypeStruct((2 * rows, width), BF16)
-    return pl.pallas_call(
-        pair_kernel,
-        out_shape=(shape, shape),
-        in_specs=[vmem()] * 2,
-        out_specs=(vmem(),) * 2,
-        compiler_params=pltpu.CompilerParams(vmem_limit_bytes=16 * 2**20),
-        cost_estimate=cost(1_000_000),
-        name="pairs",
-    )(own, other)
-
-
 def spread(norm):
     other = exchanged(norm, "seq", 0)
-    pairs = pairs_of(norm, other)
-    around = []
-    for value, dx, dy in ((pairs[0], 0, 1), (pairs[1], 1, 0)):
-        around.append(
-            [value]
-            + [shifted(value, by * dx, by * dy) for by in (1, -1, 2)]
-        )
-    lines = lines_of(*around)
+    lines = joined([norm[0], norm[1]], [other[0], other[1]], "seq", (0, 0))
+    for bits in ((1, 3), (2, 4)):
+        lines = joined(lines, [exchanged(v, "seq", b) for v, b in zip(lines, bits)], "seq", bits)
     near, far = [], []
     for value, dx, dy in ((lines[0], 1, 0), (lines[1], 0, 1)):
         low = shifted(value, dx, dy)
@@ -581,13 +532,14 @@
     return near, far, other
 
 
-def all_heads(bias, steps):
+def all_heads(bias, ready):
     heads, tokens, keys = bias.shape
     rows = bias.reshape(heads * tokens, keys)
-    for bit, after in zip((1, 2), steps):
-        (rows,) = joined([rows], [exchanged(rows, "samp", bit)], "samp", (bit,), (after,))
-    shape = (lax.axis_size("samp") // 2, heads, tokens, keys)
-    return rows.reshape(shape), exchanged(rows, "samp", 0).reshape(shape)
+    (pair,) = joined([rows], [exchanged(rows, "samp", 1)], "samp", (1,), (ready,))
+    other_pair = exchanged(pair, "samp", 0)
+    beyond = exchanged(pair, "samp", 2)
+    parts = (pair, beyond, other_pair, exchanged(beyond, "samp", 0))
+    return [part.reshape(2, heads, tokens, keys) for part in parts]
 
 
 def per_device(
@@ -638,9 +590,9 @@
         atom_output,
         gather_weight,
     )
-    absorbed = run_queries(token_norm, token_query, token_keyval)
     near, far, ready = spread(token_norm)
-    bias, turned = run_reorder(*all_heads(pair_bias, (ready, near[1][0])))
+    absorbed = run_queries(token_norm, token_query, token_keyval, token_norm)
+    bias, turned = run_reorder(all_heads(pair_bias, ready))
     early = run_early(absorbed, bias, turned, near[0] + near[1])
     atom_out, token_out, back_rows = run_late(
         absorbed,

time: 125 us -> 112 us (0.90)
  the two profiles are of different devices: /device:TPU:6 before, /device:TPU:2 now
where the time goes in v7:
time: 112 us
  waiting for transfers between devices  44 us (39%)
  Pallas kernels  34.9 us (31%)
  starting transfers between devices  26 us (23%)
  local copies, waits for them, and re-layouts  4.75 us (4%)
  other arithmetic  1.36 us (1%)
    ppermute x9, waiting for transfers between devices, exchanged(): lax.ppermute(value, axis, [(t, t ^ 1 << bit) for t in range(lax.axis_size...  18.1 us
    ppermute x1, waiting for transfers between devices, per_device(): before = lax.ppermute(last, 'seq', to_next)  11.8 us
    pallas_call x1, Pallas kernels, run_early(): pl.pallas_call(early_kernel, out_shape=(jax.ShapeDtypeStruct((samples, ro...  10.9 us
    pallas_call x1, Pallas kernels, run_late(): pl.pallas_call(late_kernel, out_shape=(jax.ShapeDtypeStruct(mid.shape, BF...  8.9 us
    ppermute x6, waiting for transfers between devices, shifted(): return lax.ppermute(value, 'seq', pairs)  8.46 us
    pallas_call x1, Pallas kernels, run_atoms(): pl.pallas_call(atom_kernel, out_shape=(jax.ShapeDtypeStruct((samples, ato...  7.79 us
    ppermute x9, starting transfers between devices, exchanged(): lax.ppermute(value, axis, [(t, t ^ 1 << bit) for t in range(lax.axis_size...  7.54 us
    ppermute x1, starting transfers between devices, per_device(): after = lax.ppermute(first, 'seq', to_previous)  6.25 us
  transfers between devices with their start and end apart: 18, of which 11 were waited for; matrix products, arithmetic and copies ran while one was open for 1% of the time, Pallas kernels for 21%

profile of v7, /device:TPU:2, one launch (start us, length us, event | category | flops | bytes accessed | tf_op | source)
XLA Modules:
  0.0 112.0 jit_solution(15549142820069926715)
XLA Ops:
  0.6 2.2 %pack.1 = (bf16[304,128]{1,0:T(8,128)(2,1)}, bf16[96,128]{1,0:T(8,128)(2,1)}) custom-call(s32[2,12]{1,0:T(2,128)} %bitcast.31, bf16[2,384,128]{2,1,0:T(8,128)(2,1)} %act_hbm.3, bf16[4,12,32,128]{3,2,1,0:T(8,128)(2,1)} %bias_hbm.3), custom_call_target="tpu_custom_call" | custom-call | tf_op jit(solution)/shard_map/pack/pallas_call | solution.py:87
  2.8 6.2 %collective-permute-start.1 = (bf16[304,128]{1,0:T(8,128)(2,1)}, bf16[304,128]{1,0:T(8,128)(2,1)S(1)}, u32[]{:S(2)}, u32[]{:S(2)}) collective-permute-start(bf16[304,128]{1,0:T(8,128)(2,1)} %get-tuple-element.22), channel_id=1, source_target_pairs={{1,0},{2,1},{3,2},{4,3},{5,4},{6,5},{7,6},{8,7},{9,8},{10,9},{11,1... | collective-permute-start | bytes 233480 | tf_op jit(solution)/shard_map/ppermute | solution.py:575
  9.1 3.4 %collective-permute-start.2 = (bf16[96,1536]{1,0:T(8,128)(2,1)}, bf16[96,1536]{1,0:T(8,128)(2,1)S(1)}, u32[]{:S(2)}, u32[]{:S(2)}) collective-permute-start(bf16[96,1536]{1,0:T(8,128)(2,1)} %bitcast.24), channel_id=1, source_target_pairs={{0,64},{32,96},{64,0},{96,32},{128,192},{160,224},{192,128},{224,1... | collective-permute-start | bytes 884744 | tf_op jit(solution)/shard_map/ppermute | solution.py:495
  12.5 1.9 %collective-permute-start = (bf16[96,128]{1,0:T(8,128)(2,1)}, bf16[96,128]{1,0:T(8,128)(2,1)S(1)}, u32[]{:S(2)}, u32[]{:S(2)}) collective-permute-start(bf16[96,128]{1,0:T(8,128)(2,1)} %get-tuple-element.21), channel_id=1, source_target_pairs={{0,1},{1,2},{2,3},{3,4},{4,5},{5,6},{6,7},{7,8},{8,9},{9,10},{10,1... | collective-permute-start | bytes 73736 | tf_op jit(solution)/shard_map/ppermute | solution.py:576
  14.4 11.8 %collective-permute-done.before_ref = bf16[96,128]{1,0:T(8,128)(2,1)S(1)} collective-permute-done((bf16[96,128]{1,0:T(8,128)(2,1)}, bf16[96,128]{1,0:T(8,128)(2,1)S(1)}, u32[]{:S(2)}, u32[]{:S(2)}) %collective-permute-start) | collective-permute-done | bytes 24608 | tf_op jit(solution)/shard_map/ppermute | solution.py:576
  26.2 0.0 collective-permute-done.1.after_ref
  26.2 0.6 copy-done.14
  26.8 0.0 copy-done.13
  26.8 7.8 %atoms.1 = (bf16[2,384,128]{2,1,0:T(8,128)(2,1)}, bf16[2,48,768]{2,1,0:T(8,128)(2,1)}, bf16[2,48,768]{2,1,0:T(8,128)(2,1)}) custom-call(s32[2,12]{1,0:T(2,128)} %bitcast.32, s32[48]{0:T(128)} %count_ref.1, bf16[96,128]{1,0:T(8,128)(2,1)} %copy-done.14, bf16[304,128]{1,0:T(8,128)(2,1)} %copy-done.13, f32[1,128]{1,0:T(1,128)} %bitcast.33, s32[3,128]{1,0:T(4,128)} %bitcast.26, ...), custom_call_target="tpu_custom_call" | custom-call | flops 1000000 | bytes 1000 | tf_op jit(solution)/shard_map/atoms/pallas_call | solution.py:239
  34.6 0.1 collective-permute-start.3
  34.7 1.0 slice_bitcast_fusion.2
  35.7 4.4 %collective-permute-done.3.refs_2_ = bf16[2,48,768]{2,1,0:T(8,128)(2,1)S(1)} collective-permute-done((bf16[2,48,768]{2,1,0:T(8,128)(2,1)}, bf16[2,48,768]{2,1,0:T(8,128)(2,1)S(1)}, u32[]{:S(2)}, u32[]{:S(2)}) %collective-permute-start.3) | collective-permute-done | bytes 147488 | tf_op jit(solution)/shard_map/ppermute | solution.py:495
  40.0 0.0 collective-permute-done.2.refs_1_
  40.0 1.0 copy-done.5
  41.0 0.1 join.4
  41.1 0.1 collective-permute-start.4
  41.2 0.1 collective-permute-start.7
  41.4 0.1 collective-permute-start.8
  41.5 5.0 %collective-permute-done.7.refs_2_ = bf16[96,768]{1,0:T(8,128)(2,1)S(1)} collective-permute-done((bf16[96,768]{1,0:T(8,128)(2,1)S(1)}, bf16[96,768]{1,0:T(8,128)(2,1)S(1)}, u32[]{:S(2)}, u32[]{:S(2)}) %collective-permute-start.7) | collective-permute-done | bytes 147488 | tf_op jit(solution)/shard_map/ppermute | solution.py:495
  46.5 0.4 collective-permute-done.8.refs_3_
  46.9 0.1 join.6
  46.9 3.8 %collective-permute-start.10 = (bf16[192,768]{1,0:T(8,128)(2,1)S(1)}, bf16[192,768]{1,0:T(8,128)(2,1)S(1)}, u32[]{:S(2)}, u32[]{:S(2)}) collective-permute-start(bf16[192,768]{1,0:T(8,128)(2,1)S(1)} %get-tuple-element.29.refs_1_), channel_id=1, source_target_pairs={{0,16},{1,17},{2,18},{3,19},{4,20},{5,21},{6,22},{7,23},{8,24},{9,... | collective-permute-start | bytes 884744 | tf_op jit(solution)/shard_map/ppermute | solution.py:495
  50.8 4.7 %collective-permute-done.10.refs_3_ = bf16[192,768]{1,0:T(8,128)(2,1)S(1)} collective-permute-done((bf16[192,768]{1,0:T(8,128)(2,1)S(1)}, bf16[192,768]{1,0:T(8,128)(2,1)S(1)}, u32[]{:S(2)}, u32[]{:S(2)}) %collective-permute-start.10) | collective-permute-done | bytes 294944 | tf_op jit(solution)/shard_map/ppermute | solution.py:495
  55.4 3.6 %collective-permute-done.9.refs_2_ = bf16[192,768]{1,0:T(8,128)(2,1)S(1)} collective-permute-done((bf16[192,768]{1,0:T(8,128)(2,1)S(1)}, bf16[192,768]{1,0:T(8,128)(2,1)S(1)}, u32[]{:S(2)}, u32[]{:S(2)}) %collective-permute-start.9) | collective-permute-done | bytes 294944 | tf_op jit(solution)/shard_map/ppermute | solution.py:495
  59.1 1.1 %join.7 = (bf16[384,768]{1,0:T(8,128)(2,1)}, bf16[384,768]{1,0:T(8,128)(2,1)}) custom-call(bf16[192,768]{1,0:T(8,128)(2,1)S(1)} %get-tuple-element.28.refs_0_, bf16[192,768]{1,0:T(8,128)(2,1)S(1)} %get-tuple-element.29.refs_1_, bf16[192,768]{1,0:T(8,128)(2,1)S(1)} %collective-permute-done.9.refs_2_, bf16[192,768]{1,0:T(8,128)(2,1)S(1)} %collective-permute-done.10.refs_3_), custom_call_target="tpu_custom_call" | custom-call | flops 1000000 | bytes 1000 | tf_op jit(solution)/shard_map/join/pallas_call | solution.py:511
  60.2 1.9 %collective-permute-start.13 = (bf16[384,768]{1,0:T(8,128)(2,1)}, bf16[384,768]{1,0:T(8,128)(2,1)}, u32[]{:S(2)}, u32[]{:S(2)}) collective-permute-start(bf16[384,768]{1,0:T(8,128)(2,1)} %get-tuple-element.31.own1_ref), channel_id=1, source_target_pairs={{0,2},{1,3},{2,4},{3,5},{4,6},{5,7},{6,0},{7,1},{8,10},{9,11},{10,... | collective-permute-start | bytes 1769480 | tf_op jit(solution)/shard_map/ppermute | solution.py:491
  62.1 2.0 %collective-permute-start.15 = (bf16[384,768]{1,0:T(8,128)(2,1)}, bf16[384,768]{1,0:T(8,128)(2,1)}, u32[]{:S(2)}, u32[]{:S(2)}) collective-permute-start(bf16[384,768]{1,0:T(8,128)(2,1)} %get-tuple-element.30.own0_ref), channel_id=1, source_target_pairs={{0,24},{1,25},{2,26},{3,27},{4,28},{5,29},{6,30},{7,31},{8,0},{9,1... | collective-permute-start | bytes 1769480 | tf_op jit(solution)/shard_map/ppermute | solution.py:491
  64.1 0.8 copy-done.11
  64.9 1.4 %collective-permute-start.16 = (bf16[384,768]{1,0:T(8,128)(2,1)}, bf16[384,768]{1,0:T(8,128)(2,1)}, u32[]{:S(2)}, u32[]{:S(2)}) collective-permute-start(bf16[384,768]{1,0:T(8,128)(2,1)} %get-tuple-element.31.own1_ref), channel_id=1, source_target_pairs={{0,6},{1,7},{2,0},{3,1},{4,2},{5,3},{6,4},{7,5},{8,14},{9,15},{10,... | collective-permute-start | bytes 1769480 | tf_op jit(solution)/shard_map/ppermute | solution.py:491
  66.3 1.3 %copy-done.4 = bf16[768,768]{1,0:T(8,128)(2,1)S(1)} copy-done((bf16[768,768]{1,0:T(8,128)(2,1)S(1)}, bf16[768,768]{1,0:T(8,128)(2,1)}, u32[]{:S(2)}) %copy-start.4) | copy-done | bytes 1179672
  67.6 1.6 %queries.1.absorbed_ref = bf16[2,768,768]{2,1,0:T(8,128)(2,1)S(1)} custom-call(bf16[2,48,768]{2,1,0:T(8,128)(2,1)S(1)} %copy-done.2, bf16[768,768]{1,0:T(8,128)(2,1)S(1)} %copy-done.4, bf16[768,1536]{1,0:T(8,128)(2,1)S(1)} %copy-done, bf16[2,48,768]{2,1,0:T(8,128)(2,1)S(1)} %copy-done.2), custom_call_target="tpu_custom_call" | custom-call | flops 1000000 | bytes 1000 | tf_op jit(solution)/shard_map/queries/pallas_call | solution.py:278
  69.2 1.1 %collective-permute-done.11.low0_ref = bf16[384,768]{1,0:T(8,128)(2,1)} collective-permute-done((bf16[384,768]{1,0:T(8,128)(2,1)}, bf16[384,768]{1,0:T(8,128)(2,1)}, u32[]{:S(2)}, u32[]{:S(2)}) %collective-permute-start.11) | collective-permute-done | bytes 589856 | tf_op jit(solution)/shard_map/ppermute | solution.py:491
  70.4 0.1 collective-permute-start.12
  70.5 1.2 %collective-permute-done.13.low1_ref = bf16[384,768]{1,0:T(8,128)(2,1)} collective-permute-done((bf16[384,768]{1,0:T(8,128)(2,1)}, bf16[384,768]{1,0:T(8,128)(2,1)}, u32[]{:S(2)}, u32[]{:S(2)}) %collective-permute-start.13) | collective-permute-done | bytes 589856 | tf_op jit(solution)/shard_map/ppermute | solution.py:491
  71.7 0.7 collective-permute-start.14
  72.4 2.2 %reorder.1 = (bf16[16,48,1536]{2,1,0:T(8,128)(2,1)S(1)}, bf16[16,48,1536]{2,1,0:T(8,128)(2,1)S(1)}) custom-call(bf16[2,2,48,1536]{3,2,1,0:T(8,128)(2,1)S(1)} %bitcast.23, bf16[2,2,48,1536]{3,2,1,0:T(8,128)(2,1)} %bitcast.6.near_far_ref, bf16[2,2,48,1536]{3,2,1,0:T(8,128)(2,1)S(1)} %bitcast.29, bf16[2,2,48,1536]{3,2,1,0:T(8,128)(2,1)} %bitcast.8.other_far_ref), custom_call_target="tpu_custom_call" | custom-call | flops 4000000000 | bytes 1000 | tf_op jit(solution)/shard_map/reorder/pallas_call | solution.py:317
  74.6 3.5 %collective-permute-done.15.high0_ref = bf16[384,768]{1,0:T(8,128)(2,1)} collective-permute-done((bf16[384,768]{1,0:T(8,128)(2,1)}, bf16[384,768]{1,0:T(8,128)(2,1)}, u32[]{:S(2)}, u32[]{:S(2)}) %collective-permute-start.15) | collective-permute-done | bytes 589856 | tf_op jit(solution)/shard_map/ppermute | solution.py:491
  78.1 2.6 %collective-permute-done.16.high1_ref = bf16[384,768]{1,0:T(8,128)(2,1)} collective-permute-done((bf16[384,768]{1,0:T(8,128)(2,1)}, bf16[384,768]{1,0:T(8,128)(2,1)}, u32[]{:S(2)}, u32[]{:S(2)}) %collective-permute-start.16) | collective-permute-done | bytes 589856 | tf_op jit(solution)/shard_map/ppermute | solution.py:491
  80.7 0.0 copy-start.6
  80.7 0.0 copy-start.7
  80.8 0.0 copy-start.8
  80.8 0.0 copy-start.9
  80.8 0.0 copy-start.10
  80.8 10.9 %early.1 = (f32[2,768,768]{2,1,0:T(8,128)S(1)}, f32[2,768,128]{2,1,0:T(8,128)S(1)}, f32[2,768,128]{2,1,0:T(8,128)S(1)}) custom-call(bf16[2,768,768]{2,1,0:T(8,128)(2,1)S(1)} %queries.1.absorbed_ref, bf16[16,48,1536]{2,1,0:T(8,128)(2,1)S(1)} %get-tuple-element.24.bias0_ref, bf16[16,48,1536]{2,1,0:T(8,128)(2,1)S(1)} %get-tuple-element.25.bias1_ref, ...), custom_call_target="tpu_custom_call" | custom-call | flops 8000000000 | bytes 1000 | tf_op jit(solution)/shard_map/early/pallas_call | solution.py:382
  91.8 8.9 %late.1 = (bf16[2,384,128]{2,1,0:T(8,128)(2,1)}, bf16[2,48,768]{2,1,0:T(8,128)(2,1)}, bf16[2,48,128]{2,1,0:T(8,128)(2,1)S(1)}) custom-call(bf16[2,768,768]{2,1,0:T(8,128)(2,1)S(1)} %queries.1.absorbed_ref, bf16[16,48,1536]{2,1,0:T(8,128)(2,1)S(1)} %get-tuple-element.24.bias0_ref, bf16[16,48,1536]{2,1,0:T(8,128)(2,1)S(1)} %get-tuple-element.25.bias1_ref, ...), custom_call_target="tpu_custom_call" | custom-call | flops 5000000000 | bytes 1000 | tf_op jit(solution)/shard_map/late/pallas_call | solution.py:470
  100.7 4.2 %collective-permute-start.17 = (bf16[2,128]{1,0:T(2,128)(2,1)S(1)}, bf16[2,128]{1,0:T(2,128)(2,1)S(1)}, u32[]{:S(2)}, u32[]{:S(2)}) collective-permute-start(bf16[2,128]{1,0:T(2,128)(2,1)S(1)} %bitcast.34), channel_id=1, source_target_pairs={{0,1},{1,2},{2,3},{3,4},{4,5},{5,6},{6,7},{7,8},{8,9},{9,10},{10,1... | collective-permute-start | bytes 1544 | tf_op jit(solution)/shard_map/ppermute | solution.py:609
  105.0 5.6 %collective-permute-done.17 = bf16[2,128]{1,0:T(2,128)(2,1)S(1)} collective-permute-done((bf16[2,128]{1,0:T(2,128)(2,1)S(1)}, bf16[2,128]{1,0:T(2,128)(2,1)S(1)}, u32[]{:S(2)}, u32[]{:S(2)}) %collective-permute-start.17) | collective-permute-done | bytes 544 | tf_op jit(solution)/shard_map/ppermute | solution.py:609
  110.6 1.4 %fusion = bf16[2,384,128]{2,1,0:T(8,128)(2,1)} fusion(bf16[2,384,128]{2,1,0:T(8,128)(2,1)} %get-tuple-element.37, f32[2,128]{1,0:T(2,128)S(1)} %convert_element_type.11, pred[8]{0:T(512)(128)(4,1)S(1)} %slice_compare_fusion), kind=kLoop, calls=%fused_computation.5 | loop fusion | flops 8192 | bytes 9224 | tf_op jit(solution)/shard_map/dynamic_update_slice | solution.py:613
  (40 shorter events, 0.1 us)
Async XLA Ops:
  2.8 23.3 %collective-permute-start.1 = (bf16[304,128]{1,0:T(8,128)(2,1)}, bf16[304,128]{1,0:T(8,128)(2,1)S(1)}, u32[]{:S(2)}, u32[]{:S(2)}) collective-permute-start(bf16[304,128]{1,0:T(8,128)(2,1)} %get-tuple-element.22), channel_id=1, source_target_pairs={{1,0},{2,1},{3,2},{4,3},{5,4},{6,5},{7,6},{8,7},{9,8},{10,9},{11,1... | collective-permute-start | bytes 233480 | tf_op jit(solution)/shard_map/ppermute | solution.py:575
  9.1 30.9 %collective-permute-start.2 = (bf16[96,1536]{1,0:T(8,128)(2,1)}, bf16[96,1536]{1,0:T(8,128)(2,1)S(1)}, u32[]{:S(2)}, u32[]{:S(2)}) collective-permute-start(bf16[96,1536]{1,0:T(8,128)(2,1)} %bitcast.24), channel_id=1, source_target_pairs={{0,64},{32,96},{64,0},{96,32},{128,192},{160,224},{192,128},{224,1... | collective-permute-start | bytes 884744 | tf_op jit(solution)/shard_map/ppermute | solution.py:495
  12.5 13.7 %collective-permute-start = (bf16[96,128]{1,0:T(8,128)(2,1)}, bf16[96,128]{1,0:T(8,128)(2,1)S(1)}, u32[]{:S(2)}, u32[]{:S(2)}) collective-permute-start(bf16[96,128]{1,0:T(8,128)(2,1)} %get-tuple-element.21), channel_id=1, source_target_pairs={{0,1},{1,2},{2,3},{3,4},{4,5},{5,6},{6,7},{7,8},{8,9},{9,10},{10,1... | collective-permute-start | bytes 73736 | tf_op jit(solution)/shard_map/ppermute | solution.py:576
  26.2 0.6 copy-start.14
  26.2 0.6 copy-start.13
  26.8 39.5 %copy-start = (bf16[768,1536]{1,0:T(8,128)(2,1)S(1)}, bf16[768,1536]{1,0:T(8,128)(2,1)}, u32[]{:S(2)}) copy-start(bf16[768,1536]{1,0:T(8,128)(2,1)} %keyval_ref.3) | copy-start | bytes 7077892
  34.6 31.7 %copy-start.2 = (bf16[2,48,768]{2,1,0:T(8,128)(2,1)S(1)}, bf16[2,48,768]{2,1,0:T(8,128)(2,1)}, u32[]{:S(2)}) copy-start(bf16[2,48,768]{2,1,0:T(8,128)(2,1)} %get-tuple-element.23.norm_ref.after_hbm) | copy-start | bytes 442372
  34.6 5.4 %collective-permute-start.3 = (bf16[2,48,768]{2,1,0:T(8,128)(2,1)}, bf16[2,48,768]{2,1,0:T(8,128)(2,1)S(1)}, u32[]{:S(2)}, u32[]{:S(2)}) collective-permute-start(bf16[2,48,768]{2,1,0:T(8,128)(2,1)} %get-tuple-element.23.norm_ref.after_hbm), channel_id=1, source_target_pairs={{0,1},{1,0},{2,3},{3,2},{4,5},{5,4},{6,7},{7,6},{8,9},{9,8},{10,11... | collective-permute-start | bytes 442376 | tf_op jit(solution)/shard_map/ppermute | solution.py:495
  40.0 1.0 copy-start.5
  41.1 21.0 %collective-permute-start.4 = (bf16[192,1536]{1,0:T(8,128)(2,1)S(1)}, bf16[192,1536]{1,0:T(8,128)(2,1)}, u32[]{:S(2)}, u32[]{:S(2)}) collective-permute-start(bf16[192,1536]{1,0:T(8,128)(2,1)S(1)} %join.4), channel_id=1, source_target_pairs={{0,128},{32,160},{64,192},{96,224},{128,0},{160,32},{192,64},{224,... | collective-permute-start | bytes 1769480 | tf_op jit(solution)/shard_map/ppermute | solution.py:495
  41.2 5.2 %collective-permute-start.7 = (bf16[96,768]{1,0:T(8,128)(2,1)S(1)}, bf16[96,768]{1,0:T(8,128)(2,1)S(1)}, u32[]{:S(2)}, u32[]{:S(2)}) collective-permute-start(bf16[96,768]{1,0:T(8,128)(2,1)S(1)} %get-tuple-element.26.refs_0_), channel_id=1, source_target_pairs={{0,2},{1,3},{2,0},{3,1},{4,6},{5,7},{6,4},{7,5},{8,10},{9,11},{10,... | collective-permute-start | bytes 442376 | tf_op jit(solution)/shard_map/ppermute | solution.py:495
  41.4 5.5 %collective-permute-start.8 = (bf16[96,768]{1,0:T(8,128)(2,1)S(1)}, bf16[96,768]{1,0:T(8,128)(2,1)S(1)}, u32[]{:S(2)}, u32[]{:S(2)}) collective-permute-start(bf16[96,768]{1,0:T(8,128)(2,1)S(1)} %get-tuple-element.27.refs_1_), channel_id=1, source_target_pairs={{0,8},{1,9},{2,10},{3,11},{4,12},{5,13},{6,14},{7,15},{8,0},{9,1},... | collective-permute-start | bytes 442376 | tf_op jit(solution)/shard_map/ppermute | solution.py:495
  46.9 8.5 %collective-permute-start.10 = (bf16[192,768]{1,0:T(8,128)(2,1)S(1)}, bf16[192,768]{1,0:T(8,128)(2,1)S(1)}, u32[]{:S(2)}, u32[]{:S(2)}) collective-permute-start(bf16[192,768]{1,0:T(8,128)(2,1)S(1)} %get-tuple-element.29.refs_1_), channel_id=1, source_target_pairs={{0,16},{1,17},{2,18},{3,19},{4,20},{5,21},{6,22},{7,23},{8,24},{9,... | collective-permute-start | bytes 884744 | tf_op jit(solution)/shard_map/ppermute | solution.py:495
  50.7 8.3 %collective-permute-start.9 = (bf16[192,768]{1,0:T(8,128)(2,1)S(1)}, bf16[192,768]{1,0:T(8,128)(2,1)S(1)}, u32[]{:S(2)}, u32[]{:S(2)}) collective-permute-start(bf16[192,768]{1,0:T(8,128)(2,1)S(1)} %get-tuple-element.28.refs_0_), channel_id=1, source_target_pairs={{0,4},{1,5},{2,6},{3,7},{4,0},{5,1},{6,2},{7,3},{8,12},{9,13},{10,... | collective-permute-start | bytes 884744 | tf_op jit(solution)/shard_map/ppermute | solution.py:495
  50.7 13.3 %collective-permute-start.5 = (bf16[192,1536]{1,0:T(8,128)(2,1)S(1)}, bf16[192,1536]{1,0:T(8,128)(2,1)S(1)}, u32[]{:S(2)}, u32[]{:S(2)}) collective-permute-start(bf16[192,1536]{1,0:T(8,128)(2,1)S(1)} %join.4), channel_id=1, source_target_pairs={{0,32},{32,0},{64,96},{96,64},{128,160},{160,128},{192,224},{224,1... | collective-permute-start | bytes 1769480 | tf_op jit(solution)/shard_map/ppermute | solution.py:495
  60.2 10.2 %collective-permute-start.11 = (bf16[384,768]{1,0:T(8,128)(2,1)}, bf16[384,768]{1,0:T(8,128)(2,1)}, u32[]{:S(2)}, u32[]{:S(2)}) collective-permute-start(bf16[384,768]{1,0:T(8,128)(2,1)} %get-tuple-element.30.own0_ref), channel_id=1, source_target_pairs={{0,8},{1,9},{2,10},{3,11},{4,12},{5,13},{6,14},{7,15},{8,16},{9,17... | collective-permute-start | bytes 1769480 | tf_op jit(solution)/shard_map/ppermute | solution.py:491
  60.2 11.5 %collective-permute-start.13 = (bf16[384,768]{1,0:T(8,128)(2,1)}, bf16[384,768]{1,0:T(8,128)(2,1)}, u32[]{:S(2)}, u32[]{:S(2)}) collective-permute-start(bf16[384,768]{1,0:T(8,128)(2,1)} %get-tuple-element.31.own1_ref), channel_id=1, source_target_pairs={{0,2},{1,3},{2,4},{3,5},{4,6},{5,7},{6,0},{7,1},{8,10},{9,11},{10,... | collective-permute-start | bytes 1769480 | tf_op jit(solution)/shard_map/ppermute | solution.py:491
  62.1 10.3 %collective-permute-start.6 = (bf16[192,1536]{1,0:T(8,128)(2,1)}, bf16[192,1536]{1,0:T(8,128)(2,1)}, u32[]{:S(2)}, u32[]{:S(2)}) collective-permute-start(bf16[192,1536]{1,0:T(8,128)(2,1)} %collective-permute-done.4), channel_id=1, source_target_pairs={{0,32},{32,0},{64,96},{96,64},{128,160},{160,128},{192,224},{224,1... | collective-permute-start | bytes 1769480 | tf_op jit(solution)/shard_map/ppermute | solution.py:495
  62.1 16.1 %collective-permute-start.15 = (bf16[384,768]{1,0:T(8,128)(2,1)}, bf16[384,768]{1,0:T(8,128)(2,1)}, u32[]{:S(2)}, u32[]{:S(2)}) collective-permute-start(bf16[384,768]{1,0:T(8,128)(2,1)} %get-tuple-element.30.own0_ref), channel_id=1, source_target_pairs={{0,24},{1,25},{2,26},{3,27},{4,28},{5,29},{6,30},{7,31},{8,0},{9,1... | collective-permute-start | bytes 1769480 | tf_op jit(solution)/shard_map/ppermute | solution.py:491
  64.1 0.8 copy-start.11
  64.9 15.8 %collective-permute-start.16 = (bf16[384,768]{1,0:T(8,128)(2,1)}, bf16[384,768]{1,0:T(8,128)(2,1)}, u32[]{:S(2)}, u32[]{:S(2)}) collective-permute-start(bf16[384,768]{1,0:T(8,128)(2,1)} %get-tuple-element.31.own1_ref), channel_id=1, source_target_pairs={{0,6},{1,7},{2,0},{3,1},{4,2},{5,3},{6,4},{7,5},{8,14},{9,15},{10,... | collective-permute-start | bytes 1769480 | tf_op jit(solution)/shard_map/ppermute | solution.py:491
  66.3 1.3 %copy-start.4 = (bf16[768,768]{1,0:T(8,128)(2,1)S(1)}, bf16[768,768]{1,0:T(8,128)(2,1)}, u32[]{:S(2)}) copy-start(bf16[768,768]{1,0:T(8,128)(2,1)} %query_ref.1) | copy-start | bytes 3538948
  67.6 4.8 %copy-start.12 = (bf16[192,1536]{1,0:T(8,128)(2,1)S(1)}, bf16[192,1536]{1,0:T(8,128)(2,1)}, u32[]{:S(2)}) copy-start(bf16[192,1536]{1,0:T(8,128)(2,1)} %copy-done.11) | copy-start | bytes 1769476
  70.4 21.3 %collective-permute-start.12 = (bf16[384,768]{1,0:T(8,128)(2,1)}, bf16[384,768]{1,0:T(8,128)(2,1)S(1)}, u32[]{:S(2)}, u32[]{:S(2)}) collective-permute-start(bf16[384,768]{1,0:T(8,128)(2,1)} %collective-permute-done.11.low0_ref), channel_id=1, source_target_pairs={{0,8},{1,9},{2,10},{3,11},{4,12},{5,13},{6,14},{7,15},{8,16},{9,17... | collective-permute-start | bytes 1769480 | tf_op jit(solution)/shard_map/ppermute | solution.py:491
  71.7 20.0 %collective-permute-start.14 = (bf16[384,768]{1,0:T(8,128)(2,1)}, bf16[384,768]{1,0:T(8,128)(2,1)S(1)}, u32[]{:S(2)}, u32[]{:S(2)}) collective-permute-start(bf16[384,768]{1,0:T(8,128)(2,1)} %collective-permute-done.13.low1_ref), channel_id=1, source_target_pairs={{0,2},{1,3},{2,4},{3,5},{4,6},{5,7},{6,0},{7,1},{8,10},{9,11},{10,... | collective-permute-start | bytes 1769480 | tf_op jit(solution)/shard_map/ppermute | solution.py:491
  80.7 11.0 %slice-start = ((s8[4718592]{0:T(1024)(128)(4,1)}), s8[4194304]{0:T(1024)(128)(4,1)S(1)}, s32[]{:S(2)}) async-start(s8[4718592]{0:T(1024)(128)(4,1)} %bitcast.21), calls=%async_computation | async-start | bytes 8388608
  80.7 11.0 %slice-start.1 = ((s8[4718592]{0:T(1024)(128)(4,1)}), s8[524288]{0:T(1024)(128)(4,1)S(1)}, s32[]{:S(2)}) async-start(s8[4718592]{0:T(1024)(128)(4,1)} %bitcast.21), calls=%async_computation.1 | async-start | bytes 1048576
  80.7 11.0 %copy-start.1 = (bf16[1536,768]{1,0:T(8,128)(2,1)S(1)}, bf16[1536,768]{1,0:T(8,128)(2,1)}, u32[]{:S(2)}) copy-start(bf16[1536,768]{1,0:T(8,128)(2,1)} %down_ref.1) | copy-start | bytes 7077892
  80.7 11.0 %copy-start.3 = (bf16[768,768]{1,0:T(8,128)(2,1)S(1)}, bf16[768,768]{1,0:T(8,128)(2,1)}, u32[]{:S(2)}) copy-start(bf16[768,768]{1,0:T(8,128)(2,1)} %output_ref.1) | copy-start | bytes 3538948
  80.7 11.0 %copy-start.6 = (bf16[768,128]{1,0:T(8,128)(2,1)S(1)}, bf16[768,128]{1,0:T(8,128)(2,1)}, u32[]{:S(2)}) copy-start(bf16[768,128]{1,0:T(8,128)(2,1)} %back_ref.1) | copy-start | bytes 589828
  80.7 11.0 %copy-start.7 = (bf16[2,384,128]{2,1,0:T(8,128)(2,1)S(1)}, bf16[2,384,128]{2,1,0:T(8,128)(2,1)}, u32[]{:S(2)}) copy-start(bf16[2,384,128]{2,1,0:T(8,128)(2,1)} %get-tuple-element.36.mid_ref) | copy-start | bytes 589828
  80.8 11.0 %copy-start.8 = (bf16[2,48,768]{2,1,0:T(8,128)(2,1)S(1)}, bf16[2,48,768]{2,1,0:T(8,128)(2,1)}, u32[]{:S(2)}) copy-start(bf16[2,48,768]{2,1,0:T(8,128)(2,1)} %get-tuple-element.35.tokact_ref) | copy-start | bytes 442372
  80.8 11.0 %copy-start.9 = (s32[384]{0:T(512)S(1)}, s32[384]{0:T(512)}, u32[]{:S(2)}) copy-start(s32[384]{0:T(512)} %param.26) | copy-start | bytes 4612
  80.8 11.0 %copy-start.10 = (f32[768]{0:T(1024)S(1)}, f32[768]{0:T(1024)}, u32[]{:S(2)}) copy-start(f32[768]{0:T(1024)} %param.34) | copy-start | bytes 9220
  100.7 9.9 %collective-permute-start.17 = (bf16[2,128]{1,0:T(2,128)(2,1)S(1)}, bf16[2,128]{1,0:T(2,128)(2,1)S(1)}, u32[]{:S(2)}, u32[]{:S(2)}) collective-permute-start(bf16[2,128]{1,0:T(2,128)(2,1)S(1)} %bitcast.34), channel_id=1, source_target_pairs={{0,1},{1,2},{2,3},{3,4},{4,5},{5,6},{6,7},{7,8},{8,9},{9,10},{10,1... | collective-permute-start | bytes 1544 | tf_op jit(solution)/shard_map/ppermute | solution.py:609

commit v8 on v7

--- a/solution.py
+++ b/solution.py
@@ -519,17 +519,19 @@
     )(*own, *other, *after)
 
 
-def spread(norm):
+def spread(norm, bias):
     other = exchanged(norm, "seq", 0)
+    heads = all_heads(bias, other)
     lines = joined([norm[0], norm[1]], [other[0], other[1]], "seq", (0, 0))
-    for bits in ((1, 3), (2, 4)):
-        lines = joined(lines, [exchanged(v, "seq", b) for v, b in zip(lines, bits)], "seq", bits)
+    for bits, after in (((1, 3), ()), ((2, 4), (heads[2],))):
+        turned = [exchanged(v, "seq", b) for v, b in zip(lines, bits)]
+        lines = joined(lines, turned, "seq", bits, after)
     near, far = [], []
     for value, dx, dy in ((lines[0], 1, 0), (lines[1], 0, 1)):
         low = shifted(value, dx, dy)
         near.append((value, low, shifted(value, -dx, -dy)))
         far.append(shifted(low, dx, dy))
-    return near, far, other
+    return near, far, heads
 
 
 def all_heads(bias, ready):
@@ -590,9 +592,9 @@
         atom_output,
         gather_weight,
     )
-    near, far, ready = spread(token_norm)
+    near, far, heads = spread(token_norm, pair_bias)
     absorbed = run_queries(token_norm, token_query, token_keyval, token_norm)
-    bias, turned = run_reorder(all_heads(pair_bias, ready))
+    bias, turned = run_reorder(heads)
     early = run_early(absorbed, bias, turned, near[0] + near[1])
     atom_out, token_out, back_rows = run_late(
         absorbed,

time: 112 us -> 119 us (1.062)
  the two profiles are of different devices: /device:TPU:2 before, /device:TPU:6 now
where the time goes in v8:
time: 119 us
  waiting for transfers between devices  52.5 us (44%)
  Pallas kernels  34.8 us (29%)
  starting transfers between devices  25.3 us (21%)
  local copies, waits for them, and re-layouts  4.03 us (3%)
  other arithmetic  1.36 us (1%)
    ppermute x9, waiting for transfers between devices, exchanged(): lax.ppermute(value, axis, [(t, t ^ 1 << bit) for t in range(lax.axis_size...  27.5 us
    ppermute x1, waiting for transfers between devices, per_device(): before = lax.ppermute(last, 'seq', to_next)  11.8 us
    pallas_call x1, Pallas kernels, run_early(): pl.pallas_call(early_kernel, out_shape=(jax.ShapeDtypeStruct((samples, ro...  10.9 us
    pallas_call x1, Pallas kernels, run_late(): pl.pallas_call(late_kernel, out_shape=(jax.ShapeDtypeStruct(mid.shape, BF...  8.91 us
    ppermute x6, starting transfers between devices, shifted(): return lax.ppermute(value, 'seq', pairs)  8.87 us
    pallas_call x1, Pallas kernels, run_atoms(): pl.pallas_call(atom_kernel, out_shape=(jax.ShapeDtypeStruct((samples, ato...  7.64 us
    ppermute x6, waiting for transfers between devices, shifted(): return lax.ppermute(value, 'seq', pairs)  6.7 us
    ppermute x1, starting transfers between devices, per_device(): after = lax.ppermute(first, 'seq', to_previous)  6.54 us
  transfers between devices with their start and end apart: 18, of which 9 were waited for; matrix products, arithmetic and copies ran while one was open for 1% of the time, Pallas kernels for 20%

profile of v8, /device:TPU:6, one launch (start us, length us, event | category | flops | bytes accessed | tf_op | source)
XLA Modules:
  0.0 119.0 jit_solution(12491469892797158379)
XLA Ops:
  0.6 2.2 %pack.1 = (bf16[304,128]{1,0:T(8,128)(2,1)}, bf16[96,128]{1,0:T(8,128)(2,1)}) custom-call(s32[2,12]{1,0:T(2,128)} %bitcast.32, bf16[2,384,128]{2,1,0:T(8,128)(2,1)} %act_hbm.3, bf16[4,12,32,128]{3,2,1,0:T(8,128)(2,1)} %bias_hbm.3), custom_call_target="tpu_custom_call" | custom-call | tf_op jit(solution)/shard_map/pack/pallas_call | solution.py:87
  2.8 6.5 %collective-permute-start.1 = (bf16[304,128]{1,0:T(8,128)(2,1)}, bf16[304,128]{1,0:T(8,128)(2,1)S(1)}, u32[]{:S(2)}, u32[]{:S(2)}) collective-permute-start(bf16[304,128]{1,0:T(8,128)(2,1)} %get-tuple-element.22), channel_id=1, source_target_pairs={{1,0},{2,1},{3,2},{4,3},{5,4},{6,5},{7,6},{8,7},{9,8},{10,9},{11,1... | collective-permute-start | bytes 233480 | tf_op jit(solution)/shard_map/ppermute | solution.py:577
  9.4 3.4 %collective-permute-start.2 = (bf16[96,1536]{1,0:T(8,128)(2,1)}, bf16[96,1536]{1,0:T(8,128)(2,1)S(1)}, u32[]{:S(2)}, u32[]{:S(2)}) collective-permute-start(bf16[96,1536]{1,0:T(8,128)(2,1)} %bitcast.26), channel_id=1, source_target_pairs={{0,64},{32,96},{64,0},{96,32},{128,192},{160,224},{192,128},{224,1... | collective-permute-start | bytes 884744 | tf_op jit(solution)/shard_map/ppermute | solution.py:495
  12.8 1.9 %collective-permute-start = (bf16[96,128]{1,0:T(8,128)(2,1)}, bf16[96,128]{1,0:T(8,128)(2,1)S(1)}, u32[]{:S(2)}, u32[]{:S(2)}) collective-permute-start(bf16[96,128]{1,0:T(8,128)(2,1)} %get-tuple-element.21), channel_id=1, source_target_pairs={{0,1},{1,2},{2,3},{3,4},{4,5},{5,6},{6,7},{7,8},{8,9},{9,10},{10,1... | collective-permute-start | bytes 73736 | tf_op jit(solution)/shard_map/ppermute | solution.py:578
  14.7 11.8 %collective-permute-done.before_ref = bf16[96,128]{1,0:T(8,128)(2,1)S(1)} collective-permute-done((bf16[96,128]{1,0:T(8,128)(2,1)}, bf16[96,128]{1,0:T(8,128)(2,1)S(1)}, u32[]{:S(2)}, u32[]{:S(2)}) %collective-permute-start) | collective-permute-done | bytes 24608 | tf_op jit(solution)/shard_map/ppermute | solution.py:578
  26.5 0.6 copy-done.14
  27.1 0.0 copy-done.13
  27.1 7.6 %atoms.1 = (bf16[2,384,128]{2,1,0:T(8,128)(2,1)}, bf16[2,48,768]{2,1,0:T(8,128)(2,1)}, bf16[2,48,768]{2,1,0:T(8,128)(2,1)}) custom-call(s32[2,12]{1,0:T(2,128)} %bitcast.33, s32[48]{0:T(128)} %count_ref.1, bf16[96,128]{1,0:T(8,128)(2,1)} %copy-done.14, bf16[304,128]{1,0:T(8,128)(2,1)} %copy-done.13, f32[1,128]{1,0:T(1,128)} %bitcast.34, s32[3,128]{1,0:T(4,128)} %bitcast.28, ...), custom_call_target="tpu_custom_call" | custom-call | flops 1000000 | bytes 1000 | tf_op jit(solution)/shard_map/atoms/pallas_call | solution.py:239
  34.7 0.0 copy-start
  34.8 0.1 collective-permute-start.3
  34.9 1.1 slice_bitcast_fusion.2
  35.9 4.3 %collective-permute-done.3.refs_2_ = bf16[2,48,768]{2,1,0:T(8,128)(2,1)S(1)} collective-permute-done((bf16[2,48,768]{2,1,0:T(8,128)(2,1)}, bf16[2,48,768]{2,1,0:T(8,128)(2,1)S(1)}, u32[]{:S(2)}, u32[]{:S(2)}) %collective-permute-start.3) | collective-permute-done | bytes 147488 | tf_op jit(solution)/shard_map/ppermute | solution.py:495
  40.2 1.0 copy-done.7
  41.2 0.1 join.4
  41.3 0.1 collective-permute-start.5
  41.4 0.1 collective-permute-start.4
  41.5 0.1 collective-permute-start.7
  41.6 0.7 collective-permute-start.8
  42.3 5.5 %collective-permute-done.7.refs_2_ = bf16[96,768]{1,0:T(8,128)(2,1)S(1)} collective-permute-done((bf16[96,768]{1,0:T(8,128)(2,1)S(1)}, bf16[96,768]{1,0:T(8,128)(2,1)S(1)}, u32[]{:S(2)}, u32[]{:S(2)}) %collective-permute-start.7) | collective-permute-done | bytes 147488 | tf_op jit(solution)/shard_map/ppermute | solution.py:495
  47.7 0.1 collective-permute-done.8.refs_3_
  47.9 0.1 join.6
  47.9 1.2 %collective-permute-start.10 = (bf16[192,768]{1,0:T(8,128)(2,1)S(1)}, bf16[192,768]{1,0:T(8,128)(2,1)S(1)}, u32[]{:S(2)}, u32[]{:S(2)}) collective-permute-start(bf16[192,768]{1,0:T(8,128)(2,1)S(1)} %get-tuple-element.29.refs_1_), channel_id=1, source_target_pairs={{0,16},{1,17},{2,18},{3,19},{4,20},{5,21},{6,22},{7,23},{8,24},{9,... | collective-permute-start | bytes 884744 | tf_op jit(solution)/shard_map/ppermute | solution.py:495
  49.1 0.5 collective-permute-start.9
  49.6 8.4 %collective-permute-done.10.refs_3_ = bf16[192,768]{1,0:T(8,128)(2,1)S(1)} collective-permute-done((bf16[192,768]{1,0:T(8,128)(2,1)S(1)}, bf16[192,768]{1,0:T(8,128)(2,1)S(1)}, u32[]{:S(2)}, u32[]{:S(2)}) %collective-permute-start.10) | collective-permute-done | bytes 294944 | tf_op jit(solution)/shard_map/ppermute | solution.py:495
  58.0 0.8 collective-permute-done.9.refs_2_
  58.8 1.1 join.7
  59.9 2.1 %collective-permute-start.11 = (bf16[384,768]{1,0:T(8,128)(2,1)}, bf16[384,768]{1,0:T(8,128)(2,1)}, u32[]{:S(2)}, u32[]{:S(2)}) collective-permute-start(bf16[384,768]{1,0:T(8,128)(2,1)} %get-tuple-element.30.own0_ref), channel_id=1, source_target_pairs={{0,8},{1,9},{2,10},{3,11},{4,12},{5,13},{6,14},{7,15},{8,16},{9,17... | collective-permute-start | bytes 1769480 | tf_op jit(solution)/shard_map/ppermute | solution.py:491
  62.0 1.4 %collective-permute-start.13 = (bf16[384,768]{1,0:T(8,128)(2,1)}, bf16[384,768]{1,0:T(8,128)(2,1)}, u32[]{:S(2)}, u32[]{:S(2)}) collective-permute-start(bf16[384,768]{1,0:T(8,128)(2,1)} %get-tuple-element.31.own1_ref), channel_id=1, source_target_pairs={{0,2},{1,3},{2,4},{3,5},{4,6},{5,7},{6,0},{7,1},{8,10},{9,11},{10,... | collective-permute-start | bytes 1769480 | tf_op jit(solution)/shard_map/ppermute | solution.py:491
  63.5 8.5 %collective-permute-done.4 = bf16[192,1536]{1,0:T(8,128)(2,1)} collective-permute-done((bf16[192,1536]{1,0:T(8,128)(2,1)S(1)}, bf16[192,1536]{1,0:T(8,128)(2,1)}, u32[]{:S(2)}, u32[]{:S(2)}) %collective-permute-start.4) | collective-permute-done | bytes 589856 | tf_op jit(solution)/shard_map/ppermute | solution.py:495
  71.9 0.0 collective-permute-start.6
  72.0 0.5 collective-permute-start.15
  72.5 0.0 copy-start.4
  72.6 1.3 %copy-done.4 = bf16[768,768]{1,0:T(8,128)(2,1)S(1)} copy-done((bf16[768,768]{1,0:T(8,128)(2,1)S(1)}, bf16[768,768]{1,0:T(8,128)(2,1)}, u32[]{:S(2)}) %copy-start.4) | copy-done | bytes 1179672
  73.8 1.6 %queries.1.absorbed_ref = bf16[2,768,768]{2,1,0:T(8,128)(2,1)S(1)} custom-call(bf16[2,48,768]{2,1,0:T(8,128)(2,1)S(1)} %copy-done.2, bf16[768,768]{1,0:T(8,128)(2,1)S(1)} %copy-done.4, bf16[768,1536]{1,0:T(8,128)(2,1)S(1)} %copy-done, bf16[2,48,768]{2,1,0:T(8,128)(2,1)S(1)} %copy-done.2), custom_call_target="tpu_custom_call" | custom-call | flops 1000000 | bytes 1000 | tf_op jit(solution)/shard_map/queries/pallas_call | solution.py:278
  75.5 2.8 %collective-permute-start.12 = (bf16[384,768]{1,0:T(8,128)(2,1)}, bf16[384,768]{1,0:T(8,128)(2,1)S(1)}, u32[]{:S(2)}, u32[]{:S(2)}) collective-permute-start(bf16[384,768]{1,0:T(8,128)(2,1)} %collective-permute-done.11.low0_ref), channel_id=1, source_target_pairs={{0,8},{1,9},{2,10},{3,11},{4,12},{5,13},{6,14},{7,15},{8,16},{9,17... | collective-permute-start | bytes 1769480 | tf_op jit(solution)/shard_map/ppermute | solution.py:491
  78.3 2.0 %collective-permute-start.14 = (bf16[384,768]{1,0:T(8,128)(2,1)}, bf16[384,768]{1,0:T(8,128)(2,1)S(1)}, u32[]{:S(2)}, u32[]{:S(2)}) collective-permute-start(bf16[384,768]{1,0:T(8,128)(2,1)} %collective-permute-done.13.low1_ref), channel_id=1, source_target_pairs={{0,2},{1,3},{2,4},{3,5},{4,6},{5,7},{6,0},{7,1},{8,10},{9,11},{10,... | collective-permute-start | bytes 1769480 | tf_op jit(solution)/shard_map/ppermute | solution.py:491
  80.3 2.2 %reorder.1 = (bf16[16,48,1536]{2,1,0:T(8,128)(2,1)S(1)}, bf16[16,48,1536]{2,1,0:T(8,128)(2,1)S(1)}) custom-call(bf16[2,2,48,1536]{3,2,1,0:T(8,128)(2,1)S(1)} %bitcast.25, bf16[2,2,48,1536]{3,2,1,0:T(8,128)(2,1)} %bitcast.6.near_far_ref, bf16[2,2,48,1536]{3,2,1,0:T(8,128)(2,1)S(1)} %bitcast.24, bf16[2,2,48,1536]{3,2,1,0:T(8,128)(2,1)} %bitcast.8.other_far_ref), custom_call_target="tpu_custom_call" | custom-call | flops 4000000000 | bytes 1000 | tf_op jit(solution)/shard_map/reorder/pallas_call | solution.py:317
  82.5 6.7 %collective-permute-done.15.high0_ref = bf16[384,768]{1,0:T(8,128)(2,1)} collective-permute-done((bf16[384,768]{1,0:T(8,128)(2,1)}, bf16[384,768]{1,0:T(8,128)(2,1)}, u32[]{:S(2)}, u32[]{:S(2)}) %collective-permute-start.15) | collective-permute-done | bytes 589856 | tf_op jit(solution)/shard_map/ppermute | solution.py:491
  89.2 0.0 copy-start.3
  89.2 0.0 copy-start.8
  89.3 0.0 copy-start.9
  89.3 0.0 copy-start.10
  89.3 0.0 copy-start.11
  89.3 10.9 %early.1 = (f32[2,768,768]{2,1,0:T(8,128)S(1)}, f32[2,768,128]{2,1,0:T(8,128)S(1)}, f32[2,768,128]{2,1,0:T(8,128)S(1)}) custom-call(bf16[2,768,768]{2,1,0:T(8,128)(2,1)S(1)} %queries.1.absorbed_ref, bf16[16,48,1536]{2,1,0:T(8,128)(2,1)S(1)} %get-tuple-element.24.bias0_ref, bf16[16,48,1536]{2,1,0:T(8,128)(2,1)S(1)} %get-tuple-element.25.bias1_ref, ...), custom_call_target="tpu_custom_call" | custom-call | flops 8000000000 | bytes 1000 | tf_op jit(solution)/shard_map/early/pallas_call | solution.py:382
  100.3 8.9 %late.1 = (bf16[2,384,128]{2,1,0:T(8,128)(2,1)}, bf16[2,48,768]{2,1,0:T(8,128)(2,1)}, bf16[2,48,128]{2,1,0:T(8,128)(2,1)S(1)}) custom-call(bf16[2,768,768]{2,1,0:T(8,128)(2,1)S(1)} %queries.1.absorbed_ref, bf16[16,48,1536]{2,1,0:T(8,128)(2,1)S(1)} %get-tuple-element.24.bias0_ref, bf16[16,48,1536]{2,1,0:T(8,128)(2,1)S(1)} %get-tuple-element.25.bias1_ref, ...), custom_call_target="tpu_custom_call" | custom-call | flops 5000000000 | bytes 1000 | tf_op jit(solution)/shard_map/late/pallas_call | solution.py:470
  109.2 1.9 %collective-permute-start.17 = (bf16[2,128]{1,0:T(2,128)(2,1)S(1)}, bf16[2,128]{1,0:T(2,128)(2,1)S(1)}, u32[]{:S(2)}, u32[]{:S(2)}) collective-permute-start(bf16[2,128]{1,0:T(2,128)(2,1)S(1)} %bitcast.35), channel_id=1, source_target_pairs={{0,1},{1,2},{2,3},{3,4},{4,5},{5,6},{6,7},{7,8},{8,9},{9,10},{10,1... | collective-permute-start | bytes 1544 | tf_op jit(solution)/shard_map/ppermute | solution.py:611
  111.2 6.5 %collective-permute-done.17 = bf16[2,128]{1,0:T(2,128)(2,1)S(1)} collective-permute-done((bf16[2,128]{1,0:T(2,128)(2,1)S(1)}, bf16[2,128]{1,0:T(2,128)(2,1)S(1)}, u32[]{:S(2)}, u32[]{:S(2)}) %collective-permute-start.17) | collective-permute-done | bytes 544 | tf_op jit(solution)/shard_map/ppermute | solution.py:611
  117.7 1.4 %fusion = bf16[2,384,128]{2,1,0:T(8,128)(2,1)} fusion(bf16[2,384,128]{2,1,0:T(8,128)(2,1)} %get-tuple-element.37, f32[2,128]{1,0:T(2,128)S(1)} %convert_element_type.11, pred[8]{0:T(512)(128)(4,1)S(1)} %slice_compare_fusion), kind=kLoop, calls=%fused_computation.5 | loop fusion | flops 8192 | bytes 9224 | tf_op jit(solution)/shard_map/dynamic_update_slice | solution.py:615
  (40 shorter events, 0.1 us)
Async XLA Ops:
  2.8 23.6 %collective-permute-start.1 = (bf16[304,128]{1,0:T(8,128)(2,1)}, bf16[304,128]{1,0:T(8,128)(2,1)S(1)}, u32[]{:S(2)}, u32[]{:S(2)}) collective-permute-start(bf16[304,128]{1,0:T(8,128)(2,1)} %get-tuple-element.22), channel_id=1, source_target_pairs={{1,0},{2,1},{3,2},{4,3},{5,4},{6,5},{7,6},{8,7},{9,8},{10,9},{11,1... | collective-permute-start | bytes 233480 | tf_op jit(solution)/shard_map/ppermute | solution.py:577
  9.4 30.8 %collective-permute-start.2 = (bf16[96,1536]{1,0:T(8,128)(2,1)}, bf16[96,1536]{1,0:T(8,128)(2,1)S(1)}, u32[]{:S(2)}, u32[]{:S(2)}) collective-permute-start(bf16[96,1536]{1,0:T(8,128)(2,1)} %bitcast.26), channel_id=1, source_target_pairs={{0,64},{32,96},{64,0},{96,32},{128,192},{160,224},{192,128},{224,1... | collective-permute-start | bytes 884744 | tf_op jit(solution)/shard_map/ppermute | solution.py:495
  12.8 13.7 %collective-permute-start = (bf16[96,128]{1,0:T(8,128)(2,1)}, bf16[96,128]{1,0:T(8,128)(2,1)S(1)}, u32[]{:S(2)}, u32[]{:S(2)}) collective-permute-start(bf16[96,128]{1,0:T(8,128)(2,1)} %get-tuple-element.21), channel_id=1, source_target_pairs={{0,1},{1,2},{2,3},{3,4},{4,5},{5,6},{6,7},{7,8},{8,9},{9,10},{10,1... | collective-permute-start | bytes 73736 | tf_op jit(solution)/shard_map/ppermute | solution.py:578
  26.5 0.6 copy-start.14
  26.5 0.6 copy-start.13
  34.7 37.8 %copy-start = (bf16[768,1536]{1,0:T(8,128)(2,1)S(1)}, bf16[768,1536]{1,0:T(8,128)(2,1)}, u32[]{:S(2)}) copy-start(bf16[768,1536]{1,0:T(8,128)(2,1)} %keyval_ref.3) | copy-start | bytes 7077892
  34.7 37.8 %copy-start.2 = (bf16[2,48,768]{2,1,0:T(8,128)(2,1)S(1)}, bf16[2,48,768]{2,1,0:T(8,128)(2,1)}, u32[]{:S(2)}) copy-start(bf16[2,48,768]{2,1,0:T(8,128)(2,1)} %get-tuple-element.23.norm_ref.after_hbm) | copy-start | bytes 442372
  34.8 5.4 %collective-permute-start.3 = (bf16[2,48,768]{2,1,0:T(8,128)(2,1)}, bf16[2,48,768]{2,1,0:T(8,128)(2,1)S(1)}, u32[]{:S(2)}, u32[]{:S(2)}) collective-permute-start(bf16[2,48,768]{2,1,0:T(8,128)(2,1)} %get-tuple-element.23.norm_ref.after_hbm), channel_id=1, source_target_pairs={{0,1},{1,0},{2,3},{3,2},{4,5},{5,4},{6,7},{7,6},{8,9},{9,8},{10,11... | collective-permute-start | bytes 442376 | tf_op jit(solution)/shard_map/ppermute | solution.py:495
  40.2 1.0 copy-start.7
  41.2 17.6 %copy-start.5 = (bf16[192,1536]{1,0:T(8,128)(2,1)}, bf16[192,1536]{1,0:T(8,128)(2,1)S(1)}, u32[]{:S(2)}) copy-start(bf16[192,1536]{1,0:T(8,128)(2,1)S(1)} %join.4) | copy-start | bytes 1769476
  41.3 17.6 %collective-permute-start.5 = (bf16[192,1536]{1,0:T(8,128)(2,1)S(1)}, bf16[192,1536]{1,0:T(8,128)(2,1)S(1)}, u32[]{:S(2)}, u32[]{:S(2)}) collective-permute-start(bf16[192,1536]{1,0:T(8,128)(2,1)S(1)} %join.4), channel_id=1, source_target_pairs={{0,32},{32,0},{64,96},{96,64},{128,160},{160,128},{192,224},{224,1... | collective-permute-start | bytes 1769480 | tf_op jit(solution)/shard_map/ppermute | solution.py:495
  41.4 30.6 %collective-permute-start.4 = (bf16[192,1536]{1,0:T(8,128)(2,1)S(1)}, bf16[192,1536]{1,0:T(8,128)(2,1)}, u32[]{:S(2)}, u32[]{:S(2)}) collective-permute-start(bf16[192,1536]{1,0:T(8,128)(2,1)S(1)} %join.4), channel_id=1, source_target_pairs={{0,128},{32,160},{64,192},{96,224},{128,0},{160,32},{192,64},{224,... | collective-permute-start | bytes 1769480 | tf_op jit(solution)/shard_map/ppermute | solution.py:495
  41.5 6.2 %collective-permute-start.7 = (bf16[96,768]{1,0:T(8,128)(2,1)S(1)}, bf16[96,768]{1,0:T(8,128)(2,1)S(1)}, u32[]{:S(2)}, u32[]{:S(2)}) collective-permute-start(bf16[96,768]{1,0:T(8,128)(2,1)S(1)} %get-tuple-element.26.refs_0_), channel_id=1, source_target_pairs={{0,2},{1,3},{2,0},{3,1},{4,6},{5,7},{6,4},{7,5},{8,10},{9,11},{10,... | collective-permute-start | bytes 442376 | tf_op jit(solution)/shard_map/ppermute | solution.py:495
  41.6 6.2 %collective-permute-start.8 = (bf16[96,768]{1,0:T(8,128)(2,1)S(1)}, bf16[96,768]{1,0:T(8,128)(2,1)S(1)}, u32[]{:S(2)}, u32[]{:S(2)}) collective-permute-start(bf16[96,768]{1,0:T(8,128)(2,1)S(1)} %get-tuple-element.27.refs_1_), channel_id=1, source_target_pairs={{0,8},{1,9},{2,10},{3,11},{4,12},{5,13},{6,14},{7,15},{8,0},{9,1},... | collective-permute-start | bytes 442376 | tf_op jit(solution)/shard_map/ppermute | solution.py:495
  47.9 10.1 %collective-permute-start.10 = (bf16[192,768]{1,0:T(8,128)(2,1)S(1)}, bf16[192,768]{1,0:T(8,128)(2,1)S(1)}, u32[]{:S(2)}, u32[]{:S(2)}) collective-permute-start(bf16[192,768]{1,0:T(8,128)(2,1)S(1)} %get-tuple-element.29.refs_1_), channel_id=1, source_target_pairs={{0,16},{1,17},{2,18},{3,19},{4,20},{5,21},{6,22},{7,23},{8,24},{9,... | collective-permute-start | bytes 884744 | tf_op jit(solution)/shard_map/ppermute | solution.py:495
  49.1 9.7 %collective-permute-start.9 = (bf16[192,768]{1,0:T(8,128)(2,1)S(1)}, bf16[192,768]{1,0:T(8,128)(2,1)S(1)}, u32[]{:S(2)}, u32[]{:S(2)}) collective-permute-start(bf16[192,768]{1,0:T(8,128)(2,1)S(1)} %get-tuple-element.28.refs_0_), channel_id=1, source_target_pairs={{0,4},{1,5},{2,6},{3,7},{4,0},{5,1},{6,2},{7,3},{8,12},{9,13},{10,... | collective-permute-start | bytes 884744 | tf_op jit(solution)/shard_map/ppermute | solution.py:495
  59.9 15.5 %collective-permute-start.11 = (bf16[384,768]{1,0:T(8,128)(2,1)}, bf16[384,768]{1,0:T(8,128)(2,1)}, u32[]{:S(2)}, u32[]{:S(2)}) collective-permute-start(bf16[384,768]{1,0:T(8,128)(2,1)} %get-tuple-element.30.own0_ref), channel_id=1, source_target_pairs={{0,8},{1,9},{2,10},{3,11},{4,12},{5,13},{6,14},{7,15},{8,16},{9,17... | collective-permute-start | bytes 1769480 | tf_op jit(solution)/shard_map/ppermute | solution.py:491
  62.0 16.2 %collective-permute-start.13 = (bf16[384,768]{1,0:T(8,128)(2,1)}, bf16[384,768]{1,0:T(8,128)(2,1)}, u32[]{:S(2)}, u32[]{:S(2)}) collective-permute-start(bf16[384,768]{1,0:T(8,128)(2,1)} %get-tuple-element.31.own1_ref), channel_id=1, source_target_pairs={{0,2},{1,3},{2,4},{3,5},{4,6},{5,7},{6,0},{7,1},{8,10},{9,11},{10,... | collective-permute-start | bytes 1769480 | tf_op jit(solution)/shard_map/ppermute | solution.py:491
  71.9 8.3 %collective-permute-start.6 = (bf16[192,1536]{1,0:T(8,128)(2,1)}, bf16[192,1536]{1,0:T(8,128)(2,1)}, u32[]{:S(2)}, u32[]{:S(2)}) collective-permute-start(bf16[192,1536]{1,0:T(8,128)(2,1)} %collective-permute-done.4), channel_id=1, source_target_pairs={{0,32},{32,0},{64,96},{96,64},{128,160},{160,128},{192,224},{224,1... | collective-permute-start | bytes 1769480 | tf_op jit(solution)/shard_map/ppermute | solution.py:495
  72.0 17.2 %collective-permute-start.15 = (bf16[384,768]{1,0:T(8,128)(2,1)}, bf16[384,768]{1,0:T(8,128)(2,1)}, u32[]{:S(2)}, u32[]{:S(2)}) collective-permute-start(bf16[384,768]{1,0:T(8,128)(2,1)} %get-tuple-element.30.own0_ref), channel_id=1, source_target_pairs={{0,24},{1,25},{2,26},{3,27},{4,28},{5,29},{6,30},{7,31},{8,0},{9,1... | collective-permute-start | bytes 1769480 | tf_op jit(solution)/shard_map/ppermute | solution.py:491
  72.5 16.7 %collective-permute-start.16 = (bf16[384,768]{1,0:T(8,128)(2,1)}, bf16[384,768]{1,0:T(8,128)(2,1)}, u32[]{:S(2)}, u32[]{:S(2)}) collective-permute-start(bf16[384,768]{1,0:T(8,128)(2,1)} %get-tuple-element.31.own1_ref), channel_id=1, source_target_pairs={{0,6},{1,7},{2,0},{3,1},{4,2},{5,3},{6,4},{7,5},{8,14},{9,15},{10,... | collective-permute-start | bytes 1769480 | tf_op jit(solution)/shard_map/ppermute | solution.py:491
  72.5 1.3 %copy-start.4 = (bf16[768,768]{1,0:T(8,128)(2,1)S(1)}, bf16[768,768]{1,0:T(8,128)(2,1)}, u32[]{:S(2)}) copy-start(bf16[768,768]{1,0:T(8,128)(2,1)} %query_ref.1) | copy-start | bytes 3538948
  73.8 6.5 %copy-start.6 = (bf16[192,1536]{1,0:T(8,128)(2,1)S(1)}, bf16[192,1536]{1,0:T(8,128)(2,1)}, u32[]{:S(2)}) copy-start(bf16[192,1536]{1,0:T(8,128)(2,1)} %copy-done.5) | copy-start | bytes 1769476
  75.5 24.7 %collective-permute-start.12 = (bf16[384,768]{1,0:T(8,128)(2,1)}, bf16[384,768]{1,0:T(8,128)(2,1)S(1)}, u32[]{:S(2)}, u32[]{:S(2)}) collective-permute-start(bf16[384,768]{1,0:T(8,128)(2,1)} %collective-permute-done.11.low0_ref), channel_id=1, source_target_pairs={{0,8},{1,9},{2,10},{3,11},{4,12},{5,13},{6,14},{7,15},{8,16},{9,17... | collective-permute-start | bytes 1769480 | tf_op jit(solution)/shard_map/ppermute | solution.py:491
  78.3 21.9 %collective-permute-start.14 = (bf16[384,768]{1,0:T(8,128)(2,1)}, bf16[384,768]{1,0:T(8,128)(2,1)S(1)}, u32[]{:S(2)}, u32[]{:S(2)}) collective-permute-start(bf16[384,768]{1,0:T(8,128)(2,1)} %collective-permute-done.13.low1_ref), channel_id=1, source_target_pairs={{0,2},{1,3},{2,4},{3,5},{4,6},{5,7},{6,0},{7,1},{8,10},{9,11},{10,... | collective-permute-start | bytes 1769480 | tf_op jit(solution)/shard_map/ppermute | solution.py:491
  89.2 11.0 %slice-start = ((s8[4718592]{0:T(1024)(128)(4,1)}), s8[4194304]{0:T(1024)(128)(4,1)S(1)}, s32[]{:S(2)}) async-start(s8[4718592]{0:T(1024)(128)(4,1)} %bitcast.21), calls=%async_computation | async-start | bytes 8388608
  89.2 11.0 %slice-start.1 = ((s8[4718592]{0:T(1024)(128)(4,1)}), s8[524288]{0:T(1024)(128)(4,1)S(1)}, s32[]{:S(2)}) async-start(s8[4718592]{0:T(1024)(128)(4,1)} %bitcast.21), calls=%async_computation.1 | async-start | bytes 1048576
  89.2 11.0 %copy-start.1 = (bf16[1536,768]{1,0:T(8,128)(2,1)S(1)}, bf16[1536,768]{1,0:T(8,128)(2,1)}, u32[]{:S(2)}) copy-start(bf16[1536,768]{1,0:T(8,128)(2,1)} %down_ref.1) | copy-start | bytes 7077892
  89.2 11.0 %copy-start.3 = (bf16[768,768]{1,0:T(8,128)(2,1)S(1)}, bf16[768,768]{1,0:T(8,128)(2,1)}, u32[]{:S(2)}) copy-start(bf16[768,768]{1,0:T(8,128)(2,1)} %output_ref.1) | copy-start | bytes 3538948
  89.2 11.0 %copy-start.8 = (bf16[768,128]{1,0:T(8,128)(2,1)S(1)}, bf16[768,128]{1,0:T(8,128)(2,1)}, u32[]{:S(2)}) copy-start(bf16[768,128]{1,0:T(8,128)(2,1)} %back_ref.1) | copy-start | bytes 589828
  89.3 11.0 %copy-start.9 = (bf16[2,384,128]{2,1,0:T(8,128)(2,1)S(1)}, bf16[2,384,128]{2,1,0:T(8,128)(2,1)}, u32[]{:S(2)}) copy-start(bf16[2,384,128]{2,1,0:T(8,128)(2,1)} %get-tuple-element.36.mid_ref) | copy-start | bytes 589828
  89.3 11.0 %copy-start.10 = (bf16[2,48,768]{2,1,0:T(8,128)(2,1)S(1)}, bf16[2,48,768]{2,1,0:T(8,128)(2,1)}, u32[]{:S(2)}) copy-start(bf16[2,48,768]{2,1,0:T(8,128)(2,1)} %get-tuple-element.35.tokact_ref) | copy-start | bytes 442372
  89.3 11.0 %copy-start.11 = (s32[384]{0:T(512)S(1)}, s32[384]{0:T(512)}, u32[]{:S(2)}) copy-start(s32[384]{0:T(512)} %param.26) | copy-start | bytes 4612
  89.3 11.0 %copy-start.12 = (f32[768]{0:T(1024)S(1)}, f32[768]{0:T(1024)}, u32[]{:S(2)}) copy-start(f32[768]{0:T(1024)} %param.34) | copy-start | bytes 9220
  109.2 8.4 %collective-permute-start.17 = (bf16[2,128]{1,0:T(2,128)(2,1)S(1)}, bf16[2,128]{1,0:T(2,128)(2,1)S(1)}, u32[]{:S(2)}, u32[]{:S(2)}) collective-permute-start(bf16[2,128]{1,0:T(2,128)(2,1)S(1)} %bitcast.35), channel_id=1, source_target_pairs={{0,1},{1,2},{2,3},{3,4},{4,5},{5,6},{6,7},{7,8},{8,9},{9,10},{10,1... | collective-permute-start | bytes 1544 | tf_op jit(solution)/shard_map/ppermute | solution.py:611
